TPU v7x, 32 devices: a whole 2x2x4 slice. The times are simulated.
32 devices in a mesh: dp: 8 (over y, x, core), tensor: 4 (over z).
Axes of the slice: x: 2, y: 2, z: 4, core: 2. Of those that a mesh axis runs over, the one named last changes fastest.
Arguments:
- tokens: bfloat16 [2, 8192, 1152], P(None, 'dp'), may hold values from -6 to 6
- conditioning: bfloat16 [2, 32, 1152], P(None, 'dp'), may hold values from -6 to 6
- lengths: int32 [2, 32], P(None, 'dp'), may hold values from 0 to 1024, as said below
- out_grad: bfloat16 [2, 8192, 1152], P(None, 'dp'), may hold values from -6 to 6
- ada_weight: bfloat16 [1152, 6912], P(None, 'tensor'), may hold values from -0.1875 to 0.1875
- ada_bias: float32 [6912], P('tensor'), may hold values from -1.75 to 1.75
- qkv_weight: bfloat16 [3, 1152, 1152], P(None, None, 'tensor'), may hold values from -0.1875 to 0.1875
- qv_bias: float32 [2, 1152], P(None, 'tensor'), may hold values from -1.75 to 1.75
- out_weight: bfloat16 [1152, 1152], P('tensor'), may hold values from -2 to 2
- out_bias: float32 [1152], replicated, may hold values from -1.75 to 1.75
- up_weight: bfloat16 [1152, 4608], P(None, 'tensor'), may hold values from -0.1875 to 0.1875
- up_bias: float32 [4608], P('tensor'), may hold values from -1.75 to 1.75
- down_weight: bfloat16 [4608, 1152], P('tensor'), may hold values from -0.09375 to 0.09375
- down_bias: float32 [1152], replicated, may hold values from -1.75 to 1.75
Outputs:
- layer_out: bfloat16 [2, 8192, 1152], P(None, ('dp', 'tensor'))
- tokens_grad: float32 [2, 8192, 1152], P(None, ('dp', 'tensor'))
- conditioning_grad: float32 [2, 32, 1152], P(None, 'dp')
- ada_weight_grad: float32 [1152, 6912], P(None, 'tensor')
- ada_bias_grad: float32 [6912], P('tensor')
- qkv_weight_grad: float32 [3, 1152, 1152], P(None, None, 'tensor')
- qv_bias_grad: float32 [2, 1152], P(None, 'tensor')
- out_weight_grad: float32 [1152, 1152], P('tensor')
- out_bias_grad: float32 [1152], replicated
- up_weight_grad: float32 [1152, 4608], P(None, 'tensor')
- up_bias_grad: float32 [4608], P('tensor')
- down_weight_grad: float32 [4608, 1152], P('tensor')
- down_bias_grad: float32 [1152], replicated
Inputs may be any that keep to these rules, and one draw needn't show every extreme that they name: `lengths`: each pack's slots come in runs of 4: a run holds one latent of 1024 tokens followed by zeros, or 2 to 4 latents of 256 tokens followed by zeros. A pack's latents lie end to end from its first row; the rows after them are padding.
All inputs are finite; a program needn't handle non-finite values.
Results may differ from a plain program's by a relative error of at most 0.013.
The roundings to bfloat16 on the way count: a program that leaves them out, or rounds other values in their place, can miss the bound.
Values may be sent and summed in bfloat16 or wider, within the bound.
No kernel may reach another device: no remote copies, remote signals or barrier semaphores. Data moves between devices by JAX's collectives and lax.ppermute only.
A program may use at most 384 MiB of HBM per device.

v0:
```python
import jax
import jax.numpy as jnp
from jax import lax
from jax.sharding import PartitionSpec as P

HEAD_DIM = 72


EPSILON = 1e-06
MASKED = -1e30
HIGHEST = lax.Precision.HIGHEST


def normalize(values):
    centred = values - jnp.mean(values, axis=-1, keepdims=True)
    inverse = lax.rsqrt(jnp.mean(centred * centred, axis=-1, keepdims=True) + EPSILON)
    return (centred * inverse, inverse)


def norm_backward(grad, normed, inverse):
    return inverse * (
        grad
        - jnp.mean(grad, axis=-1, keepdims=True)
        - normed * jnp.mean(grad * normed, axis=-1, keepdims=True)
    )


def segment_info(lengths_row, row_count):
    boundary = jnp.cumsum(lengths_row)
    position = jnp.arange(row_count, dtype=jnp.int32)
    segment = jnp.sum((boundary[None, :] <= position[:, None]).astype(jnp.int32), axis=1)
    slot_count = lengths_row.shape[0]
    onehot = (segment[:, None] == jnp.arange(slot_count, dtype=jnp.int32)[None, :]).astype(
        jnp.float32
    )
    validity = (segment < slot_count).astype(jnp.float32)
    return (segment, validity, onehot)


def per_image(onehot_rows, values):
    return jnp.einsum("ts,td->sd", onehot_rows, values, precision=HIGHEST)


def block_scores(query_block, key_heads, seg_block, segment, score_scale):
    raw_scores = jnp.einsum(
        "qhd,khd->hqk", query_block, key_heads, preferred_element_type=jnp.float32
    )
    allowed = seg_block[:, None] == segment[None, :]
    return jnp.where(allowed[None], raw_scores * score_scale, MASKED)


def attend(query_rows, key_rows, value_rows, segment, head_count):
    row_count, local_width = query_rows.shape
    head_size = local_width // head_count
    score_scale = head_size ** (-0.5)
    query_heads = query_rows.reshape(row_count, head_count, head_size)
    key_heads = key_rows.reshape(row_count, head_count, head_size)
    value_heads = value_rows.reshape(row_count, head_count, head_size)
    block_rows = min(512, row_count)
    outputs = []
    totals = []
    for block_start in range(0, row_count, block_rows):
        block_stop = block_start + block_rows
        scores = block_scores(
            query_heads[block_start:block_stop],
            key_heads,
            segment[block_start:block_stop],
            segment,
            score_scale,
        )
        row_max = jnp.max(scores, axis=-1, keepdims=True)
        exponent = jnp.exp(scores - row_max)
        row_sum = jnp.sum(exponent, axis=-1, keepdims=True)
        softmaxed = (exponent / row_sum).astype(jnp.bfloat16)
        outputs.append(
            jnp.einsum("hqk,khd->qhd", softmaxed, value_heads, preferred_element_type=jnp.float32)
        )
        totals.append(row_max[..., 0] + jnp.log(row_sum[..., 0]))
    attended = jnp.concatenate(outputs, axis=0).reshape(row_count, local_width).astype(jnp.bfloat16)
    return (attended, jnp.concatenate(totals, axis=1))


def attend_back(query_rows, key_rows, value_rows, segment, log_sums, grad_rows, head_count):
    row_count, local_width = query_rows.shape
    head_size = local_width // head_count
    score_scale = head_size ** (-0.5)
    query_heads = query_rows.reshape(row_count, head_count, head_size)
    key_heads = key_rows.reshape(row_count, head_count, head_size)
    value_heads = value_rows.reshape(row_count, head_count, head_size)
    grad_heads = grad_rows.reshape(row_count, head_count, head_size)
    key_grad = jnp.zeros((row_count, head_count, head_size), jnp.float32)
    value_grad = jnp.zeros((row_count, head_count, head_size), jnp.float32)
    query_grads = []
    block_rows = min(512, row_count)
    for block_start in range(0, row_count, block_rows):
        block_stop = block_start + block_rows
        query_block = query_heads[block_start:block_stop]
        grad_block = grad_heads[block_start:block_stop]
        scores = block_scores(
            query_block, key_heads, segment[block_start:block_stop], segment, score_scale
        )
        softmaxed = jnp.exp(scores - log_sums[:, block_start:block_stop, None])
        prob_grad = jnp.einsum(
            "qhd,khd->hqk", grad_block, value_heads, preferred_element_type=jnp.float32
        )
        inner = jnp.sum(softmaxed * prob_grad, axis=-1, keepdims=True)
        score_grad = (softmaxed * (prob_grad - inner) * score_scale).astype(jnp.bfloat16)
        query_grads.append(
            jnp.einsum("hqk,khd->qhd", score_grad, key_heads, preferred_element_type=jnp.float32)
        )
        key_grad = key_grad + jnp.einsum(
            "hqk,qhd->khd", score_grad, query_block, preferred_element_type=jnp.float32
        )
        value_grad = value_grad + jnp.einsum(
            "hqk,qhd->khd",
            softmaxed.astype(jnp.bfloat16),
            grad_block,
            preferred_element_type=jnp.float32,
        )
    query_grad = jnp.concatenate(query_grads, axis=0).reshape(row_count, local_width)
    return (
        query_grad,
        key_grad.reshape(row_count, local_width),
        value_grad.reshape(row_count, local_width),
    )


def local(
    tokens,
    conditioning,
    lengths,
    out_grad,
    ada_weight,
    ada_bias,
    qkv_weight,
    qv_bias,
    out_weight,
    out_bias,
    up_weight,
    up_bias,
    down_weight,
    down_bias,
):
    groups = lax.axis_size("tensor")
    rank = lax.axis_index("tensor")
    micro_count, row_count, width = tokens.shape
    share_rows = row_count // groups
    head_count = qkv_weight.shape[2] // HEAD_DIM

    def own_rows(array):
        return lax.dynamic_slice_in_dim(array, rank * share_rows, share_rows, 0)

    cond_float = conditioning.astype(jnp.float32)
    cond_act = jax.nn.silu(cond_float).astype(jnp.bfloat16)
    ada_part = (
        jnp.einsum("msd,de->mse", cond_act, ada_weight, preferred_element_type=jnp.float32)
        + ada_bias
    )
    modulation = lax.all_gather(ada_part, "tensor", axis=2, tiled=True)
    grad_qkv = jnp.zeros(qkv_weight.shape, jnp.float32)
    grad_qv_bias = jnp.zeros(qv_bias.shape, jnp.float32)
    grad_out_w = jnp.zeros(out_weight.shape, jnp.float32)
    grad_out_b = jnp.zeros(out_bias.shape, jnp.float32)
    grad_up_w = jnp.zeros(up_weight.shape, jnp.float32)
    grad_up_b = jnp.zeros(up_bias.shape, jnp.float32)
    grad_down_w = jnp.zeros(down_weight.shape, jnp.float32)
    grad_down_b = jnp.zeros(down_bias.shape, jnp.float32)
    layer_rows = []
    input_rows = []
    mod_grads = []
    for micro in range(micro_count):
        segment, validity, onehot = segment_info(lengths[micro], row_count)
        per_token = jnp.dot(onehot, modulation[micro], precision=HIGHEST)
        shift_one, scale_one, gate_one, shift_two, scale_two, gate_two = jnp.split(
            per_token, 6, axis=1
        )
        token_float = tokens[micro].astype(jnp.float32)
        normed_one, inverse_one = normalize(token_float)
        hidden_one = (normed_one * (1.0 + scale_one) + shift_one).astype(jnp.bfloat16)
        projected = jnp.einsum(
            "td,cde->cte", hidden_one, qkv_weight, preferred_element_type=jnp.float32
        )
        query_rows = (projected[0] + qv_bias[0]).astype(jnp.bfloat16)
        key_rows = projected[1].astype(jnp.bfloat16)
        value_rows = (projected[2] + qv_bias[1]).astype(jnp.bfloat16)
        attended, log_sums = attend(query_rows, key_rows, value_rows, segment, head_count)
        attn_part = jnp.dot(attended, out_weight, preferred_element_type=jnp.float32)
        attn_out = lax.psum(attn_part, "tensor") + out_bias
        residual_mid = token_float + gate_one * attn_out
        normed_two, inverse_two = normalize(residual_mid)
        hidden_two = (normed_two * (1.0 + scale_two) + shift_two).astype(jnp.bfloat16)
        attn_share = own_rows(attn_out)
        residual_share = own_rows(residual_mid)
        normed_two_share = own_rows(normed_two)
        pre_act = jnp.dot(hidden_two, up_weight, preferred_element_type=jnp.float32) + up_bias
        activated = jax.nn.gelu(pre_act, approximate=True).astype(jnp.bfloat16)
        mlp_part = jnp.dot(activated, down_weight, preferred_element_type=jnp.float32)
        mlp_out = (
            lax.psum_scatter(
                mlp_part.astype(jnp.bfloat16), "tensor", scatter_dimension=0, tiled=True
            ).astype(jnp.float32)
            + down_bias
        )
        valid_share = own_rows(validity)
        gate_two_share = own_rows(gate_two)
        layer_rows.append(
            (valid_share[:, None] * (residual_share + gate_two_share * mlp_out)).astype(
                jnp.bfloat16
            )
        )
        onehot_share = own_rows(onehot)
        grad_y = out_grad[micro].astype(jnp.float32) * validity[:, None]
        grad_mlp = grad_y * gate_two
        grad_down_b = grad_down_b + jnp.sum(grad_mlp, axis=0)
        grad_gate_two = per_image(onehot_share, own_rows(grad_y) * mlp_out)
        grad_mlp_low = grad_mlp.astype(jnp.bfloat16)
        grad_down_w = grad_down_w + jnp.einsum(
            "tf,td->fd", activated, grad_mlp_low, preferred_element_type=jnp.float32
        )
        grad_act = jnp.einsum(
            "td,fd->tf", grad_mlp_low, down_weight, preferred_element_type=jnp.float32
        )
        gelu_value, gelu_pull = jax.vjp(
            lambda values: jax.nn.gelu(values, approximate=True), pre_act
        )
        grad_pre = gelu_pull(grad_act)[0]
        grad_up_b = grad_up_b + jnp.sum(grad_pre, axis=0)
        grad_pre_low = grad_pre.astype(jnp.bfloat16)
        grad_up_w = grad_up_w + jnp.einsum(
            "td,tf->df", hidden_two, grad_pre_low, preferred_element_type=jnp.float32
        )
        grad_two_part = jnp.einsum(
            "tf,df->td", grad_pre_low, up_weight, preferred_element_type=jnp.float32
        )
        grad_hidden_two = lax.psum(grad_two_part, "tensor")
        grad_two_share = own_rows(grad_hidden_two)
        grad_mid = grad_y + norm_backward(
            grad_hidden_two * (1.0 + scale_two), normed_two, inverse_two
        )
        grad_shift_two = per_image(onehot_share, grad_two_share)
        grad_scale_two = per_image(onehot_share, grad_two_share * normed_two_share)
        grad_mid_share = own_rows(grad_mid)
        grad_gate_one = per_image(onehot_share, grad_mid_share * attn_share)
        grad_attn = grad_mid * gate_one
        grad_out_b = grad_out_b + jnp.sum(grad_attn, axis=0)
        grad_attn_low = grad_attn.astype(jnp.bfloat16)
        grad_out_w = grad_out_w + jnp.einsum(
            "th,td->hd", attended, grad_attn_low, preferred_element_type=jnp.float32
        )
        grad_attended = jnp.einsum(
            "td,hd->th", grad_attn_low, out_weight, preferred_element_type=jnp.float32
        ).astype(jnp.bfloat16)
        query_grad, key_grad, value_grad = attend_back(
            query_rows, key_rows, value_rows, segment, log_sums, grad_attended, head_count
        )
        grad_qv_bias = grad_qv_bias + jnp.stack(
            [jnp.sum(query_grad, axis=0), jnp.sum(value_grad, axis=0)]
        )
        grad_proj_low = jnp.stack([query_grad, key_grad, value_grad]).astype(jnp.bfloat16)
        grad_qkv = grad_qkv + jnp.einsum(
            "td,cte->cde", hidden_one, grad_proj_low, preferred_element_type=jnp.float32
        )
        grad_one_part = jnp.einsum(
            "cte,cde->td", grad_proj_low, qkv_weight, preferred_element_type=jnp.float32
        )
        grad_one_share = lax.psum_scatter(grad_one_part, "tensor", scatter_dimension=0, tiled=True)
        normed_one_share = own_rows(normed_one)
        input_rows.append(
            grad_mid_share
            + norm_backward(
                grad_one_share * (1.0 + own_rows(scale_one)),
                normed_one_share,
                own_rows(inverse_one),
            )
        )
        grad_shift_one = per_image(onehot_share, grad_one_share)
        grad_scale_one = per_image(onehot_share, grad_one_share * normed_one_share)
        mod_grads.append(
            jnp.concatenate(
                [
                    grad_shift_one,
                    grad_scale_one,
                    grad_gate_one,
                    grad_shift_two,
                    grad_scale_two,
                    grad_gate_two,
                ],
                axis=1,
            )
        )
    mod_grad_all = jnp.stack(mod_grads)
    mod_grad_own = lax.psum_scatter(mod_grad_all, "tensor", scatter_dimension=2, tiled=True)
    grad_ada_b = jnp.sum(mod_grad_own, axis=(0, 1))
    mod_grad_low = mod_grad_own.astype(jnp.bfloat16)
    cond_part = jnp.einsum(
        "mse,de->msd", mod_grad_low, ada_weight, preferred_element_type=jnp.float32
    )
    cond_act_grad = lax.psum(cond_part, "tensor")
    silu_value, silu_pull = jax.vjp(jax.nn.silu, cond_float)
    conditioning_grad = silu_pull(cond_act_grad)[0]
    grad_ada_w = jnp.einsum(
        "msd,mse->de", cond_act, mod_grad_low, preferred_element_type=jnp.float32
    )
    shares = (
        lax.psum_scatter(grad_ada_w, "dp", scatter_dimension=0, tiled=True),
        lax.psum_scatter(grad_qkv, "dp", scatter_dimension=1, tiled=True),
        lax.psum_scatter(grad_out_w, "dp", scatter_dimension=1, tiled=True),
        lax.psum_scatter(grad_up_w, "dp", scatter_dimension=0, tiled=True),
        lax.psum_scatter(grad_down_w, "dp", scatter_dimension=1, tiled=True),
    )
    summed = (
        lax.all_gather(shares[0], "dp", axis=0, tiled=True),
        lax.all_gather(shares[1], "dp", axis=1, tiled=True),
        lax.all_gather(shares[2], "dp", axis=1, tiled=True),
        lax.all_gather(shares[3], "dp", axis=0, tiled=True),
        lax.all_gather(shares[4], "dp", axis=1, tiled=True),
    )
    ada_weight_grad, qkv_weight_grad, out_weight_grad, up_weight_grad, down_weight_grad = summed
    bias_grads = lax.psum((grad_ada_b, grad_qv_bias, grad_out_b, grad_up_b, grad_down_b), "dp")
    layer_out = jnp.stack(layer_rows)
    tokens_grad = jnp.stack(input_rows)
    return (
        layer_out,
        tokens_grad,
        conditioning_grad,
        ada_weight_grad,
        bias_grads[0],
        qkv_weight_grad,
        bias_grads[1],
        out_weight_grad,
        bias_grads[2],
        up_weight_grad,
        bias_grads[3],
        down_weight_grad,
        bias_grads[4],
    )


def solution(mesh):
    placed = (
        P(None, "dp", None),
        P(None, "dp", None),
        P(None, "dp"),
        P(None, "dp", None),
        P(None, "tensor"),
        P("tensor"),
        P(None, None, "tensor"),
        P(None, "tensor"),
        P("tensor", None),
        P(),
        P(None, "tensor"),
        P("tensor"),
        P("tensor", None),
        P(),
    )
    return jax.shard_map(
        local,
        mesh=mesh,
        in_specs=placed,
        out_specs=(
            P(None, ("dp", "tensor"), None),
            P(None, ("dp", "tensor"), None),
            P(None, "dp", None),
            P(None, "tensor"),
            P("tensor"),
            P(None, None, "tensor"),
            P(None, "tensor"),
            P("tensor", None),
            P(),
            P(None, "tensor"),
            P("tensor"),
            P("tensor", None),
            P(),
        ),
        check_vma=False,
    )
```

profile of v0, /device:TPU:10, one launch (start us, length us, event | category | flops | bytes accessed | tf_op | source)
XLA Modules:
  0.0 2031.9 jit_solution(5553610816085237550)
XLA Ops:
  13.0 118.0 %all_gather.18 = f32[2,4,6912]{1,0,2:T(2,128)S(1)} all-gather(f32[2,4,1728]{1,0,2:T(2,128)} %copy.36), channel_id=1, replica_groups=mesh['dp'=8,'tensor'=4] {'tensor'}, dimensions={2}, use_global_device_ids=true | all-gather | bytes 276480 | tf_op jit(solution)/shard_map/all_gather | solution.py:159
  131.0 6.6 fusion.353
  144.5 17.3 fusion.265
  161.8 15.2 fusion.264
  177.0 11.4 fusion.16
  239.5 325.9 %all-reduce.8.cloned.1.call-done = (f32[1024,1152]{1,0:T(8,128)}, f32[1024,1152]{1,0:T(8,128)}) async-done(((f32[1024,1152]{1,0:T(8,128)}, f32[1024,1152]{1,0:T(8,128)}), (f32[1024,1152]{1,0:T(8,128)}, f32[1024,1152]{1,0:T(8,128)})) %all-reduce.8.cloned.1.call-update) | async-done | bytes 9437200 | tf_op jit(solution)/shard_map/psum | solution.py:188
  565.4 12.6 fusion.347
  581.7 17.1 fusion.351
  598.7 7.8 fusion.376
  606.5 18.1 fusion.352
  624.7 6.1 fusion.379
  630.8 7.5 fusion.343
  638.4 5.5 fusion.233
  644.0 7.5 fusion.345
  652.9 5.1 fusion.237
  658.1 324.4 %all-reduce.6.cloned.1.call-done = (f32[1024,1152]{1,0:T(8,128)}, f32[1024,1152]{1,0:T(8,128)}) async-done(((f32[1024,1152]{1,0:T(8,128)}, f32[1024,1152]{1,0:T(8,128)}), (f32[1024,1152]{1,0:T(8,128)}, f32[1024,1152]{1,0:T(8,128)})) %all-reduce.6.cloned.1.call-update) | async-done | bytes 9437200 | tf_op jit(solution)/shard_map/psum | solution.py:235
  982.6 10.2 fusion.341
  995.6 16.2 multiply_reduce_fusion.8
  1011.8 4.6 fusion.173
  1018.2 4.6 fusion.380
  1022.8 19.1 fusion.66
  1041.9 19.0 fusion.357
  1065.5 5.0 fusion.126
  1074.5 17.4 fusion.356
  1091.9 24.1 %fusion.195 = bf16[4,72,1024]{2,1,0:T(8,128)(2,1)} fusion(f32[4,72,1024]{2,1,0:T(8,128)} %fusion.66, bf16[512,4,72]{0,2,1:T(8,128)(2,1)S(1)} %bitcast.262, f32[4,512,1024]{2,1,0:T(8,128)} %fusion.381, f32[4,512,1024]{2,1,0:T(8,128)} %copy-done.6, f32[4,512]{1,0:T(4,128)S(1)} %log_add_fusion, pred[512,1024]{1,0:T(8,128)(4,1)S(1)} %copy-done.29), kind=kOutput, calls=%fused_computation.205 | convolution fusion | flops 325651456 | bytes 19374080 | tf_op jit(solution)/shard_map/hqk,qhd->khd/dot_general | solution.py:111
  1116.2 7.1 convolution_bitcast_fusion.1
  1129.8 4.6 fusion.378
  1134.4 17.4 fusion.358
  1156.3 17.4 fusion.359
  1173.9 19.1 fusion.52
  1193.0 23.1 %fusion.192 = bf16[4,72,1024]{2,1,0:T(8,128)(2,1)S(1)} fusion(f32[4,72,1024]{2,1,0:T(8,128)} %fusion.52, bf16[512,4,72]{0,2,1:T(8,128)(2,1)S(1)} %bitcast.258, f32[4,512,1024]{2,1,0:T(8,128)} %fusion.378, f32[4,512,1024]{2,1,0:T(8,128)} %copy-done.4, f32[4,512]{1,0:T(4,128)S(1)} %log_add_fusion.2, pred[512,1024]{1,0:T(8,128)(4,1)S(1)} %copy-done.27), kind=kOutput, calls=%fused_computation.204 | convolution fusion | flops 325651456 | bytes 19374080 | tf_op jit(solution)/shard_map/hqk,qhd->khd/dot_general | solution.py:111
  1216.1 5.0 fusion.130
  1221.2 5.2 fusion.355
  1233.4 7.9 convolution_convert_fusion
  1241.6 8.8 convolution_convert_fusion.1
  1261.0 57.0 %reduce-scatter.19.cloned.1.call-done = f32[256,1152]{1,0:T(8,128)} async-done(((f32[1024,1152]{1,0:T(8,128)}), f32[256,1152]{1,0:T(8,128)}) %reduce-scatter.19.cloned.1.call-update) | async-done | bytes 1179664 | tf_op jit(solution)/shard_map/reduce_scatter | solution.py:266
  1328.5 39.2 %reduce-scatter.17.cloned.1.call-done = bf16[256,1152]{1,0:T(8,128)(2,1)} async-done(((bf16[1024,1152]{1,0:T(8,128)(2,1)}), bf16[256,1152]{1,0:T(8,128)(2,1)}) %reduce-scatter.17.cloned.1.call-update) | async-done | bytes 589840 | tf_op jit(solution)/shard_map/reduce_scatter | solution.py:199
  1369.7 48.3 %reduce-scatter.15.cloned.1.call-done = bf16[256,1152]{1,0:T(8,128)(2,1)} async-done(((bf16[1024,1152]{1,0:T(8,128)(2,1)}), bf16[256,1152]{1,0:T(8,128)(2,1)}) %reduce-scatter.15.cloned.1.call-update) | async-done | bytes 589840 | tf_op jit(solution)/shard_map/reduce_scatter | solution.py:199
  1420.1 6.6 copy.42
  1426.7 7.9 reshape.438
  1441.3 6.1 fusion.235
  1447.5 5.6 convolution_add_fusion.1
  1454.8 6.1 fusion.340
  1460.9 8.3 convolution_add_fusion
  1469.3 4.9 fusion.251
  1478.7 8.6 copy.44
  1487.3 8.9 reshape.440
  1496.5 5.1 reduce-scatter.31.cloned.1.call-done
  1510.0 34.8 %reduce-scatter.25.cloned.1.call-done = f32[288,144]{0,1:T(8,128)} async-done(((f32[288,1152]{0,1:T(8,128)}), f32[288,144]{0,1:T(8,128)}) %reduce-scatter.25.cloned.1.call-update) | async-done | bytes 165904 | tf_op jit(solution)/shard_map/reduce_scatter | solution.py:307
  1544.9 60.8 %reduce-scatter.27.cloned.1.call-done = f32[144,1152]{1,0:T(8,128)} async-done(((f32[1152,1152]{1,0:T(8,128)}), f32[144,1152]{1,0:T(8,128)}) %reduce-scatter.27.cloned.1.call-update) | async-done | bytes 663568 | tf_op jit(solution)/shard_map/reduce_scatter | solution.py:308
  1605.8 61.1 %reduce-scatter.29.cloned.1.call-done = f32[1152,144]{0,1:T(8,128)} async-done(((f32[1152,1152]{0,1:T(8,128)}), f32[1152,144]{0,1:T(8,128)}) %reduce-scatter.29.cloned.1.call-update) | async-done | bytes 663568 | tf_op jit(solution)/shard_map/reduce_scatter | solution.py:309
  1667.0 54.5 %reduce-scatter.33.cloned.1.call-done = f32[144,864]{1,0:T(8,128)} async-done(((f32[1152,864]{1,0:T(8,128)}), f32[144,864]{1,0:T(8,128)}) %reduce-scatter.33.cloned.1.call-update) | async-done | bytes 497680
  1724.0 71.6 %reduce-scatter.23.cloned.1.call-done = f32[144,1728]{1,0:T(8,128)} async-done(((f32[1152,1728]{1,0:T(8,128)}), f32[144,1728]{1,0:T(8,128)}) %reduce-scatter.23.cloned.1.call-update) | async-done | bytes 995344 | tf_op jit(solution)/shard_map/reduce_scatter | solution.py:305
  1803.0 21.2 %all-gather.10.cloned.1.call-done = f32[288,1152]{0,1:T(8,128)} async-done(((f32[288,144]{0,1:T(8,128)}), f32[288,1152]{0,1:T(8,128)}) %all-gather.10.cloned.1.call-update) | async-done | bytes 1327120 | tf_op jit(solution)/shard_map/all_gather | solution.py:314
  1827.3 40.3 %all-gather.12.cloned.1.call-done = f32[1152,1152]{1,0:T(8,128)} async-done(((f32[144,1152]{1,0:T(8,128)}), f32[1152,1152]{1,0:T(8,128)}) %all-gather.12.cloned.1.call-update) | async-done | bytes 5308432 | tf_op jit(solution)/shard_map/all_gather | solution.py:315
  1867.5 43.3 %all-gather.14.cloned.1.call-done = f32[1152,1152]{0,1:T(8,128)} async-done(((f32[1152,144]{0,1:T(8,128)}), f32[1152,1152]{0,1:T(8,128)}) %all-gather.14.cloned.1.call-update) | async-done | bytes 5308432 | tf_op jit(solution)/shard_map/all_gather | solution.py:316
  1910.8 6.9 copy.41
  1928.3 12.9 bitcast_reduce_fusion
  1941.2 22.8 %all-reduce = (f32[1728]{0:T(1024)}, f32[2,288]{1,0:T(2,128)}, f32[1152]{0:T(1024)}, f32[1152]{0:T(1024)}, f32[1152]{0:T(1024)}) all-reduce(f32[1728]{0:T(1024)S(1)} %bitcast_reduce_fusion, f32[2,288]{1,0:T(2,128)S(1)} %maximum_add_fusion, f32[1152]{0:T(1024)S(1)} %add.414, ...), channel_id=1, replica_groups=mesh['dp'=8,'tensor'=4] {'dp'}, use_global_device_ids=true, to_apply=%region_44.45 | all-reduce | flops 5760 | bytes 46080 | tf_op jit(solution)/shard_map/psum | solution.py:319
  1967.2 15.8 psum.74
  1983.6 6.0 copy.39
  1989.7 21.2 %all-gather.6.cloned.1.call-done = f32[1152,1728]{1,0:T(8,128)} async-done(((f32[144,1728]{1,0:T(8,128)}), f32[1152,1728]{1,0:T(8,128)}) %all-gather.6.cloned.1.call-update) | async-done | bytes 7962640 | tf_op jit(solution)/shard_map/all_gather | solution.py:312
  2010.9 8.8 copy.38
  2019.7 5.4 copy.77
  (401 shorter events, 173.9 us)
Async XLA Ops:
  7.2 623.6 %copy-start = (bf16[1152,1152]{1,0:T(8,128)(2,1)S(1)}, bf16[1152,1152]{1,0:T(8,128)(2,1)}, u32[]{:S(2)}) copy-start(bf16[1152,1152]{1,0:T(8,128)(2,1)} %param.24) | copy-start | bytes 7962628
  7.2 558.2 %all-reduce.8.cloned.1.call-start = ((), (), s32[]{:S(2)}) async-start(), calls=%async_computation.26 | async-start | bytes 18874368 | tf_op jit(solution)/shard_map/psum | solution.py:188
  137.8 101.6 %copy-start.66 = (s32[1024]{0:T(1024)}, s32[1024]{0:T(1024)S(1)}, u32[]{:S(2)}) copy-start(s32[1024]{0:T(1024)S(1)} %convert_reduce_fusion.3) | copy-start | bytes 12292
  144.2 32.8 %copy-start.90 = (f32[1024]{0:T(1024)}, f32[1024]{0:T(1024)S(1)}, u32[]{:S(2)}) copy-start(f32[1024]{0:T(1024)S(1)} %add_rsqrt_fusion.3) | copy-start | bytes 12292
  144.5 95.0 %copy-start.68 = (s32[1024]{0:T(1024)}, s32[1024]{0:T(1024)S(1)}, u32[]{:S(2)}) copy-start(s32[1024]{0:T(1024)S(1)} %convert_reduce_fusion.2) | copy-start | bytes 12292
  144.5 17.3 copy-start.15
  144.5 32.5 %slice-start = ((s8[4718592]{0:T(1024)(128)(4,1)}), s8[4194304]{0:T(1024)(128)(4,1)S(1)}, s32[]{:S(2)}) async-start(s8[4718592]{0:T(1024)(128)(4,1)} %bitcast.231), calls=%async_computation.27 | async-start | bytes 8388608
  161.8 15.2 slice-start.1
  161.8 15.2 copy-start.91
  177.0 11.4 copy-start.100
  196.3 27.2 %copy-start.16 = (bf16[1,1024,288]{1,2,0:T(8,128)(2,1)}, bf16[1,1024,288]{1,2,0:T(8,128)(2,1)S(1)}, u32[]{:S(2)}) copy-start(bf16[1,1024,288]{1,2,0:T(8,128)(2,1)S(1)} %slice.215) | copy-start | bytes 1769476
  198.4 9.3 copy-start.60
  199.1 12.9 copy-start.30
  204.6 7.4 copy-start.22
  204.6 23.2 %copy-start.20 = (bf16[1024,4,72]{0,2,1:T(8,128)(2,1)}, bf16[1024,4,72]{0,2,1:T(8,128)(2,1)S(1)}, u32[]{:S(2)}) copy-start(bf16[1024,4,72]{0,2,1:T(8,128)(2,1)S(1)} %get-tuple-element.152) | copy-start | bytes 1769476
  215.5 8.1 copy-start.56
  216.2 11.7 copy-start.24
  239.4 326.0 %copy-start.92 = (f32[1152]{0:T(1024)S(1)}, f32[1152]{0:T(1024)}, u32[]{:S(2)}) copy-start(f32[1152]{0:T(1024)} %param.23) | copy-start | bytes 13828
  239.4 743.1 %all-reduce.6.cloned.1.call-start = ((), (), s32[]{:S(2)}) async-start(), calls=%async_computation.25 | async-start | bytes 18874368 | tf_op jit(solution)/shard_map/psum | solution.py:235
  239.5 753.3 %copy-start.81 = (f32[1024]{0:T(1024)}, f32[1024]{0:T(1024)S(1)}, u32[]{:S(2)}) copy-start(f32[1024]{0:T(1024)S(1)} %compare_convert_fusion.1) | copy-start | bytes 12292
  239.5 753.3 %copy-start.80 = (f32[1024]{0:T(1024)}, f32[1024]{0:T(1024)S(1)}, u32[]{:S(2)}) copy-start(f32[1024]{0:T(1024)S(1)} %compare_convert_fusion) | copy-start | bytes 12292
  598.7 7.8 copy-start.48
  624.7 19.3 slice-start.8
  630.8 13.1 slice-start.9
  658.0 334.8 %slice-start.2 = ((s8[4718592]{0:T(1024)(128)(4,1)}), s8[524288]{0:T(1024)(128)(4,1)S(1)}, s32[]{:S(2)}) async-start(s8[4718592]{0:T(1024)(128)(4,1)} %bitcast.233), calls=%async_computation.29 | async-start | bytes 1048576
  658.0 592.9 %reduce-scatter.21.cloned.1.call-start = ((), (), s32[]{:S(2)}) async-start(), calls=%async_computation.13 | async-start | bytes 5898240 | tf_op jit(solution)/shard_map/reduce_scatter | solution.py:266
  982.6 10.3 slice-start.3
  982.6 11.7 copy-start.9
  982.6 13.1 copy-start.10
  1018.2 23.7 %copy-start.62 = (bf16[512,288]{0,1:T(8,128)(2,1)}, bf16[512,288]{0,1:T(8,128)(2,1)S(1)}, u32[]{:S(2)}) copy-start(bf16[512,288]{0,1:T(8,128)(2,1)S(1)} %get-tuple-element.134) | copy-start | bytes 884740
  1022.8 19.1 copy-start.19
  1041.9 19.0 copy-start.64
  1060.9 9.6 slice-start.4
  1074.5 17.4 copy-start.59
  1091.9 24.2 %copy-start.74 = (bf16[512,4,72]{0,2,1:T(8,128)(2,1)S(1)}, bf16[512,4,72]{0,2,1:T(8,128)(2,1)}, u32[]{:S(2)}) copy-start(bf16[512,4,72]{0,2,1:T(8,128)(2,1)} %get-tuple-element.127) | copy-start | bytes 884740
  1123.4 194.7 %reduce-scatter.19.cloned.1.call-start = ((), (), s32[]{:S(2)}) async-start(), calls=%async_computation.12 | async-start | bytes 5898240 | tf_op jit(solution)/shard_map/reduce_scatter | solution.py:266
  1156.3 17.5 copy-start.57
  1173.8 52.5 %copy-start.72 = (bf16[1024,4,72]{0,2,1:T(8,128)(2,1)}, bf16[1024,4,72]{0,2,1:T(8,128)(2,1)S(1)}, u32[]{:S(2)}) copy-start(bf16[1024,4,72]{0,2,1:T(8,128)(2,1)S(1)} %pad_maximum_fusion.10) | copy-start | bytes 1769476
  1173.8 19.1 copy-start.55
  1216.1 10.3 copy-start.105
  1231.6 136.0 %reduce-scatter.17.cloned.1.call-start = ((), (), s32[]{:S(2)}) async-start(), calls=%async_computation.11 | async-start | bytes 2949120 | tf_op jit(solution)/shard_map/reduce_scatter | solution.py:199
  1241.3 176.6 %reduce-scatter.15.cloned.1.call-start = ((), (), s32[]{:S(2)}) async-start(), calls=%async_computation.10 | async-start | bytes 2949120 | tf_op jit(solution)/shard_map/reduce_scatter | solution.py:199
  1241.6 8.9 copy-start.69
  1241.6 9.1 copy-start.67
  1250.4 251.1 %reduce-scatter.31.cloned.1.call-start = ((), (), s32[]{:S(2)}) async-start(), calls=%async_computation.23 | async-start | bytes 4423680
  1261.0 106.7 %copy-start.75 = (f32[1152]{0:T(1024)S(1)}, f32[1152]{0:T(1024)}, u32[]{:S(2)}) copy-start(f32[1152]{0:T(1024)} %param.27) | copy-start | bytes 13828
  1426.7 8.4 copy-start.37
  1434.7 110.2 %reduce-scatter.25.cloned.1.call-start = ((), (), s32[]{:S(2)}) async-start(), calls=%async_computation.17 | async-start | bytes 1990656 | tf_op jit(solution)/shard_map/reduce_scatter | solution.py:307
  1441.3 164.5 %reduce-scatter.27.cloned.1.call-start = ((), (), s32[]{:S(2)}) async-start(), calls=%async_computation.19 | async-start | bytes 5971968 | tf_op jit(solution)/shard_map/reduce_scatter | solution.py:308
  1453.1 213.8 %reduce-scatter.29.cloned.1.call-start = ((), (), s32[]{:S(2)}) async-start(), calls=%async_computation.21 | async-start | bytes 5971968 | tf_op jit(solution)/shard_map/reduce_scatter | solution.py:309
  1469.3 252.1 %reduce-scatter.33.cloned.1.call-start = ((), (), s32[]{:S(2)}) async-start(), calls=%async_computation.24 | async-start | bytes 4644864
  1496.2 9.2 copy-start.73
  1496.2 299.3 %reduce-scatter.23.cloned.1.call-start = ((), (), s32[]{:S(2)}) async-start(), calls=%async_computation.14 | async-start | bytes 9289728 | tf_op jit(solution)/shard_map/reduce_scatter | solution.py:305
  1510.0 288.6 %copy-start.93 = (f32[1152]{0:T(1024)S(1)}, f32[1152]{0:T(1024)}, u32[]{:S(2)}) copy-start(f32[1152]{0:T(1024)} %get-tuple-element.81) | copy-start | bytes 13828
  1510.0 288.6 %copy-start.94 = (f32[1152]{0:T(1024)S(1)}, f32[1152]{0:T(1024)}, u32[]{:S(2)}) copy-start(f32[1152]{0:T(1024)} %get-tuple-element.83) | copy-start | bytes 13828
  1510.0 288.6 %copy-start.43 = (bf16[256,1152]{1,0:T(8,128)(2,1)S(1)}, bf16[256,1152]{1,0:T(8,128)(2,1)}, u32[]{:S(2)}) copy-start(bf16[256,1152]{1,0:T(8,128)(2,1)} %reduce-scatter.17.cloned.1.call-done) | copy-start | bytes 1769476
  1510.0 288.6 %copy-start.44 = (bf16[256,1152]{1,0:T(8,128)(2,1)S(1)}, bf16[256,1152]{1,0:T(8,128)(2,1)}, u32[]{:S(2)}) copy-start(bf16[256,1152]{1,0:T(8,128)(2,1)} %reduce-scatter.15.cloned.1.call-done) | copy-start | bytes 1769476
  1510.0 314.2 %all-gather.10.cloned.1.call-start = ((), (), s32[]{:S(2)}) async-start(), calls=%async_computation.18 | async-start | bytes 1990656 | tf_op jit(solution)/shard_map/all_gather | solution.py:314
  1544.8 322.7 %all-gather.12.cloned.1.call-start = ((), (), s32[]{:S(2)}) async-start(), calls=%async_computation.20 | async-start | bytes 5971968 | tf_op jit(solution)/shard_map/all_gather | solution.py:315
  1605.7 305.1 %all-gather.14.cloned.1.call-start = ((), (), s32[]{:S(2)}) async-start(), calls=%async_computation.22 | async-start | bytes 5971968 | tf_op jit(solution)/shard_map/all_gather | solution.py:316
  1666.9 316.7 %all-gather.8.cloned.1.call-start = ((), (), s32[]{:S(2)}) async-start(), calls=%async_computation.16 | async-start | bytes 5971968 | tf_op jit(solution)/shard_map/all_gather | solution.py:313
  1723.9 286.9 %all-gather.6.cloned.1.call-start = ((), (), s32[]{:S(2)}) async-start(), calls=%async_computation.15 | async-start | bytes 9289728 | tf_op jit(solution)/shard_map/all_gather | solution.py:312
  1827.3 90.4 %copy-start.11 = (f32[256,1152]{1,0:T(8,128)S(1)}, f32[256,1152]{1,0:T(8,128)}, u32[]{:S(2)}) copy-start(f32[256,1152]{1,0:T(8,128)} %reduce-scatter.21.cloned.1.call-done) | copy-start | bytes 3538948
  1827.3 92.4 %copy-start.12 = (f32[256,1152]{1,0:T(8,128)S(1)}, f32[256,1152]{1,0:T(8,128)}, u32[]{:S(2)}) copy-start(f32[256,1152]{1,0:T(8,128)} %reduce-scatter.19.cloned.1.call-done) | copy-start | bytes 3538948
  (73 other events, 286.4 us)
Sparse Core Ops, SparseCore 0:
  239.5 325.8 all-reduce.7
  658.2 324.3 all-reduce.5
  1123.5 86.2 reduce-scatter.20
  1231.8 86.2 reduce-scatter.18
  1320.2 47.4 reduce-scatter.16
  1370.4 47.5 reduce-scatter.14
  1434.8 66.7 reduce-scatter.30
  1504.9 39.8 reduce-scatter.24
  1548.8 56.8 reduce-scatter.26
  1609.9 56.8 reduce-scatter.28
  1670.3 51.0 reduce-scatter.32
  1724.9 70.5 reduce-scatter.22
  1797.6 26.5 all-gather.9
  1826.1 41.3 all-gather.11
  1869.4 41.3 all-gather.13
  1913.3 41.6 all-gather.7
  1956.9 53.8 all-gather.5
where the time goes:
time: 2040 us; the launch traced here: 2030 us
  waiting for transfers between devices  1210 us (59%)
  matrix products  406 us (20%)
  blocking collectives  157 us (8%)
  other arithmetic  144 us (7%)
  local copies, waits for them, and re-layouts  98.3 us (5%)
    psum x1, waiting for transfers between devices, local(): attn_out = lax.psum(attn_part, 'tensor') + out_bias  326 us
    psum x1, waiting for transfers between devices, local(): grad_hidden_two = lax.psum(grad_two_part, 'tensor')  324 us
    all_gather x1, blocking collectives, local(): modulation = lax.all_gather(ada_part, 'tensor', axis=2, tiled=True)  118 us
    reduce_scatter x2, waiting for transfers between devices, local(): lax.psum_scatter(mlp_part.astype(jnp.bfloat16), 'tensor', scatter_dimensi...  87.5 us
    dot_general x4, matrix products, attend_back(): jnp.einsum('hqk,qhd->khd', score_grad, query_block, preferred_element_typ...  85.5 us
    unnamed x248, local copies, waits for them, and re-layouts  82.2 us
    reduce_scatter x1, waiting for transfers between devices, local(): lax.psum_scatter(grad_ada_w, 'dp', scatter_dimension=0, tiled=True)  71.6 us
    dot_general x4, matrix products, attend_back(): jnp.einsum('hqk,khd->qhd', score_grad, key_heads, preferred_element_type=...  71.2 us
  transfers between devices with their start and end apart: 17, of which 15 were waited for; matrix products, arithmetic and copies ran while one was open for 13% of the time, Pallas kernels for 0%

commit v1 on v0

v1 whole, which is shorter than its diff:
```python
import functools
import math

import jax
import jax.numpy as jnp
from jax import lax
from jax.experimental import pallas as pl
from jax.experimental.pallas import tpu as pltpu
from jax.sharding import PartitionSpec as P

HEAD_DIM = 72
EPSILON = 1e-06
LOG2E = math.log2(math.e)
GELU_C = 0.7978845608
GELU_A = 0.044715
VMEM = 56 * 1024 * 1024
BF = jnp.bfloat16
F32 = jnp.float32


def nn(a, b):
    return lax.dot_general(a, b, (((1,), (0,)), ((), ())), preferred_element_type=F32)


def nt(a, b):
    return lax.dot_general(a, b, (((1,), (1,)), ((), ())), preferred_element_type=F32)


def tn(a, b):
    return lax.dot_general(a, b, (((0,), (0,)), ((), ())), preferred_element_type=F32)


def params(semantics=None):
    return pltpu.CompilerParams(vmem_limit_bytes=VMEM)


def cost(flops, moved, exps=0):
    return pl.CostEstimate(flops=int(flops), bytes_accessed=int(moved), transcendentals=int(exps))


def normalize(values):
    centred = values - jnp.mean(values, axis=-1, keepdims=True)
    inverse = lax.rsqrt(jnp.mean(centred * centred, axis=-1, keepdims=True) + EPSILON)
    return centred * inverse, inverse


def norm_backward(grad, normed, inverse):
    return inverse * (
        grad
        - jnp.mean(grad, axis=-1, keepdims=True)
        - normed * jnp.mean(grad * normed, axis=-1, keepdims=True)
    )


def project_kernel(tok_ref, mod_ref, w_ref, bias_ref, hid_ref, q_ref, k_ref, v_ref):
    normed, _ = normalize(tok_ref[0].astype(F32))
    hidden = (normed * (1.0 + mod_ref[0, 1:2, :]) + mod_ref[0, 0:1, :]).astype(BF)
    hid_ref[0] = hidden
    heads = q_ref.shape[1]
    size = q_ref.shape[3]
    for which, out in enumerate((q_ref, k_ref, v_ref)):
        proj = nn(hidden, w_ref[which])
        if which == 0:
            proj = proj + bias_ref[0:1, :]
        if which == 2:
            proj = proj + bias_ref[1:2, :]
        proj = proj.astype(BF)
        for h in range(heads):
            out[0, h] = proj[:, h * size : (h + 1) * size]


def project(tokens, mod_blocks, qkv_weight, qv_bias, blocks):
    micro, rows, width = tokens.shape
    share = rows // blocks
    local = qkv_weight.shape[2]
    heads = local // HEAD_DIM
    head_shape = jax.ShapeDtypeStruct((micro, heads, rows, HEAD_DIM), BF)
    head_spec = pl.BlockSpec((1, heads, share, HEAD_DIM), lambda m, b: (m, 0, b, 0))
    return pl.pallas_call(
        project_kernel,
        grid=(micro, blocks),
        in_specs=[
            pl.BlockSpec((1, share, width), lambda m, b: (m, b, 0)),
            pl.BlockSpec((1, 6, width), lambda m, b: (m * blocks + b, 0, 0)),
            pl.BlockSpec(qkv_weight.shape, lambda m, b: (0, 0, 0)),
            pl.BlockSpec(qv_bias.shape, lambda m, b: (0, 0)),
        ],
        out_specs=[
            pl.BlockSpec((1, share, width), lambda m, b: (m, b, 0)),
            head_spec,
            head_spec,
            head_spec,
        ],
        out_shape=[jax.ShapeDtypeStruct(tokens.shape, BF), head_shape, head_shape, head_shape],
        compiler_params=params(),
        cost_estimate=cost(2 * micro * rows * width * 3 * local, 20e6),
        name="project",
    )(tokens, mod_blocks, qkv_weight, qv_bias)


def attend_kernel(info_ref, q_ref, k_ref, v_ref, att_ref, lse_ref):
    heads, share, size = q_ref.shape[1:]
    block = info_ref[0]
    whole = info_ref[1 + pl.program_id(0)]
    factor = size ** (-0.5) * LOG2E

    def run(span):
        for h in range(heads):
            keys = k_ref[0, h, span, :]
            values = v_ref[0, h, span, :]
            scores = nt(q_ref[0, h], keys) * factor
            top = jnp.max(scores, axis=-1, keepdims=True)
            weight = jnp.exp2(scores - top)
            total = jnp.sum(weight, axis=-1, keepdims=True)
            out = nn(weight.astype(BF), values) / total
            att_ref[0, :, h * size : (h + 1) * size] = out.astype(BF)
            lse = jnp.broadcast_to(top + jnp.log2(total), (share, 128))
            lse_ref[0, h : h + 1, :] = lse.T[0:1, :]

    @pl.when(whole == 1)
    def _():
        run(slice(None))

    @pl.when(whole == 0)
    def _():
        run(pl.ds(pl.multiple_of(block * share, share), share))


def attend(info, query, key, value, blocks):
    micro, heads, rows, size = query.shape
    share = rows // blocks
    full = pl.BlockSpec((1, heads, rows, size), lambda m, s: (m, 0, 0, 0))
    return pl.pallas_call(
        attend_kernel,
        grid_spec=pltpu.PrefetchScalarGridSpec(
            num_scalar_prefetch=1,
            grid=(micro,),
            in_specs=[
                pl.BlockSpec((1, heads, share, size), lambda m, s: (m, 0, s[0], 0)),
                full,
                full,
            ],
            out_specs=[
                pl.BlockSpec((1, share, heads * size), lambda m, s: (m, 0, 0)),
                pl.BlockSpec((1, heads, share), lambda m, s: (m, 0, 0)),
            ],
        ),
        out_shape=[
            jax.ShapeDtypeStruct((micro, share, heads * size), BF),
            jax.ShapeDtypeStruct((micro, heads, share), F32),
        ],
        compiler_params=params(),
        cost_estimate=cost(
            4 * micro * heads * share * rows * 256, 6e6, micro * heads * share * rows
        ),
        name="attend",
    )(info, query, key, value)


def middle_kernel(info_ref, a0, a1, a2, a3, w_ref, bias_ref, tok_ref, mod_ref, attn_ref, mid_ref, hid_ref):
    rank = info_ref[0]
    total = bias_ref[0:1, :]
    for shift, part in enumerate((a0, a1, a2, a3)):
        total = total + nn(part[0], w_ref[lax.rem(rank + 4 - shift, 4)])
    attn_ref[0] = total
    mid = tok_ref[0].astype(F32) + mod_ref[0, 2:3, :] * total
    mid_ref[0] = mid
    normed, _ = normalize(mid)
    hid_ref[0] = (normed * (1.0 + mod_ref[0, 4:5, :]) + mod_ref[0, 3:4, :]).astype(BF)


def middle(info, parts, out_full, out_bias, tokens, mod_blocks, blocks):
    micro, share, local = parts[0].shape
    width = tokens.shape[2]
    part = pl.BlockSpec((1, share, local), lambda m, s: (m, 0, 0))
    row = pl.BlockSpec((1, share, width), lambda m, s: (m, 0, 0))
    return pl.pallas_call(
        middle_kernel,
        grid_spec=pltpu.PrefetchScalarGridSpec(
            num_scalar_prefetch=1,
            grid=(micro,),
            in_specs=[part] * 4
            + [
                pl.BlockSpec(out_full.shape, lambda m, s: (0, 0, 0)),
                pl.BlockSpec((1, width), lambda m, s: (0, 0)),
                pl.BlockSpec((1, share, width), lambda m, s: (m, s[0], 0)),
                pl.BlockSpec((1, 6, width), lambda m, s: (m * blocks + s[0], 0, 0)),
            ],
            out_specs=[row, row, row],
        ),
        out_shape=[
            jax.ShapeDtypeStruct((micro, share, width), F32),
            jax.ShapeDtypeStruct((micro, share, width), F32),
            jax.ShapeDtypeStruct((micro, share, width), BF),
        ],
        compiler_params=params(),
        cost_estimate=cost(2 * micro * share * width * width, 12e6),
        name="middle",
    )(info, *parts, out_full, out_bias, tokens, mod_blocks)


def feed_kernel(first, shapes, *refs):
    n_up, n_down = shapes
    xo, xt, go, gt = refs[:4]
    up_parts = refs[4 : 4 + n_up]
    down_parts = refs[4 + n_up : 4 + n_up + n_down]
    at = 4 + n_up + n_down
    bias_ref = refs[at]
    at += 1
    if not first:
        mlp_in, gh_in = refs[at : at + 2]
        at += 2
    mlp_ref, gh_ref, wu_ref, wd_ref, bsum_ref = refs[at : at + 5]
    xs, gs, us, ds, acts, dps = refs[at + 5 :]
    half = xo.shape[0]
    units = us.shape[0]
    step = pl.program_id(0)
    chunk = 256

    @pl.when(step == 0)
    def _():
        xs[:half] = xo[...]
        xs[half:] = xt[...]
        gs[:half] = go[...]
        gs[half:] = gt[...]

    def fill(target, parts):
        start = 0
        for ref in parts:
            block = ref[...]
            block = block.reshape(-1, block.shape[-1])
            target[start : start + block.shape[0]] = block
            start += block.shape[0]

    fill(us, up_parts)
    fill(ds, down_parts)
    bias = bias_ref[0]

    def rows_step(i, sums):
        rows = pl.ds(pl.multiple_of(i * chunk, chunk), chunk)
        pre = nt(xs[rows, :], us[...]) + bias
        square = pre * pre
        tanh = jnp.tanh(GELU_C * pre * (1.0 + GELU_A * square))
        act = (0.5 * pre * (1.0 + tanh)).astype(BF)
        acts[rows, :] = act
        slope = 0.5 * (1.0 + tanh) + (0.5 * GELU_C) * pre * (1.0 - tanh * tanh) * (
            1.0 + 3.0 * GELU_A * square
        )
        dpre = nt(gs[rows, :], ds[...]) * slope
        low = dpre.astype(BF)
        dps[rows, :] = low
        mlp = nn(act, ds[...])
        gh = nn(low, us[...])
        old_mlp = mlp_ref[rows, :]
        old_gh = gh_ref[rows, :]
        mlp_ref[rows, :] = old_mlp + mlp
        gh_ref[rows, :] = old_gh + gh
        return sums + jnp.sum(dpre, axis=0, keepdims=True)

    @pl.when(step == 0)
    def _():
        if first:
            mlp_ref[...] = jnp.zeros_like(mlp_ref)
            gh_ref[...] = jnp.zeros_like(gh_ref)
        else:
            mlp_ref[...] = mlp_in[...]
            gh_ref[...] = gh_in[...]

    bsum_ref[0] = lax.fori_loop(0, 2 * half // chunk, rows_step, jnp.zeros((1, units), F32))
    for start in range(0, units, 256):
        stop = min(start + 256, units)
        wu_ref[0, start:stop] = tn(dps[:, start:stop], xs[...]).astype(BF)
        wd_ref[0, start:stop] = tn(acts[:, start:stop], gs[...]).astype(BF)


def feed(own_x, other_x, own_g, other_g, ups, downs, bias, carry):
    half, width = own_x.shape
    count, _, units = bias.shape
    first = carry is None
    rows = pl.BlockSpec((half, width), lambda k: (0, 0))
    acc = pl.BlockSpec((2 * half, width), lambda k: (0, 0))
    wspec = pl.BlockSpec((1, units, width), lambda k: (k, 0, 0))
    in_specs = [rows] * 4
    operands = [own_x, other_x, own_g, other_g]
    for array, block, index in ups + downs:
        in_specs.append(pl.BlockSpec(block, index))
        operands.append(array)
    in_specs.append(pl.BlockSpec((1, 1, units), lambda k: (k, 0, 0)))
    operands.append(bias)
    if not first:
        in_specs += [acc, acc]
        operands += list(carry)
    return pl.pallas_call(
        functools.partial(feed_kernel, first, (len(ups), len(downs))),
        grid=(count,),
        in_specs=in_specs,
        out_specs=[acc, acc, wspec, wspec, pl.BlockSpec((1, 1, units), lambda k: (k, 0, 0))],
        out_shape=[
            jax.ShapeDtypeStruct((2 * half, width), F32),
            jax.ShapeDtypeStruct((2 * half, width), F32),
            jax.ShapeDtypeStruct((count, units, width), BF),
            jax.ShapeDtypeStruct((count, units, width), BF),
            jax.ShapeDtypeStruct((count, 1, units), F32),
        ],
        scratch_shapes=[
            pltpu.VMEM((2 * half, width), BF),
            pltpu.VMEM((2 * half, width), BF),
            pltpu.VMEM((units, width), BF),
            pltpu.VMEM((units, width), BF),
            pltpu.VMEM((2 * half, units), BF),
            pltpu.VMEM((2 * half, units), BF),
        ],
        compiler_params=params(),
        cost_estimate=cost(
            12 * count * 2 * half * width * units, 20e6 + count * 6e6, count * 2 * half * units
        ),
        name="feed",
    )(*operands)


def between_kernel(
    info_ref, gho, ght, mlpo, mlpt, mid_ref, attn_ref, og_ref, mod_ref, dbias_ref, w_ref,
    a0, a1, a2, a3, layer_ref, gmid_ref, d0, d1, d2, d3, wout_ref, sums_ref,
):
    rank = info_ref[0]
    micro = pl.program_id(0)
    valid = info_ref[1 + micro].astype(F32)
    mod = mod_ref[0]
    mid = mid_ref[0]
    attn = attn_ref[0]
    normed, inverse = normalize(mid)
    mlp_out = mlpo[...] + mlpt[...] + dbias_ref[0:1, :]
    layer_ref[0] = (valid * (mid + mod[5:6, :] * mlp_out)).astype(BF)
    grad_y = og_ref[0].astype(F32) * valid
    grad_hidden = gho[...] + ght[...]
    grad_mid = grad_y + norm_backward(grad_hidden * (1.0 + mod[4:5, :]), normed, inverse)
    gmid_ref[0] = grad_mid
    grad_attn = grad_mid * mod[2:3, :]
    sums_ref[0, 0:1, :] = jnp.sum(grad_mid * attn, axis=0, keepdims=True)
    sums_ref[0, 1:2, :] = jnp.sum(grad_hidden, axis=0, keepdims=True)
    sums_ref[0, 2:3, :] = jnp.sum(grad_hidden * normed, axis=0, keepdims=True)
    sums_ref[0, 3:4, :] = jnp.sum(grad_y * mlp_out, axis=0, keepdims=True)
    sums_ref[0, 4:5, :] = jnp.sum(grad_attn, axis=0, keepdims=True)
    sums_ref[0, 5:6, :] = jnp.sum(grad_y * mod[5:6, :], axis=0, keepdims=True)
    low = grad_attn.astype(BF)
    for shift, (out, part) in enumerate(((d0, a0), (d1, a1), (d2, a2), (d3, a3))):
        out[0] = nt(low, w_ref[lax.rem(rank + 4 - shift, 4)]).astype(BF)
        update = tn(part[0], low)
        wout_ref[shift] = jnp.where(micro == 0, update, wout_ref[shift] + update)


def between(info, feed_own, feed_other, mid, attn, out_grad, mod_blocks, down_bias, out_full, parts, blocks):
    micro, share, width = mid.shape
    local = parts[0].shape[2]
    half = pl.BlockSpec((share, width), lambda m, s: (m, 0))
    row = pl.BlockSpec((1, share, width), lambda m, s: (m, 0, 0))
    part = pl.BlockSpec((1, share, local), lambda m, s: (m, 0, 0))
    mlp_own, gh_own = feed_own
    mlp_other, gh_other = feed_other
    dshape = jax.ShapeDtypeStruct((micro, share, local), BF)
    return pl.pallas_call(
        between_kernel,
        grid_spec=pltpu.PrefetchScalarGridSpec(
            num_scalar_prefetch=1,
            grid=(micro,),
            in_specs=[half] * 4
            + [
                row,
                row,
                pl.BlockSpec((1, share, width), lambda m, s: (m, s[0], 0)),
                pl.BlockSpec((1, 6, width), lambda m, s: (m * blocks + s[0], 0, 0)),
                pl.BlockSpec((1, width), lambda m, s: (0, 0)),
                pl.BlockSpec(out_full.shape, lambda m, s: (0, 0, 0)),
            ]
            + [part] * 4,
            out_specs=[row, row, part, part, part, part]
            + [
                pl.BlockSpec((blocks, local, width), lambda m, s: (0, 0, 0)),
                pl.BlockSpec((1, 8, width), lambda m, s: (m, 0, 0)),
            ],
        ),
        out_shape=[
            jax.ShapeDtypeStruct((micro, share, width), BF),
            jax.ShapeDtypeStruct((micro, share, width), F32),
            dshape,
            dshape,
            dshape,
            dshape,
            jax.ShapeDtypeStruct((blocks, local, width), F32),
            jax.ShapeDtypeStruct((micro, 8, width), F32),
        ],
        compiler_params=params(),
        cost_estimate=cost(4 * micro * share * width * width, 30e6),
        name="between",
    )(info, gh_own, gh_other, mlp_own, mlp_other, mid, attn, out_grad, mod_blocks, down_bias, out_full, *parts)


def attend_back_kernel(
    info_ref, q_ref, k_ref, v_ref, l0, l1, l2, l3, g0, g1, g2, g3, w_ref,
    dq_ref, dk_ref, dv_ref, part_ref, dos, dqs, dks, dvs,
):
    _, heads, rows, size = q_ref.shape
    share = g0.shape[1]
    rank = info_ref[0]
    whole = info_ref[1]
    scale = size ** (-0.5)
    factor = scale * LOG2E
    lses = (l0, l1, l2, l3)
    for shift, grad in enumerate((g0, g1, g2, g3)):
        for h in range(heads):
            dos[h, shift] = grad[0, :, h * size : (h + 1) * size]

    def block_of(shift):
        return pl.multiple_of(lax.rem(rank + shift, 4) * share, share)

    def tile(h, shift, keys, values, keys_t):
        query = q_ref[0, h, pl.ds(block_of(shift), share), :]
        grad = dos[h, shift]
        lse = lses[shift][0, pl.ds(h, 1), :]
        probs = jnp.exp2(nt(keys, query) * factor - lse)
        dprobs = nt(values, grad)
        inner = jnp.sum(probs * dprobs, axis=0, keepdims=True)
        dscores = (probs * (dprobs - inner) * scale).astype(BF)
        dqs[h, pl.ds(block_of(shift), share), :] = nn(keys_t, dscores).T.astype(BF)
        return nn(dscores, query), nn(probs.astype(BF), grad)

    @pl.when(whole == 1)
    def _():
        def head(h, carry):
            keys = k_ref[0, h]
            values = v_ref[0, h]
            keys_t = keys.astype(F32).T.astype(BF)
            dkey, dvalue = tile(h, 0, keys, values, keys_t)
            for shift in range(1, 4):
                more_key, more_value = tile(h, shift, keys, values, keys_t)
                dkey = dkey + more_key
                dvalue = dvalue + more_value
            dks[h] = dkey.astype(BF)
            dvs[h] = dvalue.astype(BF)
            return carry

        lax.fori_loop(0, heads, head, 0)

    @pl.when(whole == 0)
    def _():
        def head(h, carry):
            for shift in range(4):
                span = pl.ds(block_of(shift), share)
                keys = k_ref[0, h, span, :]
                values = v_ref[0, h, span, :]
                dkey, dvalue = tile(h, shift, keys, values, keys.astype(F32).T.astype(BF))
                dks[h, span, :] = dkey.astype(BF)
                dvs[h, span, :] = dvalue.astype(BF)
            return carry

        lax.fori_loop(0, heads, head, 0)

    for src, dst in ((dqs, dq_ref), (dks, dk_ref), (dvs, dv_ref)):
        for h in range(heads):
            dst[:, h * size : (h + 1) * size] = src[h]

    def out_rows(i, carry):
        span = pl.ds(pl.multiple_of(i * share, share), share)
        part_ref[span, :] = (
            nt(dq_ref[span, :], w_ref[0]) + nt(dk_ref[span, :], w_ref[1]) + nt(dv_ref[span, :], w_ref[2])
        ).astype(BF)
        return carry

    lax.fori_loop(0, rows // share, out_rows, 0)


def attend_back(micro, info, query, key, value, lses, grads, qkv_weight):
    _, heads, rows, size = query.shape
    share = rows // 4
    local = heads * size
    width = qkv_weight.shape[1]
    full = pl.BlockSpec((1, heads, rows, size), lambda i, s: (micro, 0, 0, 0))
    return pl.pallas_call(
        attend_back_kernel,
        grid_spec=pltpu.PrefetchScalarGridSpec(
            num_scalar_prefetch=1,
            grid=(1,),
            in_specs=[full] * 3
            + [pl.BlockSpec((1, heads, share), lambda i, s: (micro, 0, 0))] * 4
            + [pl.BlockSpec((1, share, local), lambda i, s: (micro, 0, 0))] * 4
            + [pl.BlockSpec(qkv_weight.shape, lambda i, s: (0, 0, 0))],
            out_specs=[pl.BlockSpec((rows, local), lambda i, s: (0, 0))] * 3
            + [pl.BlockSpec((rows, width), lambda i, s: (0, 0))],
            scratch_shapes=[
                pltpu.VMEM((heads, 4, share, size), BF),
                pltpu.VMEM((heads, rows, size), BF),
                pltpu.VMEM((heads, rows, size), BF),
                pltpu.VMEM((heads, rows, size), BF),
            ],
        ),
        out_shape=[jax.ShapeDtypeStruct((rows, local), BF)] * 3
        + [jax.ShapeDtypeStruct((rows, width), BF)],
        compiler_params=params(),
        cost_estimate=cost(10 * heads * rows * rows * 256, 12e6, heads * rows * rows),
        name="attend_back",
    )(info, query, key, value, *lses, *grads, qkv_weight)


def finish_kernel(info_ref, grad_ref, tok_ref, mod_ref, gmid_ref, out_ref, sums_ref):
    normed, inverse = normalize(tok_ref[0].astype(F32))
    grad = grad_ref[0].astype(F32)
    out_ref[0] = gmid_ref[0] + norm_backward(grad * (1.0 + mod_ref[0, 1:2, :]), normed, inverse)
    sums_ref[0, 0:1, :] = jnp.sum(grad, axis=0, keepdims=True)
    sums_ref[0, 1:2, :] = jnp.sum(grad * normed, axis=0, keepdims=True)


def finish(info, grad, tokens, mod_blocks, gmid, blocks):
    micro, share, width = gmid.shape
    row = pl.BlockSpec((1, share, width), lambda m, s: (m, 0, 0))
    return pl.pallas_call(
        finish_kernel,
        grid_spec=pltpu.PrefetchScalarGridSpec(
            num_scalar_prefetch=1,
            grid=(micro,),
            in_specs=[
                row,
                pl.BlockSpec((1, share, width), lambda m, s: (m, s[0], 0)),
                pl.BlockSpec((1, 6, width), lambda m, s: (m * blocks + s[0], 0, 0)),
                row,
            ],
            out_specs=[row, pl.BlockSpec((1, 2, width), lambda m, s: (m, 0, 0))],
        ),
        out_shape=[
            jax.ShapeDtypeStruct((micro, share, width), F32),
            jax.ShapeDtypeStruct((micro, 2, width), F32),
        ],
        compiler_params=params(),
        cost_estimate=cost(micro * share * width * 20, 8e6),
        name="finish",
    )(info, grad, tokens, mod_blocks, gmid)


def turn(array, shift):
    count = lax.axis_size("tensor")
    return lax.ppermute(array, "tensor", [(i, (i + shift) % count) for i in range(count)])


def flip(array, bit):
    return lax.ppermute(array, "dp", [(i, i ^ bit) for i in range(lax.axis_size("dp"))])


def by_rank(array, rank, axis):
    count = array.shape[axis]
    index = jnp.mod(rank - jnp.arange(count), count)
    return jnp.take(array, index, axis=axis)


def by_quarter(array, quarter, axis):
    index = jnp.bitwise_xor(jnp.arange(4), quarter)
    return jnp.take(array, index, axis=axis)


def add(a, b):
    return (a.astype(F32) + b.astype(F32)).astype(BF)


CORE, SIDE_X, SIDE_Y = 1, 2, 4


def local(
    tokens, conditioning, lengths, out_grad, ada_weight, ada_bias, qkv_weight, qv_bias,
    out_weight, out_bias, up_weight, up_bias, down_weight, down_bias,
):
    groups = lax.axis_size("tensor")
    dp = lax.axis_size("dp")
    rank = lax.axis_index("tensor")
    place = lax.axis_index("dp")
    core = jnp.bitwise_and(place, 1)
    quarter = jnp.bitwise_and(place >> 1, 3)
    micro, rows, width = tokens.shape
    share = rows // groups
    slots = lengths.shape[1]
    part = up_weight.shape[1]
    half = part // 2
    piece = half // 4
    columns = ada_weight.shape[1]

    up_half = lax.dynamic_slice_in_dim(up_weight, core * half, half, 1).T
    down_half = lax.dynamic_slice_in_dim(down_weight, core * half, half, 0)
    mine = jnp.concatenate(
        [
            lax.dynamic_slice_in_dim(up_half, quarter * piece, piece, 0),
            lax.dynamic_slice_in_dim(down_half, quarter * piece, piece, 0),
        ]
    )
    received = [turn(mine, k) for k in (1, 2, 3)]
    up0 = jnp.stack([r[:piece] for r in received])
    down0 = jnp.stack([r[piece:] for r in received])
    up_x = flip(up0, SIDE_X)
    down_y = flip(down0, SIDE_Y)
    up_y = flip(jnp.stack([up0, up_x]), SIDE_Y)
    down_x = flip(jnp.stack([down0, down_y]), SIDE_X)
    out_full = lax.all_gather(out_weight, "tensor", axis=0)

    cond_float = conditioning.astype(F32)
    cond_act = jax.nn.silu(cond_float).astype(BF).reshape(micro * slots, width)
    ada_part = jnp.dot(cond_act, ada_weight, preferred_element_type=F32) + ada_bias
    small = jnp.concatenate([ada_part, jnp.pad(up_bias, (0, columns - part))[None]])
    gathered = lax.all_gather(small, "tensor", axis=0)
    modulation = gathered[:, : micro * slots].transpose(1, 0, 2).reshape(micro, slots, 6 * width)
    boundary = jnp.cumsum(lengths, axis=1)
    starts = jnp.arange(groups, dtype=jnp.int32) * share
    segment = jnp.sum((boundary[:, None, :] <= starts[None, :, None]).astype(jnp.int32), axis=2)
    onehot = (segment[:, :, None] == jnp.arange(slots)[None, None, :]).astype(F32)
    mod_blocks = jnp.sum(onehot[:, :, :, None] * modulation[:, None], axis=2)
    mod_blocks = mod_blocks.reshape(micro * groups, 6, width)
    whole = (segment[:, groups - 1] == 0).astype(jnp.int32)
    valid = (segment < slots).astype(jnp.int32)
    own_valid = lax.dynamic_index_in_dim(valid, rank, 1, False)
    own_gate = lax.dynamic_index_in_dim(
        mod_blocks.reshape(micro, groups, 6, width), rank, 1, False
    )[:, 5:6]

    bias_all = by_rank(gathered[:, micro * slots, :part], rank, 0).reshape(groups, 2, half)
    bias_all = lax.dynamic_index_in_dim(bias_all, core, 1, False)
    bias_rel = by_quarter(bias_all.reshape(groups, 4, piece), quarter, 1).reshape(groups, half)
    bias_own = bias_all[0].reshape(1, 1, half)
    bias_far = bias_rel[1:].reshape(groups - 1, 1, half)

    hidden_one, query, key, value = project(tokens, mod_blocks, qkv_weight, qv_bias, groups)

    own_grad = lax.dynamic_slice_in_dim(out_grad, rank * share, share, 1).astype(F32)
    grad_mlp = own_grad * (own_valid.astype(F32)[:, None, None] * own_gate)
    own_g = grad_mlp.astype(BF).reshape(micro * share, width)
    other_g = flip(own_g, CORE)

    att = [None] * groups
    lse = [None] * groups
    parts = [None] * groups
    for shift in (1, 2, 3, 0):
        info = jnp.concatenate([jnp.mod(rank + shift, groups)[None], whole])
        att[shift], lse[shift] = attend(info, query, key, value, groups)
        parts[shift] = turn(att[shift], shift) if shift else att[shift]

    rank_info = rank[None]
    attn, mid, hidden_two = middle(
        rank_info, parts, out_full, out_bias[None], tokens, mod_blocks, groups
    )
    own_x = hidden_two.reshape(micro * share, width)
    other_x = flip(own_x, CORE)

    near = lambda k: (0, 0)
    far = lambda k: (k, 0, 0)
    pair = lambda k: (0, k, 0, 0)
    mlp, gh, wu0, wd0, bsum0 = feed(
        own_x, other_x, own_g, other_g,
        [(up_half, (half, width), near)],
        [(down_half, (half, width), near)],
        bias_own, None,
    )
    one = (1, piece, width)
    two = (2, 1, piece, width)
    mlp, gh, wu, wd, bsum = feed(
        own_x, other_x, own_g, other_g,
        [(up0, one, far), (up_x, one, far), (up_y, two, pair)],
        [
            (down0, one, far),
            (down_x, (1, 1, piece, width), lambda k: (0, k, 0, 0)),
            (down_y, one, far),
            (down_x, (1, 1, piece, width), lambda k: (1, k, 0, 0)),
        ],
        bias_far, (mlp, gh),
    )
    mine_rows = micro * share
    passed = flip(jnp.stack([mlp[mine_rows:], gh[mine_rows:]]), CORE)
    layer_out, grad_mid, d0, d1, d2, d3, out_wgrad, sums = between(
        jnp.concatenate([rank_info, own_valid]),
        (mlp[:mine_rows], gh[:mine_rows]),
        (passed[0], passed[1]),
        mid, attn, out_grad, mod_blocks, down_bias[None], out_full, parts, groups,
    )
    grads = [d0] + [turn(d, -k) for k, d in ((1, d1), (2, d2), (3, d3))]

    pieces = []
    shares = []
    for m in range(micro):
        info = jnp.stack([rank, whole[m]])
        dq, dk, dv, partial = attend_back(m, info, query, key, value, lse, grads, qkv_weight)
        pieces.append((dq, dk, dv))
        shares.append(lax.psum_scatter(partial, "tensor", scatter_dimension=0, tiled=True))
    tokens_grad, sums_one = finish(
        rank_info, jnp.stack(shares), tokens, mod_blocks, grad_mid, groups
    )

    wu = wu.reshape(groups - 1, 4, piece, width)
    wd = wd.reshape(groups - 1, 4, piece, width)
    wu0 = by_quarter(wu0.reshape(1, 4, piece, width), quarter, 1)
    wd0 = by_quarter(wd0.reshape(1, 4, piece, width), quarter, 1)
    wu = jnp.concatenate([wu0, wu])
    wd = jnp.concatenate([wd0, wd])
    wu = add(wu[:, :2], flip(wu[:, 2:], SIDE_Y))
    wd = wd.reshape(groups, 2, 2, piece, width)
    wd = add(wd[:, :, 0], flip(wd[:, :, 1], SIDE_X))
    wu = add(wu[:, 0], flip(wu[:, 1], SIDE_X))
    wd = add(wd[:, 0], flip(wd[:, 1], SIDE_Y))
    summed = jnp.stack([wu, wd], axis=1)
    arrived = [summed[0]] + [turn(summed[k], -k) for k in (1, 2, 3)]
    total = sum(a.astype(F32) for a in arrived).astype(BF)
    bit = 8
    while bit < dp:
        total = add(total, flip(total, bit))
        bit *= 2
    both = jnp.stack([total, flip(total, SIDE_X)], axis=1)
    both = jnp.concatenate([both, flip(both, SIDE_Y)], axis=1)
    both = by_quarter(both, quarter, 1).reshape(2, half, width)
    away = flip(both, CORE)
    low = jnp.where(core == 0, both, away)
    high = jnp.where(core == 0, away, both)
    both = jnp.concatenate([low, high], axis=1).astype(F32)
    up_weight_grad = both[0].T
    down_weight_grad = both[1]

    stacked = [jnp.stack([pieces[m][i] for m in range(micro)]) for i in range(3)]
    attn_grads = [
        jnp.einsum("mte,mtd->ed", s, hidden_one, preferred_element_type=F32).astype(BF)
        for s in stacked
    ]
    out_low = out_wgrad.astype(BF)
    out_mine = [out_low[0]] + [turn(out_low[k], -k) for k in (1, 2, 3)]
    attn_grads.append(sum(a.astype(F32) for a in out_mine).astype(BF))
    block = jnp.concatenate(attn_grads)
    size = block.shape[0] // 2
    for bit in (CORE, SIDE_X, SIDE_Y):
        side = (jnp.bitwise_and(place, bit) > 0).astype(jnp.int32)
        keep = lax.dynamic_slice_in_dim(block, side * size, size, 0)
        give = lax.dynamic_slice_in_dim(block, (1 - side) * size, size, 0)
        block = add(keep, flip(give, bit))
        size //= 2
    bit = 8
    while bit < dp:
        block = add(block, flip(block, bit))
        bit *= 2
    for bit in (SIDE_Y, SIDE_X, CORE):
        side = jnp.bitwise_and(place, bit) > 0
        other = flip(block, bit)
        block = jnp.concatenate(
            [jnp.where(side, other, block), jnp.where(side, block, other)]
        )
    block = block.astype(F32)
    local_width = qkv_weight.shape[2]
    qkv_weight_grad = block[: 3 * local_width].reshape(3, local_width, width).transpose(0, 2, 1)
    out_weight_grad = block[3 * local_width :]

    qv_sums = jnp.stack(
        [jnp.sum(stacked[0].astype(F32), axis=(0, 1)), jnp.sum(stacked[2].astype(F32), axis=(0, 1))]
    )
    bsum_rel = by_quarter(bsum.reshape(groups - 1, 4, piece), quarter, 1).reshape(groups - 1, half)
    up_sums = by_rank(jnp.concatenate([bsum0.reshape(1, half), bsum_rel]), rank, 0)
    early = jnp.concatenate([sums.reshape(-1), up_sums.reshape(-1)])
    late = jnp.concatenate([sums_one.reshape(-1), qv_sums.reshape(-1)])
    early = lax.all_gather(early, ("dp", "tensor"), axis=0).reshape(dp, groups, -1)
    late = lax.all_gather(late, ("dp", "tensor"), axis=0).reshape(dp, groups, -1)
    n_sums = micro * 8 * width
    rows_early = early[:, :, :n_sums].reshape(dp, groups, micro, 8, width)
    rows_late = late[:, :, : micro * 2 * width].reshape(dp, groups, micro, 2, width)
    out_bias_grad = jnp.sum(rows_early[:, :, :, 4], axis=(0, 1, 2))
    down_bias_grad = jnp.sum(rows_early[:, :, :, 5], axis=(0, 1, 2))
    up_all = early[:, :, n_sums:].reshape(dp // 2, 2, groups, groups, half)
    up_all = jnp.sum(lax.dynamic_index_in_dim(up_all, rank, 3, False), axis=(0, 2))
    up_bias_grad = up_all.reshape(part)
    qv_all = late[:, :, micro * 2 * width :].reshape(dp, groups, 2, local_width)
    qv_bias_grad = jnp.sum(lax.dynamic_index_in_dim(qv_all, rank, 1, False), axis=0)

    segments = lax.all_gather(segment, "dp", axis=0)
    pick = (segments[..., None] == jnp.arange(slots)).astype(F32)
    mod_rows = jnp.concatenate([rows_late, rows_early[:, :, :, :4]], axis=3)
    mod_rows = mod_rows.reshape(dp, groups, micro, 6 * width)
    own_columns = lax.dynamic_slice_in_dim(mod_rows, rank * columns, columns, 3)
    mod_grad = jnp.sum(
        pick.transpose(0, 2, 1, 3)[..., None] * own_columns[:, :, :, None], axis=1
    )
    ada_bias_grad = jnp.sum(mod_grad, axis=(0, 1, 2))
    mod_low = mod_grad.astype(BF).reshape(dp, micro * slots, columns)
    acts = lax.all_gather(cond_act, "dp", axis=0)
    ada_weight_grad = jnp.einsum("psd,pse->de", acts, mod_low, preferred_element_type=F32)
    own_mod = lax.dynamic_index_in_dim(mod_low, place, 0, False)
    cond_part = jnp.einsum("se,de->sd", own_mod, ada_weight, preferred_element_type=F32)
    cond_grad = (cond_part + turn(cond_part, 1) + turn(cond_part, 2) + turn(cond_part, 3)).reshape(
        micro, slots, width
    )
    sigmoid = jax.nn.sigmoid(cond_float)
    conditioning_grad = cond_grad * (sigmoid * (1.0 + cond_float * (1.0 - sigmoid)))

    return (
        layer_out,
        tokens_grad,
        conditioning_grad,
        ada_weight_grad,
        ada_bias_grad,
        qkv_weight_grad,
        qv_bias_grad,
        out_weight_grad,
        out_bias_grad,
        up_weight_grad,
        up_bias_grad,
        down_weight_grad,
        down_bias_grad,
    )


def solution(mesh):
    placed = (
        P(None, "dp", None),
        P(None, "dp", None),
        P(None, "dp"),
        P(None, "dp", None),
        P(None, "tensor"),
        P("tensor"),
        P(None, None, "tensor"),
        P(None, "tensor"),
        P("tensor", None),
        P(),
        P(None, "tensor"),
        P("tensor"),
        P("tensor", None),
        P(),
    )
    return jax.shard_map(
        local,
        mesh=mesh,
        in_specs=placed,
        out_specs=(
            P(None, ("dp", "tensor"), None),
            P(None, ("dp", "tensor"), None),
            P(None, "dp", None),
            P(None, "tensor"),
            P("tensor"),
            P(None, None, "tensor"),
            P(None, "tensor"),
            P("tensor", None),
            P(),
            P(None, "tensor"),
            P("tensor"),
            P("tensor", None),
            P(),
        ),
        check_vma=False,
    )
```

time: 2040 us -> 929 us (0.46)
  waiting for transfers between devices: 1210 us -> 363 us
  matrix products: 406 us -> 23.4 us
  Pallas kernels: 0 us -> 192 us
  blocking collectives: 157 us -> 97.7 us
  other arithmetic: 144 us -> 92.9 us
  starting transfers between devices: 1.7 us -> 42.5 us
    psum x2 -> x0, waiting for transfers between devices: 650 us -> none  [the longest x1 326 us: local(): attn_out = lax.psum(attn_part, 'tensor') + out_bias]
    dot_general x65 -> x6, matrix products: 406 us -> 23.4 us  [the longest x3 12.9 us: local(): jnp.einsum('mte,mtd->ed', s, hidden_one, preferred_element_type=F32)]
    reduce_scatter x8 -> x2, waiting for transfers between devices: 373 us -> 0.01 us  [local(): lax.psum_scatter(partial, 'tensor', scatter_dimension=0, tiled=True)]
    ppermute x0 -> x38, waiting for transfers between devices: none -> 229 us  [the longest x20 122 us: flip(): lax.ppermute(array, 'dp', [(i, i ^ bit) for i in range(lax.axis_size('dp'...]
    pallas_call x0 -> x12, Pallas kernels: none -> 192 us  [the longest x2 73.8 us: feed(): pl.pallas_call(functools.partial(feed_kernel, first, (len(ups), len(downs...]
    all_gather x5 -> x2, waiting for transfers between devices: 126 us -> 26.7 us  [the longest x1 17.3 us: local(): lax.all_gather(early, ('dp', 'tensor'), axis=0).reshape(dp, groups, -1)]
    reduce_sum x18 -> x8, other arithmetic: 73.2 us -> 9.38 us  [the longest x1 3.64 us: local(): down_bias_grad = jnp.sum(rows_early[:, :, :, 5], axis=(0, 1, 2))]
    unnamed x248 -> x97, local copies, waits for them, and re-layouts: 82.2 us -> 24.3 us
  transfers between devices with their start and end apart: 17 -> 43, of which waited for: 15 -> 18; matrix products, arithmetic and copies ran while one was open for 13% -> 19% of each run, Pallas kernels for 0% -> 16%
where the time goes in v1:
time: 929 us; the launch traced here: 916 us
  waiting for transfers between devices  363 us (39%)
  Pallas kernels  192 us (21%)
  blocking collectives  97.7 us (11%)
  other arithmetic  92.9 us (10%)
  local copies, waits for them, and re-layouts  90 us (10%)
  starting transfers between devices  42.5 us (5%)
  matrix products  23.4 us (3%)
  between operations  15.2 us (2%)
    ppermute x20, waiting for transfers between devices, flip(): lax.ppermute(array, 'dp', [(i, i ^ bit) for i in range(lax.axis_size('dp'...  122 us
    ppermute x18, waiting for transfers between devices, turn(): lax.ppermute(array, 'tensor', [(i, (i + shift) % count) for i in range(co...  108 us
    unnamed x6, waiting for transfers between devices  107 us
    pallas_call x2, Pallas kernels, feed(): pl.pallas_call(functools.partial(feed_kernel, first, (len(ups), len(downs...  73.8 us
    all_gather x1, blocking collectives, local(): gathered = lax.all_gather(small, 'tensor', axis=0)  61.7 us
    pallas_call x2, Pallas kernels, attend_back(): pl.pallas_call(attend_back_kernel, grid_spec=pltpu.PrefetchScalarGridSpec...  46.2 us
    ppermute x18, starting transfers between devices, turn(): lax.ppermute(array, 'tensor', [(i, (i + shift) % count) for i in range(co...  28.1 us
    pallas_call x4, Pallas kernels, attend(): pl.pallas_call(attend_kernel, grid_spec=pltpu.PrefetchScalarGridSpec(num_...  27.4 us
  transfers between devices with their start and end apart: 43, of which 18 were waited for; matrix products, arithmetic and copies ran while one was open for 19% of the time, Pallas kernels for 16%

profile of v1, /device:TPU:10, one launch (start us, length us, event | category | flops | bytes accessed | tf_op | source)
XLA Modules:
  0.0 916.2 jit_solution(16363724464501821080)
XLA Ops:
  18.4 3.3 convolution_add_fusion
  21.7 61.7 %all-gather.5 = f32[4,9,1728]{2,1,0:T(8,128)S(1)} all-gather(f32[1,9,1728]{2,1,0:T(8,128)S(1)} %maximum_bitcast_fusion), channel_id=2, replica_groups=mesh['dp'=8,'tensor'=4] {'tensor'}, dimensions={0}, use_global_device_ids=true | all-gather | bytes 311040 | tf_op jit(solution)/shard_map/all_gather | solution.py:604
  86.0 4.2 copy.171.w_ref
  90.2 15.9 %project.1 = (bf16[2,1024,1152]{2,1,0:T(8,128)(2,1)}, bf16[2,4,1024,72]{3,2,1,0:T(8,128)(2,1)}, bf16[2,4,1024,72]{3,2,1,0:T(8,128)(2,1)}, bf16[2,4,1024,72]{3,2,1,0:T(8,128)(2,1)}) custom-call(bf16[2,1024,1152]{2,1,0:T(8,128)(2,1)} %tok_ref.5, f32[8,6,1152]{2,1,0:T(8,128)} %reshape.262.mod_ref, bf16[3,1152,288]{2,1,0:T(8,128)(2,1)} %copy.171.w_ref, ...), custom_call_target="tpu_custom_call" | custom-call | flops 4076863488 | bytes 20000000 | tf_op jit(solution)/shard_map/project/pallas_call | solution.py:79
  106.7 6.8 attend.7
  114.7 6.9 attend.6
  129.3 2.5 multiply_convert_fusion
  131.8 6.9 attend.5
  138.8 2.9 collective-permute-start
  146.2 3.8 collective-permute-start.10
  154.6 6.8 attend.4
  161.5 20.6 %collective-permute-done.a1 = bf16[2,256,288]{2,1,0:T(8,128)(2,1)} collective-permute-done((bf16[2,256,288]{2,1,0:T(8,128)(2,1)}, bf16[2,256,288]{2,1,0:T(8,128)(2,1)}, u32[]{:S(2)}, u32[]{:S(2)}) %collective-permute-start) | collective-permute-done | bytes 294944 | tf_op jit(solution)/shard_map/ppermute | solution.py:540
  182.1 9.3 %all-gather.11.cloned.1.call-done = bf16[1152,1152]{1,0:T(8,128)(2,1)} async-done(((bf16[288,1152]{1,0:T(8,128)(2,1)}), bf16[1152,1152]{1,0:T(8,128)(2,1)}) %all-gather.11.cloned.1.call-update) | async-done | bytes 2654224 | tf_op jit(solution)/shard_map/all_gather | solution.py:598
  191.4 7.4 middle.1
  199.0 2.8 pad_maximum_fusion.7
  202.4 2.7 pad_maximum_fusion.6
  207.3 2.5 constant_dynamic-slice_fusion.4.refs_5_
  209.8 26.9 %feed.2 = (f32[1024,1152]{1,0:T(8,128)}, f32[1024,1152]{1,0:T(8,128)}, bf16[1,576,1152]{2,1,0:T(8,128)(2,1)}, bf16[1,576,1152]{2,1,0:T(8,128)(2,1)}, f32[1,1,576]{2,1,0:T(1,128)}) custom-call(bf16[512,1152]{1,0:T(8,128)(2,1)} %bitcast.220, bf16[512,1152]{1,0:T(8,128)(2,1)} %collective-permute-done.3.refs_1_, bf16[512,1152]{1,0:T(8,128)(2,1)} %bitcast.10.refs_2_, ...), custom_call_target="tpu_custom_call" | custom-call | flops 8153726976 | bytes 26000000 | tf_op jit(solution)/shard_map/feed/pallas_call | solution.py:293
  239.0 8.7 collective-permute-done.11.refs_8_.refs_10_
  247.7 3.0 collective-permute-done.9.refs_6_
  250.7 46.9 %feed.3 = (f32[1024,1152]{1,0:T(8,128)}, f32[1024,1152]{1,0:T(8,128)}, bf16[3,576,1152]{2,1,0:T(8,128)(2,1)}, bf16[3,576,1152]{2,1,0:T(8,128)(2,1)}, f32[3,1,576]{2,1,0:T(1,128)}) custom-call(bf16[512,1152]{1,0:T(8,128)(2,1)} %bitcast.221, bf16[512,1152]{1,0:T(8,128)(2,1)} %collective-permute-done.3.refs_1_, bf16[512,1152]{1,0:T(8,128)(2,1)} %bitcast.10.refs_2_, ...), custom_call_target="tpu_custom_call" | custom-call | flops 24461180928 | bytes 38000000 | tf_op jit(solution)/shard_map/feed/pallas_call | solution.py:293
  297.6 3.5 fusion.4
  312.8 2.7 pad_maximum_fusion
  315.5 44.6 %collective-permute-done.30 = bf16[4,2,144,1152]{3,2,1,0:T(8,128)(2,1)} collective-permute-done((bf16[4,2,144,1152]{3,2,1,0:T(8,128)(2,1)}, bf16[4,2,144,1152]{3,2,1,0:T(8,128)(2,1)}, u32[]{:S(2)}, u32[]{:S(2)}) %collective-permute-start.30) | collective-permute-done | bytes 2654240 | tf_op jit(solution)/shard_map/ppermute | solution.py:544
  360.1 2.3 fusion
  364.0 4.4 collective-permute-done.28
  375.2 19.8 %collective-permute-done.31 = bf16[4,144,1152]{2,1,0:T(8,128)(2,1)} collective-permute-done((bf16[4,144,1152]{2,1,0:T(8,128)(2,1)S(1)}, bf16[4,144,1152]{2,1,0:T(8,128)(2,1)}, u32[]{:S(2)}, u32[]{:S(2)}) %collective-permute-start.31) | collective-permute-done | bytes 1327136 | tf_op jit(solution)/shard_map/ppermute | solution.py:544
  404.7 4.9 slice_bitcast_fusion.2
  409.5 16.6 %between.1 = (bf16[2,256,1152]{2,1,0:T(8,128)(2,1)}, f32[2,256,1152]{2,1,0:T(8,128)}, bf16[2,256,288]{2,1,0:T(8,128)(2,1)}, bf16[2,256,288]{2,1,0:T(8,128)(2,1)}...) custom-call(s32[3]{0:T(128)} %pad_add_fusion.info_ref, ...), custom_call_target="tpu_custom_call" | custom-call | flops 2717908992 | bytes 30000000 | tf_op jit(solution)/shard_map/between/pallas_call | solution.py:361
  427.6 2.9 collective-permute-start.14
  430.6 2.8 convert_element_type.214
  436.2 36.6 %collective-permute-done.13.g1 = bf16[2,256,288]{2,1,0:T(8,128)(2,1)S(1)} collective-permute-done((bf16[2,256,288]{2,1,0:T(8,128)(2,1)}, bf16[2,256,288]{2,1,0:T(8,128)(2,1)S(1)}, u32[]{:S(2)}, u32[]{:S(2)}) %collective-permute-start.13) | collective-permute-done | bytes 294944 | tf_op jit(solution)/shard_map/ppermute | solution.py:540
  472.8 26.7 %collective-permute-done.14.g2 = bf16[2,256,288]{2,1,0:T(8,128)(2,1)S(1)} collective-permute-done((bf16[2,256,288]{2,1,0:T(8,128)(2,1)}, bf16[2,256,288]{2,1,0:T(8,128)(2,1)S(1)}, u32[]{:S(2)}, u32[]{:S(2)}) %collective-permute-start.14) | collective-permute-done | bytes 294944 | tf_op jit(solution)/shard_map/ppermute | solution.py:540
  499.5 3.3 collective-permute-start.20
  502.8 5.1 collective-permute-done.15.g3
  507.9 2.4 collective-permute-start.21
  510.3 18.4 %attend_back.2 = (bf16[1024,288]{1,0:T(8,128)(2,1)}, bf16[1024,288]{1,0:T(8,128)(2,1)}, bf16[1024,288]{1,0:T(8,128)(2,1)}, bf16[1024,1152]{1,0:T(8,128)(2,1)}) custom-call(s32[2]{0:T(128)} %get-tuple-element.235.info_ref, bf16[2,4,1024,72]{3,2,1,0:T(8,128)(2,1)} %get-tuple-element.57.q_ref, bf16[2,4,1024,72]{3,2,1,0:T(8,128)(2,1)} %get-tuple-element.58.k_ref, ...), custom_call_target="tpu_custom_call" | custom-call | flops 10737418240 | bytes 12000000 | tf_op jit(solution)/shard_map/attend_back/pallas_call | solution.py:478
  528.8 27.9 %attend_back.3 = (bf16[1024,288]{1,0:T(8,128)(2,1)}, bf16[1024,288]{1,0:T(8,128)(2,1)}, bf16[1024,288]{1,0:T(8,128)(2,1)}, bf16[1024,1152]{1,0:T(8,128)(2,1)}) custom-call(s32[2]{0:T(128)} %get-tuple-element.236.info_ref, bf16[2,4,1024,72]{3,2,1,0:T(8,128)(2,1)} %get-tuple-element.57.q_ref, bf16[2,4,1024,72]{3,2,1,0:T(8,128)(2,1)} %get-tuple-element.58.k_ref, ...), custom_call_target="tpu_custom_call" | custom-call | flops 10737418240 | bytes 12000000 | tf_op jit(solution)/shard_map/attend_back/pallas_call | solution.py:478
  556.6 4.4 fusion.7
  561.1 4.3 fusion.8
  565.4 4.2 fusion.9
  572.4 4.8 pad_maximum_fusion.3
  578.5 18.6 %collective-permute-done.34 = bf16[2,144,1152]{2,1,0:T(8,128)(2,1)S(1)} collective-permute-done((bf16[2,144,1152]{2,1,0:T(8,128)(2,1)S(1)}, bf16[2,144,1152]{2,1,0:T(8,128)(2,1)S(1)}, u32[]{:S(2)}, u32[]{:S(2)}) %collective-permute-start.34) | collective-permute-done | bytes 663584 | tf_op jit(solution)/shard_map/ppermute | solution.py:540
  599.1 15.5 %collective-permute-done.35 = bf16[2,144,1152]{2,1,0:T(8,128)(2,1)S(1)} collective-permute-done((bf16[2,144,1152]{2,1,0:T(8,128)(2,1)S(1)}, bf16[2,144,1152]{2,1,0:T(8,128)(2,1)S(1)}, u32[]{:S(2)}, u32[]{:S(2)}) %collective-permute-start.35) | collective-permute-done | bytes 663584 | tf_op jit(solution)/shard_map/ppermute | solution.py:544
  622.5 26.3 %all-gather.6 = s32[8,2,4]{2,1,0:T(2,128)S(1)} all-gather(s32[1,2,4]{2,1,0:T(2,128)S(1)} %bitcast.217), channel_id=4, replica_groups=mesh['dp'=8,'tensor'=4] {'dp'}, dimensions={0}, use_global_device_ids=true | all-gather | bytes 288 | tf_op jit(solution)/shard_map/all_gather | solution.py:769
  648.9 9.6 %all_gather.43 = bf16[8,8,1152]{2,1,0:T(8,128)(2,1)S(1)} all-gather(bf16[1,8,1152]{2,1,0:T(8,128)(2,1)S(1)} %all_gather_reshape.3), channel_id=1, replica_groups=mesh['dp'=8,'tensor'=4] {'dp'}, dimensions={0}, use_global_device_ids=true | all-gather | bytes 165888 | tf_op jit(solution)/shard_map/all_gather | solution.py:779
  661.8 2.3 gather_fusion.4
  670.2 7.6 collective-permute-done.24
  678.9 8.4 collective-permute-done.25
  696.1 8.7 collective-permute-done.26
  707.5 4.1 broadcast_select_fusion.1
  711.6 2.4 maximum_convert_fusion
  714.0 4.8 slice_bitcast_fusion
  718.8 6.9 copy.197
  725.7 2.4 pad_maximum_fusion.12.grad_ref
  728.1 4.6 finish.1
  734.8 17.3 %all-gather.13.cloned.1.call-done = f32[32,1,20736]{2,1,0:T(1,128)} async-done(((f32[1,1,20736]{2,1,0:T(1,128)}), f32[32,1,20736]{2,1,0:T(1,128)}) %all-gather.13.cloned.1.call-update) | async-done | bytes 2654224 | tf_op jit(solution)/shard_map/all_gather | solution.py:756
  752.1 8.1 reduce.9
  766.3 2.9 slice.227
  770.3 3.6 slice_reduce_fusion
  779.7 106.6 %all-reduce.4.cloned.1.call-done = f32[165888]{0:T(1024)} async-done(((f32[165888]{0:T(1024)}), f32[165888]{0:T(1024)}) %all-reduce.4.cloned.1.call-update) | async-done | bytes 663568
  891.2 2.3 reshape.390
  896.1 2.8 fusion.35
  902.4 4.5 convolution_bitcast_fusion
  (304 shorter events, 136.0 us)
Async XLA Ops:
  7.2 10.5 %copy-start.34 = (s32[2,4]{1,0:T(2,128)S(1)}, s32[2,4]{1,0:T(2,128)}, u32[]{:S(2)}) copy-start(s32[2,4]{1,0:T(2,128)} %param.18) | copy-start | bytes 100
  7.2 11.1 %copy-start.25 = (bf16[2,4,1152]{2,1,0:T(4,128)(2,1)S(1)}, bf16[2,4,1152]{2,1,0:T(4,128)(2,1)}, u32[]{:S(2)}) copy-start(bf16[2,4,1152]{2,1,0:T(4,128)(2,1)} %param.17) | copy-start | bytes 55300
  7.2 11.2 %copy-start.29 = (f32[1152]{0:T(1024)S(1)}, f32[1152]{0:T(1024)}, u32[]{:S(2)}) copy-start(f32[1152]{0:T(1024)} %param.27) | copy-start | bytes 13828
  7.2 11.2 %copy-start.28 = (f32[1728]{0:T(1024)S(1)}, f32[1728]{0:T(1024)}, u32[]{:S(2)}) copy-start(f32[1728]{0:T(1024)} %param.21) | copy-start | bytes 20740
  7.2 184.2 %all-gather.11.cloned.1.call-start = ((), (), s32[]{:S(2)}) async-start(), calls=%async_computation.4 | async-start | bytes 3317760 | tf_op jit(solution)/shard_map/all_gather | solution.py:598
  13.1 125.7 %collective-permute-start.5 = (bf16[288,1152]{1,0:T(8,128)(2,1)}, bf16[288,1152]{1,0:T(8,128)(2,1)}, u32[]{:S(2)}, u32[]{:S(2)}) collective-permute-start(bf16[288,1152]{1,0:T(8,128)(2,1)} %pad_maximum_fusion.18), channel_id=1, source_target_pairs={{0,1},{1,2},{2,3},{3,0},{4,5},{5,6},{6,7},{7,4},{8,9},{9,10},{10,1... | collective-permute-start | bytes 1990664 | tf_op jit(solution)/shard_map/ppermute | solution.py:540
  14.6 128.1 %collective-permute-start.6 = (bf16[288,1152]{1,0:T(8,128)(2,1)}, bf16[288,1152]{1,0:T(8,128)(2,1)}, u32[]{:S(2)}, u32[]{:S(2)}) collective-permute-start(bf16[288,1152]{1,0:T(8,128)(2,1)} %pad_maximum_fusion.18), channel_id=1, source_target_pairs={{0,2},{1,3},{2,0},{3,1},{4,6},{5,7},{6,4},{7,5},{8,10},{9,11},{10,... | collective-permute-start | bytes 1990664 | tf_op jit(solution)/shard_map/ppermute | solution.py:540
  15.9 128.0 %collective-permute-start.7 = (bf16[288,1152]{1,0:T(8,128)(2,1)}, bf16[288,1152]{1,0:T(8,128)(2,1)}, u32[]{:S(2)}, u32[]{:S(2)}) collective-permute-start(bf16[288,1152]{1,0:T(8,128)(2,1)} %pad_maximum_fusion.18), channel_id=1, source_target_pairs={{0,3},{1,0},{2,1},{3,2},{4,7},{5,4},{6,5},{7,6},{8,11},{9,8},{10,9... | collective-permute-start | bytes 1990664 | tf_op jit(solution)/shard_map/ppermute | solution.py:540
  113.5 47.9 %collective-permute-start.2 = (bf16[2,256,288]{2,1,0:T(8,128)(2,1)}, bf16[2,256,288]{2,1,0:T(8,128)(2,1)S(1)}, u32[]{:S(2)}, u32[]{:S(2)}) collective-permute-start(bf16[2,256,288]{2,1,0:T(8,128)(2,1)} %get-tuple-element.63), channel_id=1, source_target_pairs={{0,3},{1,0},{2,1},{3,2},{4,7},{5,4},{6,5},{7,6},{8,11},{9,8},{10,9... | collective-permute-start | bytes 884744 | tf_op jit(solution)/shard_map/ppermute | solution.py:540
  114.7 10.4 %copy-start.30 = (f32[1152]{0:T(1024)S(1)}, f32[1152]{0:T(1024)}, u32[]{:S(2)}) copy-start(f32[1152]{0:T(1024)} %param.25) | copy-start | bytes 13828
  121.6 39.9 %collective-permute-start.1 = (bf16[2,256,288]{2,1,0:T(8,128)(2,1)}, bf16[2,256,288]{2,1,0:T(8,128)(2,1)}, u32[]{:S(2)}, u32[]{:S(2)}) collective-permute-start(bf16[2,256,288]{2,1,0:T(8,128)(2,1)} %get-tuple-element.62), channel_id=1, source_target_pairs={{0,2},{1,3},{2,0},{3,1},{4,6},{5,7},{6,4},{7,5},{8,10},{9,11},{10,... | collective-permute-start | bytes 884744 | tf_op jit(solution)/shard_map/ppermute | solution.py:540
  123.0 602.7 %reduce-scatter.3.cloned.1.call-start = ((), (), s32[]{:S(2)}) async-start(), calls=%async_computation.2 | async-start | bytes 2949120 | tf_op jit(solution)/shard_map/reduce_scatter | solution.py:685
  138.8 43.3 %collective-permute-start = (bf16[2,256,288]{2,1,0:T(8,128)(2,1)}, bf16[2,256,288]{2,1,0:T(8,128)(2,1)}, u32[]{:S(2)}, u32[]{:S(2)}) collective-permute-start(bf16[2,256,288]{2,1,0:T(8,128)(2,1)} %get-tuple-element.61), channel_id=1, source_target_pairs={{0,1},{1,2},{2,3},{3,0},{4,5},{5,6},{6,7},{7,4},{8,9},{9,10},{10,1... | collective-permute-start | bytes 884744 | tf_op jit(solution)/shard_map/ppermute | solution.py:540
  145.1 7.1 copy-start.11
  146.2 52.8 %collective-permute-start.10 = (bf16[3,144,1152]{2,1,0:T(8,128)(2,1)}, bf16[3,144,1152]{2,1,0:T(8,128)(2,1)}, u32[]{:S(2)}, u32[]{:S(2)}) collective-permute-start(bf16[3,144,1152]{2,1,0:T(8,128)(2,1)} %get-tuple-element.218.refs_7_), channel_id=1, source_target_pairs={{0,16},{4,20},{8,24},{12,28},{16,0},{20,4},{24,8},{28,12},{1,17},{... | collective-permute-start | bytes 2985992 | tf_op jit(solution)/shard_map/ppermute | solution.py:544
  151.5 50.9 %collective-permute-start.8 = (bf16[3,144,1152]{2,1,0:T(8,128)(2,1)}, bf16[3,144,1152]{2,1,0:T(8,128)(2,1)}, u32[]{:S(2)}, u32[]{:S(2)}) collective-permute-start(bf16[3,144,1152]{2,1,0:T(8,128)(2,1)} %get-tuple-element.220.refs_4_), channel_id=1, source_target_pairs={{0,8},{4,12},{8,0},{12,4},{16,24},{20,28},{24,16},{28,20},{1,9},{5... | collective-permute-start | bytes 2985992 | tf_op jit(solution)/shard_map/ppermute | solution.py:544
  161.4 30.1 %copy-start.19 = (bf16[2,256,288]{2,1,0:T(8,128)(2,1)}, bf16[2,256,288]{2,1,0:T(8,128)(2,1)S(1)}, u32[]{:S(2)}) copy-start(bf16[2,256,288]{2,1,0:T(8,128)(2,1)S(1)} %collective-permute-done.2.a3) | copy-start | bytes 884740
  161.4 48.4 %collective-permute-start.4 = (bf16[512,1152]{1,0:T(8,128)(2,1)}, bf16[512,1152]{1,0:T(8,128)(2,1)}, u32[]{:S(2)}, u32[]{:S(2)}) collective-permute-start(bf16[512,1152]{1,0:T(8,128)(2,1)} %bitcast.10.refs_2_), channel_id=1, source_target_pairs={{0,4},{4,0},{8,12},{12,8},{16,20},{20,16},{24,28},{28,24},{1,5},{5... | collective-permute-start | bytes 3538952 | tf_op jit(solution)/shard_map/ppermute | solution.py:544
  198.9 11.0 %collective-permute-start.3 = (bf16[512,1152]{1,0:T(8,128)(2,1)}, bf16[512,1152]{1,0:T(8,128)(2,1)}, u32[]{:S(2)}, u32[]{:S(2)}) collective-permute-start(bf16[512,1152]{1,0:T(8,128)(2,1)} %bitcast.219), channel_id=1, source_target_pairs={{0,4},{4,0},{8,12},{12,8},{16,20},{20,16},{24,28},{28,24},{1,5},{5... | collective-permute-start | bytes 3538952 | tf_op jit(solution)/shard_map/ppermute | solution.py:544
  201.8 45.9 %collective-permute-start.11 = (bf16[2,3,144,1152]{3,2,1,0:T(8,128)(2,1)}, bf16[2,3,144,1152]{3,2,1,0:T(8,128)(2,1)}, u32[]{:S(2)}, u32[]{:S(2)}) collective-permute-start(bf16[2,3,144,1152]{3,2,1,0:T(8,128)(2,1)} %pad_maximum_fusion.7), channel_id=1, source_target_pairs={{0,8},{4,12},{8,0},{12,4},{16,24},{20,28},{24,16},{28,20},{1,9},{5... | collective-permute-start | bytes 5971976 | tf_op jit(solution)/shard_map/ppermute | solution.py:544
  205.1 45.6 %collective-permute-start.9 = (bf16[2,3,144,1152]{3,2,1,0:T(8,128)(2,1)}, bf16[2,3,144,1152]{3,2,1,0:T(8,128)(2,1)}, u32[]{:S(2)}, u32[]{:S(2)}) collective-permute-start(bf16[2,3,144,1152]{3,2,1,0:T(8,128)(2,1)} %pad_maximum_fusion.6), channel_id=1, source_target_pairs={{0,16},{4,20},{8,24},{12,28},{16,0},{20,4},{24,8},{28,12},{1,17},{... | collective-permute-start | bytes 5971976 | tf_op jit(solution)/shard_map/ppermute | solution.py:544
  297.6 11.7 %slice-start.4 = ((s8[4718592]{0:T(1024)(128)(4,1)}), s8[524288]{0:T(1024)(128)(4,1)S(1)}, s32[]{:S(2)}) async-start(s8[4718592]{0:T(1024)(128)(4,1)} %bitcast.192), calls=%async_computation.11 | async-start | bytes 1048576
  301.1 59.0 %collective-permute-start.30 = (bf16[4,2,144,1152]{3,2,1,0:T(8,128)(2,1)}, bf16[4,2,144,1152]{3,2,1,0:T(8,128)(2,1)}, u32[]{:S(2)}, u32[]{:S(2)}) collective-permute-start(bf16[4,2,144,1152]{3,2,1,0:T(8,128)(2,1)} %fusion.4), channel_id=1, source_target_pairs={{0,8},{4,12},{8,0},{12,4},{16,24},{20,28},{24,16},{28,20},{1,9},{5... | collective-permute-start | bytes 7962632 | tf_op jit(solution)/shard_map/ppermute | solution.py:544
  307.9 60.6 %collective-permute-start.28 = (bf16[4,2,144,1152]{3,2,0,1:T(8,128)(2,1)S(1)}, bf16[4,2,144,1152]{3,2,0,1:T(8,128)(2,1)S(1)}, u32[]{:S(2)}, u32[]{:S(2)}) collective-permute-start(bf16[4,2,144,1152]{3,2,0,1:T(8,128)(2,1)S(1)} %pad_maximum_fusion.2), channel_id=1, source_target_pairs={{0,16},{4,20},{8,24},{12,28},{16,0},{20,4},{24,8},{28,12},{1,17},{... | collective-permute-start | bytes 7962632 | tf_op jit(solution)/shard_map/ppermute | solution.py:544
  312.8 47.3 %copy-start.3 = (bf16[3,576,1152]{2,1,0:T(8,128)(2,1)S(1)}, bf16[3,576,1152]{2,1,0:T(8,128)(2,1)}, u32[]{:S(2)}) copy-start(bf16[3,576,1152]{2,1,0:T(8,128)(2,1)} %get-tuple-element.99) | copy-start | bytes 11943940
  315.5 89.1 %collective-permute-start.12 = (f32[2,512,1152]{2,1,0:T(8,128)}, f32[2,512,1152]{2,1,0:T(8,128)}, u32[]{:S(2)}, u32[]{:S(2)}) collective-permute-start(f32[2,512,1152]{2,1,0:T(8,128)} %pad_maximum_fusion), channel_id=1, source_target_pairs={{0,4},{4,0},{8,12},{12,8},{16,20},{20,16},{24,28},{28,24},{1,5},{5... | collective-permute-start | bytes 14155784 | tf_op jit(solution)/shard_map/ppermute | solution.py:544
  360.1 8.4 copy-start.2
  362.4 7.1 copy-start.7
  362.5 32.4 %collective-permute-start.31 = (bf16[4,144,1152]{2,1,0:T(8,128)(2,1)S(1)}, bf16[4,144,1152]{2,1,0:T(8,128)(2,1)}, u32[]{:S(2)}, u32[]{:S(2)}) collective-permute-start(bf16[4,144,1152]{2,1,0:T(8,128)(2,1)S(1)} %slice_bitcast_fusion.6), channel_id=1, source_target_pairs={{0,16},{4,20},{8,24},{12,28},{16,0},{20,4},{24,8},{28,12},{1,17},{... | collective-permute-start | bytes 3981320 | tf_op jit(solution)/shard_map/ppermute | solution.py:544
  371.0 27.1 %collective-permute-start.29 = (bf16[4,144,1152]{2,1,0:T(8,128)(2,1)S(1)}, bf16[4,144,1152]{2,1,0:T(8,128)(2,1)}, u32[]{:S(2)}, u32[]{:S(2)}) collective-permute-start(bf16[4,144,1152]{2,1,0:T(8,128)(2,1)S(1)} %slice_bitcast_fusion.8), channel_id=1, source_target_pairs={{0,8},{4,12},{8,0},{12,4},{16,24},{20,28},{24,16},{28,20},{1,9},{5... | collective-permute-start | bytes 3981320 | tf_op jit(solution)/shard_map/ppermute | solution.py:544
  372.0 26.0 %copy-start.9 = (bf16[4,2,144,1152]{3,2,0,1:T(8,128)(2,1)S(1)}, bf16[4,2,144,1152]{3,2,0,1:T(8,128)(2,1)}, u32[]{:S(2)}) copy-start(bf16[4,2,144,1152]{3,2,0,1:T(8,128)(2,1)} %copy-done.8) | copy-start | bytes 7962628
  401.0 177.5 %collective-permute-start.32 = (bf16[2,144,1152]{2,1,0:T(8,128)(2,1)}, bf16[2,144,1152]{2,1,0:T(8,128)(2,1)}, u32[]{:S(2)}, u32[]{:S(2)}) collective-permute-start(bf16[2,144,1152]{2,1,0:T(8,128)(2,1)} %get-tuple-element.207), channel_id=1, source_target_pairs={{0,3},{1,0},{2,1},{3,2},{4,7},{5,4},{6,5},{7,6},{8,11},{9,8},{10,9... | collective-permute-start | bytes 1990664 | tf_op jit(solution)/shard_map/ppermute | solution.py:540
  403.1 175.4 %collective-permute-start.33 = (bf16[2,144,1152]{2,1,0:T(8,128)(2,1)}, bf16[2,144,1152]{2,1,0:T(8,128)(2,1)}, u32[]{:S(2)}, u32[]{:S(2)}) collective-permute-start(bf16[2,144,1152]{2,1,0:T(8,128)(2,1)} %get-tuple-element.209), channel_id=1, source_target_pairs={{0,2},{1,3},{2,0},{3,1},{4,6},{5,7},{6,4},{7,5},{8,10},{9,11},{10,... | collective-permute-start | bytes 1990664 | tf_op jit(solution)/shard_map/ppermute | solution.py:540
  426.1 46.7 %collective-permute-start.13 = (bf16[2,256,288]{2,1,0:T(8,128)(2,1)}, bf16[2,256,288]{2,1,0:T(8,128)(2,1)S(1)}, u32[]{:S(2)}, u32[]{:S(2)}) collective-permute-start(bf16[2,256,288]{2,1,0:T(8,128)(2,1)} %get-tuple-element.77), channel_id=1, source_target_pairs={{0,3},{1,0},{2,1},{3,2},{4,7},{5,4},{6,5},{7,6},{8,11},{9,8},{10,9... | collective-permute-start | bytes 884744 | tf_op jit(solution)/shard_map/ppermute | solution.py:540
  427.6 71.9 %collective-permute-start.14 = (bf16[2,256,288]{2,1,0:T(8,128)(2,1)}, bf16[2,256,288]{2,1,0:T(8,128)(2,1)S(1)}, u32[]{:S(2)}, u32[]{:S(2)}) collective-permute-start(bf16[2,256,288]{2,1,0:T(8,128)(2,1)} %get-tuple-element.78), channel_id=1, source_target_pairs={{0,2},{1,3},{2,0},{3,1},{4,6},{5,7},{6,4},{7,5},{8,10},{9,11},{10,... | collective-permute-start | bytes 884744 | tf_op jit(solution)/shard_map/ppermute | solution.py:540
  430.6 77.4 %collective-permute-start.15 = (bf16[2,256,288]{2,1,0:T(8,128)(2,1)}, bf16[2,256,288]{2,1,0:T(8,128)(2,1)S(1)}, u32[]{:S(2)}, u32[]{:S(2)}) collective-permute-start(bf16[2,256,288]{2,1,0:T(8,128)(2,1)} %get-tuple-element.79), channel_id=1, source_target_pairs={{0,1},{1,2},{2,3},{3,0},{4,5},{5,6},{6,7},{7,4},{8,9},{9,10},{10,1... | collective-permute-start | bytes 884744 | tf_op jit(solution)/shard_map/ppermute | solution.py:540
  472.8 37.5 %copy-start.35 = (bf16[2,256,288]{2,1,0:T(8,128)(2,1)}, bf16[2,256,288]{2,1,0:T(8,128)(2,1)S(1)}, u32[]{:S(2)}) copy-start(bf16[2,256,288]{2,1,0:T(8,128)(2,1)S(1)} %collective-permute-done.13.g1) | copy-start | bytes 884740
  472.8 96.8 %collective-permute-start.19 = (bf16[288,1152]{1,0:T(8,128)(2,1)}, bf16[288,1152]{1,0:T(8,128)(2,1)}, u32[]{:S(2)}, u32[]{:S(2)}) collective-permute-start(bf16[288,1152]{1,0:T(8,128)(2,1)} %get-tuple-element.212), channel_id=1, source_target_pairs={{0,3},{1,0},{2,1},{3,2},{4,7},{5,4},{6,5},{7,6},{8,11},{9,8},{10,9... | collective-permute-start | bytes 1990664 | tf_op jit(solution)/shard_map/ppermute | solution.py:540
  499.5 10.8 %copy-start.36 = (bf16[2,256,288]{2,1,0:T(8,128)(2,1)}, bf16[2,256,288]{2,1,0:T(8,128)(2,1)S(1)}, u32[]{:S(2)}) copy-start(bf16[2,256,288]{2,1,0:T(8,128)(2,1)S(1)} %collective-permute-done.14.g2) | copy-start | bytes 884740
  499.5 70.9 %collective-permute-start.20 = (bf16[288,1152]{1,0:T(8,128)(2,1)}, bf16[288,1152]{1,0:T(8,128)(2,1)}, u32[]{:S(2)}, u32[]{:S(2)}) collective-permute-start(bf16[288,1152]{1,0:T(8,128)(2,1)} %get-tuple-element.214), channel_id=1, source_target_pairs={{0,2},{1,3},{2,0},{3,1},{4,6},{5,7},{6,4},{7,5},{8,10},{9,11},{10,... | collective-permute-start | bytes 1990664 | tf_op jit(solution)/shard_map/ppermute | solution.py:540
  507.9 62.4 %collective-permute-start.21 = (bf16[288,1152]{1,0:T(8,128)(2,1)}, bf16[288,1152]{1,0:T(8,128)(2,1)}, u32[]{:S(2)}, u32[]{:S(2)}) collective-permute-start(bf16[288,1152]{1,0:T(8,128)(2,1)} %get-tuple-element.213), channel_id=1, source_target_pairs={{0,1},{1,2},{2,3},{3,0},{4,5},{5,6},{6,7},{7,4},{8,9},{9,10},{10,1... | collective-permute-start | bytes 1990664 | tf_op jit(solution)/shard_map/ppermute | solution.py:540
  528.7 197.0 %reduce-scatter.5.cloned.1.call-start = ((), (), s32[]{:S(2)}) async-start(), calls=%async_computation.3 | async-start | bytes 2949120 | tf_op jit(solution)/shard_map/reduce_scatter | solution.py:685
  528.7 27.9 %copy-start.23 = (bf16[1024,288]{1,0:T(8,128)(2,1)S(1)}, bf16[1024,288]{1,0:T(8,128)(2,1)}, u32[]{:S(2)}) copy-start(bf16[1024,288]{1,0:T(8,128)(2,1)} %get-tuple-element.85) | copy-start | bytes 1769476
  569.6 27.5 %collective-permute-start.34 = (bf16[2,144,1152]{2,1,0:T(8,128)(2,1)S(1)}, bf16[2,144,1152]{2,1,0:T(8,128)(2,1)S(1)}, u32[]{:S(2)}, u32[]{:S(2)}) collective-permute-start(bf16[2,144,1152]{2,1,0:T(8,128)(2,1)S(1)} %get-tuple-element.208), channel_id=1, source_target_pairs={{0,1},{1,2},{2,3},{3,0},{4,5},{5,6},{6,7},{7,4},{8,9},{9,10},{10,1... | collective-permute-start | bytes 1990664 | tf_op jit(solution)/shard_map/ppermute | solution.py:540
  577.2 21.5 %copy-start.5 = (bf16[1152,1152]{1,0:T(8,128)(2,1)}, bf16[1152,1152]{1,0:T(8,128)(2,1)S(1)}, u32[]{:S(2)}) copy-start(bf16[1152,1152]{1,0:T(8,128)(2,1)S(1)} %pad_maximum_fusion.3) | copy-start | bytes 7962628
  578.5 38.5 %collective-permute-start.22 = (bf16[576,1152]{1,0:T(8,128)(2,1)}, bf16[576,1152]{1,0:T(8,128)(2,1)}, u32[]{:S(2)}, u32[]{:S(2)}) collective-permute-start(bf16[576,1152]{1,0:T(8,128)(2,1)} %constant_dynamic-slice_fusion.2), channel_id=1, source_target_pairs={{0,4},{4,0},{8,12},{12,8},{16,20},{20,16},{24,28},{28,24},{1,5},{5... | collective-permute-start | bytes 3981320 | tf_op jit(solution)/shard_map/ppermute | solution.py:544
  598.7 15.9 %collective-permute-start.35 = (bf16[2,144,1152]{2,1,0:T(8,128)(2,1)S(1)}, bf16[2,144,1152]{2,1,0:T(8,128)(2,1)S(1)}, u32[]{:S(2)}, u32[]{:S(2)}) collective-permute-start(bf16[2,144,1152]{2,1,0:T(8,128)(2,1)S(1)} %fusion.17), channel_id=1, source_target_pairs={{0,8},{4,12},{8,0},{12,4},{16,24},{20,28},{24,16},{28,20},{1,9},{5... | collective-permute-start | bytes 1990664 | tf_op jit(solution)/shard_map/ppermute | solution.py:544
  616.6 43.4 %collective-permute-start.36 = (bf16[2,2,144,1152]{3,2,0,1:T(8,128)(2,1)}, bf16[2,2,144,1152]{3,2,0,1:T(8,128)(2,1)}, u32[]{:S(2)}, u32[]{:S(2)}) collective-permute-start(bf16[2,2,144,1152]{3,2,0,1:T(8,128)(2,1)} %pad_maximum_fusion.11), channel_id=1, source_target_pairs={{0,16},{4,20},{8,24},{12,28},{16,0},{20,4},{24,8},{28,12},{1,17},{... | collective-permute-start | bytes 3981320 | tf_op jit(solution)/shard_map/ppermute | solution.py:544
  616.9 42.2 %copy-start.32 = (f32[3,1,576]{2,1,0:T(1,128)S(1)}, f32[3,1,576]{2,1,0:T(1,128)}, u32[]{:S(2)}) copy-start(f32[3,1,576]{2,1,0:T(1,128)} %get-tuple-element.91) | copy-start | bytes 20740
  617.0 135.2 %all-gather.13.cloned.1.call-start = ((), (), s32[]{:S(2)}) async-start(), calls=%async_computation.6 | async-start | bytes 2737152 | tf_op jit(solution)/shard_map/all_gather | solution.py:756
  621.2 45.0 %collective-permute-start.23 = (bf16[288,1152]{1,0:T(8,128)(2,1)}, bf16[288,1152]{1,0:T(8,128)(2,1)}, u32[]{:S(2)}, u32[]{:S(2)}) collective-permute-start(bf16[288,1152]{1,0:T(8,128)(2,1)} %constant_dynamic-slice_fusion.1), channel_id=1, source_target_pairs={{0,8},{4,12},{8,0},{12,4},{16,24},{20,28},{24,16},{28,20},{1,9},{5... | collective-permute-start | bytes 1990664 | tf_op jit(solution)/shard_map/ppermute | solution.py:544
  667.6 10.6 %copy-start.33 = (f32[1,1,576]{2,1,0:T(1,128)S(1)}, f32[1,1,576]{2,1,0:T(1,128)}, u32[]{:S(2)}) copy-start(f32[1,1,576]{2,1,0:T(1,128)} %get-tuple-element.90) | copy-start | bytes 6916
  667.6 10.1 %collective-permute-start.24 = (bf16[144,1152]{1,0:T(8,128)(2,1)S(1)}, bf16[144,1152]{1,0:T(8,128)(2,1)S(1)}, u32[]{:S(2)}, u32[]{:S(2)}) collective-permute-start(bf16[144,1152]{1,0:T(8,128)(2,1)S(1)} %constant_dynamic-slice_fusion), channel_id=1, source_target_pairs={{0,16},{4,20},{8,24},{12,28},{16,0},{20,4},{24,8},{28,12},{1,17},{... | collective-permute-start | bytes 995336 | tf_op jit(solution)/shard_map/ppermute | solution.py:544
  670.1 37.4 %collective-permute-start.37 = (bf16[2,576,1152]{2,1,0:T(8,128)(2,1)}, bf16[2,576,1152]{2,1,0:T(8,128)(2,1)}, u32[]{:S(2)}, u32[]{:S(2)}) collective-permute-start(bf16[2,576,1152]{2,1,0:T(8,128)(2,1)} %bitcast_select_fusion), channel_id=1, source_target_pairs={{0,4},{4,0},{8,12},{12,8},{16,20},{20,16},{24,28},{28,24},{1,5},{5... | collective-permute-start | bytes 7962632 | tf_op jit(solution)/shard_map/ppermute | solution.py:544
  677.9 9.4 %collective-permute-start.25 = (bf16[144,1152]{1,0:T(8,128)(2,1)S(1)}, bf16[144,1152]{1,0:T(8,128)(2,1)}, u32[]{:S(2)}, u32[]{:S(2)}) collective-permute-start(bf16[144,1152]{1,0:T(8,128)(2,1)S(1)} %add_convert_fusion.3), channel_id=1, source_target_pairs={{0,16},{4,20},{8,24},{12,28},{16,0},{20,4},{24,8},{28,12},{1,17},{... | collective-permute-start | bytes 995336 | tf_op jit(solution)/shard_map/ppermute | solution.py:544
  689.2 15.6 %collective-permute-start.26 = (bf16[288,1152]{1,0:T(8,128)(2,1)S(1)}, bf16[288,1152]{1,0:T(8,128)(2,1)}, u32[]{:S(2)}, u32[]{:S(2)}) collective-permute-start(bf16[288,1152]{1,0:T(8,128)(2,1)S(1)} %pad_maximum_fusion.19), channel_id=1, source_target_pairs={{0,8},{4,12},{8,0},{12,4},{16,24},{20,28},{24,16},{28,20},{1,9},{5... | collective-permute-start | bytes 1990664 | tf_op jit(solution)/shard_map/ppermute | solution.py:544
  692.5 193.7 %all-reduce.4.cloned.1.call-start = ((), (), s32[]{:S(2)}) async-start(), calls=%async_computation.5 | async-start | bytes 1327104
  707.5 66.5 %collective-permute-start.27 = (bf16[576,1152]{1,0:T(8,128)(2,1)}, bf16[576,1152]{1,0:T(8,128)(2,1)}, u32[]{:S(2)}, u32[]{:S(2)}) collective-permute-start(bf16[576,1152]{1,0:T(8,128)(2,1)} %pad_maximum_fusion.10), channel_id=1, source_target_pairs={{0,4},{4,0},{8,12},{12,8},{16,20},{20,16},{24,28},{28,24},{1,5},{5... | collective-permute-start | bytes 3981320 | tf_op jit(solution)/shard_map/ppermute | solution.py:544
  764.1 5.1 slice-start.1
  898.8 9.6 %copy-start.26 = (bf16[2,4,1152]{2,1,0:T(4,128)(2,1)S(1)}, bf16[2,4,1152]{2,1,0:T(4,128)(2,1)}, u32[]{:S(2)}) copy-start(bf16[2,4,1152]{2,1,0:T(4,128)(2,1)} %param.17) | copy-start | bytes 55300
  898.8 8.8 collective-permute-start.16
  899.5 8.2 collective-permute-start.17
  900.4 7.2 collective-permute-start.18
  902.4 6.8 copy-start.1
  (25 other events, 63.4 us)
Sparse Core Ops, SparseCore 0:
  123.1 68.2 all-gather.10
  528.8 67.9 reduce-scatter.2
  617.1 48.5 reduce-scatter.4
  692.7 59.4 all-gather.12
  757.2 129.0 all-reduce.3

commit v2 on v1

v2 whole, which is shorter than its diff:
```python
import functools
import math

import jax
import jax.numpy as jnp
from jax import lax
from jax.experimental import pallas as pl
from jax.experimental.pallas import tpu as pltpu
from jax.sharding import Mesh
from jax.sharding import PartitionSpec as P

HEAD_DIM = 72
EPSILON = 1e-06
LOG2E = math.log2(math.e)
GELU_C = 0.7978845608
GELU_A = 0.044715
VMEM = 60 * 1024 * 1024
BF = jnp.bfloat16
F32 = jnp.float32


def nn(a, b):
    return lax.dot_general(a, b, (((1,), (0,)), ((), ())), preferred_element_type=F32)


def nt(a, b):
    return lax.dot_general(a, b, (((1,), (1,)), ((), ())), preferred_element_type=F32)


def tn(a, b):
    return lax.dot_general(a, b, (((0,), (0,)), ((), ())), preferred_element_type=F32)


def params():
    return pltpu.CompilerParams(vmem_limit_bytes=VMEM)


def cost(micros):
    return pl.CostEstimate(
        flops=int(micros * 1.15e9), bytes_accessed=int(micros * 1e5), transcendentals=0
    )


ANY = pl.BlockSpec(memory_space=pl.ANY)


def shape(dims, dtype):
    return pltpu.HBM(tuple(dims), dtype)


def skipping(kernel, start, count):
    def body(*refs):
        kernel(*refs[:start], *refs[start + count :])

    return body


def simple(kernel, outs, operands, scalars=None, after=(), scratch=(), name="glue", micros=3):
    count = len(after)
    n_scalar = 0 if scalars is None else 1
    n_in = len(operands)

    body = skipping(kernel, n_scalar + n_in, count)

    def whole(array):
        zeros = (0,) * len(array.shape)
        return pl.BlockSpec(array.shape, lambda *_: zeros)

    return pl.pallas_call(
        body,
        grid_spec=pltpu.PrefetchScalarGridSpec(
            num_scalar_prefetch=n_scalar,
            grid=(1,),
            in_specs=[whole(a) for a in operands] + [ANY] * count,
            out_specs=[whole(o) for o in outs],
            scratch_shapes=list(scratch),
        ),
        out_shape=list(outs),
        compiler_params=params(),
        cost_estimate=cost(micros),
        name=name,
    )(*([] if scalars is None else [scalars]), *operands, *after)


def normalize(values):
    centred = values - jnp.mean(values, axis=-1, keepdims=True)
    inverse = lax.rsqrt(jnp.mean(centred * centred, axis=-1, keepdims=True) + EPSILON)
    return centred * inverse, inverse


def norm_backward(grad, normed, inverse):
    return inverse * (
        grad
        - jnp.mean(grad, axis=-1, keepdims=True)
        - normed * jnp.mean(grad * normed, axis=-1, keepdims=True)
    )


def project_kernel(tok_ref, mod_ref, w_ref, bias_ref, hid_ref, q_ref, k_ref, v_ref):
    heads = q_ref.shape[1]
    size = q_ref.shape[3]
    share = tok_ref.shape[1] // mod_ref.shape[0]
    for i in range(mod_ref.shape[0]):
        rows = slice(i * share, (i + 1) * share)
        normed, _ = normalize(tok_ref[0, rows].astype(F32))
        hid_ref[0, rows] = (normed * (1.0 + mod_ref[i, 1:2, :]) + mod_ref[i, 0:1, :]).astype(BF)
    proj = (nt(hid_ref[0], w_ref[...]) + bias_ref[...]).astype(BF)
    for which, out in enumerate((q_ref, k_ref, v_ref)):
        for h in range(heads):
            at = (which * heads + h) * size
            out[0, h] = proj[:, at : at + size]


def project(tokens, mod_blocks, qkv_weight, qv_bias, blocks):
    micro, rows, width = tokens.shape
    share = rows // blocks
    local = qkv_weight.shape[1]
    heads = local // HEAD_DIM
    weight = qkv_weight.reshape(3 * local, width)
    bias = jnp.concatenate([qv_bias[0], jnp.zeros_like(qv_bias[0]), qv_bias[1]])[None]
    head_shape = shape((micro, heads, rows, HEAD_DIM), BF)
    head_spec = pl.BlockSpec((1, heads, 2 * share, HEAD_DIM), lambda m, b: (m, 0, b, 0))
    return pl.pallas_call(
        project_kernel,
        grid=(micro, blocks // 2),
        in_specs=[
            pl.BlockSpec((1, 2 * share, width), lambda m, b: (m, b, 0)),
            pl.BlockSpec((2, 6, width), lambda m, b: (m * (blocks // 2) + b, 0, 0)),
            pl.BlockSpec(weight.shape, lambda m, b: (0, 0)),
            pl.BlockSpec(bias.shape, lambda m, b: (0, 0)),
        ],
        out_specs=[
            pl.BlockSpec((1, 2 * share, width), lambda m, b: (m, b, 0)),
            head_spec,
            head_spec,
            head_spec,
        ],
        out_shape=[shape(tokens.shape, BF), head_shape, head_shape, head_shape],
        compiler_params=params(),
        cost_estimate=cost(0.01),
        name="project",
    )(tokens, mod_blocks, weight, bias)


def attend_kernel(info_ref, q_ref, k_ref, v_ref, a0, a1, a2, a3, lse_ref):
    _, heads, rows, size = q_ref.shape
    share = rows // 4
    rank = info_ref[0]
    whole = info_ref[1 + pl.program_id(0)]
    factor = size ** (-0.5) * LOG2E
    lane = lax.broadcasted_iota(jnp.int32, (share, 128), 1)

    def run(full):
        for shift, att_ref in enumerate((a0, a1, a2, a3)):
            block = pl.ds(pl.multiple_of(lax.rem(rank + shift, 4) * share, share), share)
            span = slice(None) if full else block
            logs = jnp.zeros((share, 128), F32)
            outs = []
            for h in range(heads):
                scores = nt(q_ref[0, h, block, :], k_ref[0, h, span, :])
                top = jnp.max(scores, axis=-1, keepdims=True)
                weight = jnp.exp2((scores - top) * factor)
                total = jnp.sum(weight, axis=-1, keepdims=True)
                out = nn(weight.astype(BF), v_ref[0, h, span, :])
                outs.append((out * (1.0 / total)).astype(BF))
                logs = jnp.where(lane == h, top * factor + jnp.log2(total), logs)
            att_ref[0] = pack_rows(jnp.concatenate(outs, axis=1))
            lse_ref[0, :, block] = logs.T[0:heads, :]

    @pl.when(whole == 1)
    def _():
        run(True)

    @pl.when(whole == 0)
    def _():
        run(False)


def attend(info, query, key, value, after=()):
    micro, heads, rows, size = query.shape
    share = rows // 4
    full = pl.BlockSpec((1, heads, rows, size), lambda m, s: (m, 0, 0, 0))
    packed = (share // 4, 4 * heads * size)
    part = pl.BlockSpec((1, *packed), lambda m, s: (m, 0, 0))
    return pl.pallas_call(
        skipping(attend_kernel, 4, len(after)),
        grid_spec=pltpu.PrefetchScalarGridSpec(
            num_scalar_prefetch=1,
            grid=(micro,),
            in_specs=[full] * 3 + [ANY] * len(after),
            out_specs=[part] * 4 + [pl.BlockSpec((1, heads, rows), lambda m, s: (m, 0, 0))],
        ),
        out_shape=[shape((micro, *packed), BF)] * 4 + [shape((micro, heads, rows), F32)],
        compiler_params=params(),
        cost_estimate=cost(0.01),
        name="attend",
    )(info, query, key, value, *after)


def middle_kernel(info_ref, a0, a1, a2, a3, w_ref, bias_ref, tok_ref, mod_ref, attn_ref, mid_ref, hid_ref):
    rank = info_ref[0]
    total = bias_ref[0:1, :]
    for shift, part in enumerate((a0, a1, a2, a3)):
        total = total + nn(unpack_rows(part[0]), w_ref[lax.rem(rank + 4 - shift, 4)])
    attn_ref[0] = total
    mid = tok_ref[0].astype(F32) + mod_ref[0, 2:3, :] * total
    mid_ref[0] = mid
    normed, _ = normalize(mid)
    hid_ref[0] = (normed * (1.0 + mod_ref[0, 4:5, :]) + mod_ref[0, 3:4, :]).astype(BF)


def middle(info, parts, out_full, out_bias, tokens, mod_blocks, blocks, after=()):
    micro = parts[0].shape[0]
    share, width = tokens.shape[1] // blocks, tokens.shape[2]
    part = pl.BlockSpec((1, *parts[0].shape[1:]), lambda m, s: (m, 0, 0))
    row = pl.BlockSpec((1, share, width), lambda m, s: (m, 0, 0))
    return pl.pallas_call(
        skipping(middle_kernel, 9, len(after)),
        grid_spec=pltpu.PrefetchScalarGridSpec(
            num_scalar_prefetch=1,
            grid=(micro,),
            in_specs=[part] * 4
            + [
                pl.BlockSpec(out_full.shape, lambda m, s: (0, 0, 0)),
                pl.BlockSpec((1, width), lambda m, s: (0, 0)),
                pl.BlockSpec((1, share, width), lambda m, s: (m, s[0], 0)),
                pl.BlockSpec((1, 6, width), lambda m, s: (m * blocks + s[0], 0, 0)),
            ]
            + [ANY] * len(after),
            out_specs=[row, row, row],
        ),
        out_shape=[
            shape((micro, share, width), F32),
            shape((micro, share, width), F32),
            shape((micro, share, width), BF),
        ],
        compiler_params=params(),
        cost_estimate=cost(8),
        name="middle",
    )(info, *parts, out_full, out_bias, tokens, mod_blocks, *after)


def feed_kernel(first, kinds, *refs):
    xo, xt, go, gt = refs[:4]
    at = 4
    weights = []
    for kind in kinds:
        weights.append(refs[at : at + kind])
        at += kind
    bias_ref = refs[at]
    at += 1
    if not first:
        carry = refs[at : at + 4]
        at += 4
    mo, mt, ho, ht, wuk, wus, wdk, wds, bsum_ref = refs[at : at + 9]
    xs, gs, us, ds, acts, dps, wtmp = refs[at + 9 :]
    half = xo.shape[0]
    units = us.shape[0]
    piece = units // 4
    step = pl.program_id(0)
    chunk = 512

    @pl.when(step == 0)
    def _():
        xs[:half] = xo[...]
        xs[half:] = xt[...]
        gs[:half] = go[...]
        gs[half:] = gt[...]
        if first:
            for ref in (mo, mt, ho, ht):
                ref[...] = jnp.zeros_like(ref)
        else:
            for ref, old in zip((mo, mt, ho, ht), carry):
                ref[...] = old[...]

    index = 0
    for parts in weights:
        blocks = [parts]
        if len(parts[0].shape) == 3:
            blocks = [[ref.at[i] for ref in parts] for i in range(parts[0].shape[0])]
        for block in blocks:

            @pl.when(step == index)
            def _(block=block):
                if len(block) == 2:
                    us[...] = block[0][...]
                    ds[...] = block[1][...]
                    return
                for j, ref in enumerate(block):
                    us[j * piece : (j + 1) * piece] = ref[:piece]
                    ds[j * piece : (j + 1) * piece] = ref[piece:]

            index += 1

    bias = bias_ref[0]

    def rows_step(base, mlp_ref, gh_ref):
        def run(i, sums):
            rows = pl.ds(pl.multiple_of(base + i * chunk, chunk), chunk)
            out = pl.ds(pl.multiple_of(i * chunk, chunk), chunk)
            pre = nt(xs[rows, :], us[...]) + bias
            square = pre * pre
            tanh = jnp.tanh(GELU_C * pre * (1.0 + GELU_A * square))
            act = (0.5 * pre * (1.0 + tanh)).astype(BF)
            acts[rows, :] = act
            slope = 0.5 * (1.0 + tanh) + (0.5 * GELU_C) * pre * (1.0 - tanh * tanh) * (
                1.0 + 3.0 * GELU_A * square
            )
            dpre = nt(gs[rows, :], ds[...]) * slope
            low = dpre.astype(BF)
            dps[rows, :] = low
            mlp_ref[out, :] = mlp_ref[out, :] + nn(act, ds[...])
            gh_ref[out, :] = gh_ref[out, :] + nn(low, us[...])
            return sums + jnp.sum(dpre, axis=0, keepdims=True)

        return run

    sums = jnp.zeros((1, units), F32)
    sums = lax.fori_loop(0, half // chunk, rows_step(0, mo, ho), sums)
    sums = lax.fori_loop(0, half // chunk, rows_step(half, mt, ht), sums)
    bsum_ref[0] = sums
    for lhs, rhs, order in ((dps, xs, ((wuk, 0), (wuk, 1), (wus, 0), (wus, 1))),
                            (acts, gs, ((wdk, 0), (wds, 0), (wdk, 1), (wds, 1)))):
        for start in range(0, units, 256):
            stop = min(start + 256, units)
            wtmp[start:stop] = tn(lhs[:, start:stop], rhs[...]).astype(BF)
        for j, (ref, place) in enumerate(order):
            ref[0, place] = wtmp[j * piece : (j + 1) * piece]


def feed(own_x, other_x, own_g, other_g, weights, bias, carry):
    half, width = own_x.shape
    count, _, units = bias.shape
    piece = units // 4
    first = carry is None

    def whole(array):
        zeros = (0,) * len(array.shape)
        return pl.BlockSpec(array.shape, lambda k: zeros)

    operands = [own_x, other_x, own_g, other_g]
    for parts in weights:
        operands += list(parts)
    in_specs = [whole(a) for a in operands]
    in_specs.append(pl.BlockSpec((1, 1, units), lambda k: (k, 0, 0)))
    operands.append(bias)
    acc = pl.BlockSpec((half, width), lambda k: (0, 0))
    if not first:
        in_specs += [acc] * 4
        operands += list(carry)
    wspec = pl.BlockSpec((1, 2, piece, width), lambda k: (k, 0, 0, 0))
    return pl.pallas_call(
        functools.partial(feed_kernel, first, tuple(len(p) for p in weights)),
        grid=(count,),
        in_specs=in_specs,
        out_specs=[acc] * 4 + [wspec] * 4 + [pl.BlockSpec((1, 1, units), lambda k: (k, 0, 0))],
        out_shape=[shape((half, width), F32)] * 4
        + [shape((count, 2, piece, width), BF)] * 4
        + [shape((count, 1, units), F32)],
        scratch_shapes=[
            pltpu.VMEM((2 * half, width), BF),
            pltpu.VMEM((2 * half, width), BF),
            pltpu.VMEM((units, width), BF),
            pltpu.VMEM((units, width), BF),
            pltpu.VMEM((2 * half, units), BF),
            pltpu.VMEM((2 * half, units), BF),
            pltpu.VMEM((units, width), BF),
        ],
        compiler_params=params(),
        cost_estimate=cost(34),
        name="feed",
    )(*operands)


def between_kernel(
    info_ref, gho, ght, mlpo, mlpt, mid_ref, attn_ref, og_ref, mod_ref, dbias_ref, w_ref,
    a0, a1, a2, a3, layer_ref, gmid_ref, d0, d1, d2, d3, wkeep, wsend, sums_ref, wout_ref,
):
    rank = info_ref[0]
    micro = pl.program_id(0)
    valid = info_ref[1 + micro].astype(F32)
    mod = mod_ref[0]
    mid = mid_ref[0]
    attn = attn_ref[0]
    normed, inverse = normalize(mid)
    mlp_out = mlpo[...] + mlpt[...] + dbias_ref[0:1, :]
    layer_ref[0] = (valid * (mid + mod[5:6, :] * mlp_out)).astype(BF)
    grad_y = og_ref[0].astype(F32) * valid
    grad_hidden = gho[...] + ght[...]
    grad_mid = grad_y + norm_backward(grad_hidden * (1.0 + mod[4:5, :]), normed, inverse)
    gmid_ref[0] = grad_mid
    grad_attn = grad_mid * mod[2:3, :]
    sums_ref[0, 0:1, :] = jnp.sum(grad_mid * attn, axis=0, keepdims=True)
    sums_ref[0, 1:2, :] = jnp.sum(grad_hidden, axis=0, keepdims=True)
    sums_ref[0, 2:3, :] = jnp.sum(grad_hidden * normed, axis=0, keepdims=True)
    sums_ref[0, 3:4, :] = jnp.sum(grad_y * mlp_out, axis=0, keepdims=True)
    sums_ref[0, 4:5, :] = jnp.sum(grad_attn, axis=0, keepdims=True)
    sums_ref[0, 5:6, :] = jnp.sum(grad_y * mod[5:6, :], axis=0, keepdims=True)
    low = grad_attn.astype(BF)
    for shift, (out, part) in enumerate(((d0, a0), (d1, a1), (d2, a2), (d3, a3))):
        out[0] = pack_rows(nt(low, w_ref[lax.rem(rank + 4 - shift, 4)]).astype(BF))
        update = tn(unpack_rows(part[0]), low)
        half = update.shape[0] // 2

        @pl.when(micro == 0)
        def _(shift=shift, update=update):
            wout_ref[shift] = update

        @pl.when(micro > 0)
        def _(shift=shift, update=update):
            wout_ref[shift] = wout_ref[shift] + update

    @pl.when(micro == pl.num_programs(0) - 1)
    def _():
        core = info_ref[3]
        for shift in range(4):
            here = pl.ds(pl.multiple_of(core * half, half), half)
            there = pl.ds(pl.multiple_of((1 - core) * half, half), half)
            wkeep[shift] = wout_ref[shift, here, :].astype(BF)
            wsend[shift] = wout_ref[shift, there, :].astype(BF)


def between(info, feed_own, feed_other, mid, attn, out_grad, mod_blocks, down_bias, out_full, parts, blocks, after=()):
    micro, share, width = mid.shape
    local = parts[0].shape[2] // 4
    half = pl.BlockSpec((share, width), lambda m, s: (m, 0))
    row = pl.BlockSpec((1, share, width), lambda m, s: (m, 0, 0))
    part = pl.BlockSpec((1, *parts[0].shape[1:]), lambda m, s: (m, 0, 0))
    mlp_own, gh_own = feed_own
    mlp_other, gh_other = feed_other
    dshape = shape(parts[0].shape, BF)
    return pl.pallas_call(
        skipping(between_kernel, 15, len(after)),
        grid_spec=pltpu.PrefetchScalarGridSpec(
            num_scalar_prefetch=1,
            grid=(micro,),
            in_specs=[half] * 4
            + [
                row,
                row,
                pl.BlockSpec((1, share, width), lambda m, s: (m, s[0], 0)),
                pl.BlockSpec((1, 6, width), lambda m, s: (m * blocks + s[0], 0, 0)),
                pl.BlockSpec((1, width), lambda m, s: (0, 0)),
                pl.BlockSpec(out_full.shape, lambda m, s: (0, 0, 0)),
            ]
            + [part] * 4
            + [ANY] * len(after),
            out_specs=[row, row, part, part, part, part]
            + [
                pl.BlockSpec((blocks, local // 2, width), lambda m, s: (0, 0, 0)),
                pl.BlockSpec((blocks, local // 2, width), lambda m, s: (0, 0, 0)),
                pl.BlockSpec((1, 8, width), lambda m, s: (m, 0, 0)),
            ],
            scratch_shapes=[pltpu.VMEM((blocks, local, width), F32)],
        ),
        out_shape=[
            shape((micro, share, width), BF),
            shape((micro, share, width), F32),
            dshape,
            dshape,
            dshape,
            dshape,
            shape((blocks, local // 2, width), BF),
            shape((blocks, local // 2, width), BF),
            shape((micro, 8, width), F32),
        ],
        compiler_params=params(),
        cost_estimate=cost(18),
        name="between",
    )(info, gh_own, gh_other, mlp_own, mlp_other, mid, attn, out_grad, mod_blocks, down_bias, out_full, *parts, *after)


def attend_back_kernel(
    last, count, info_ref, q_ref, k_ref, v_ref, lse_ref, g0, g1, g2, g3, w_ref, hid_ref, tok_ref, *refs
):
    if last:
        old_ref, refs = refs[0], refs[1:]
    refs = refs[count:]
    part_ref, refs = refs[0], refs[1:]
    if last:
        sums_ref, bias_ref, wkeep, wsend = refs[:4]
        refs = refs[4:]
    else:
        sums_ref, bias_ref, wout = refs[:3]
        refs = refs[3:]
    dos, dqs, dks, dvs, dq_ref, dk_ref, dv_ref, wtmp = refs
    _, heads, rows, size = q_ref.shape
    share = rows // 4
    local = heads * size
    rank = info_ref[0]
    whole = info_ref[1]
    scale = size ** (-0.5)
    factor = scale * LOG2E
    for shift, grad in enumerate((g0, g1, g2, g3)):
        grad = unpack_rows(grad[0])
        for h in range(heads):
            dos[h, shift] = grad[:, h * size : (h + 1) * size]

    def block_of(shift):
        return pl.multiple_of(lax.rem(rank + shift, 4) * share, share)

    def tile(h, shift, keys, values, keys_t):
        query = q_ref[0, h, pl.ds(block_of(shift), share), :]
        grad = dos[h, shift]
        lse = lse_ref[0, pl.ds(h, 1), pl.ds(block_of(shift), share)]
        probs = jnp.exp2(nt(keys, query) * factor - lse)
        dprobs = nt(values, grad)
        inner = jnp.sum(probs * dprobs, axis=0, keepdims=True)
        dscores = (probs * (dprobs - inner) * scale).astype(BF)
        dqs[h, pl.ds(block_of(shift), share), :] = nn(keys_t, dscores).T.astype(BF)
        return nn(dscores, query), nn(probs.astype(BF), grad)

    @pl.when(whole == 1)
    def _():
        def head(h, carry):
            keys = k_ref[0, h]
            values = v_ref[0, h]
            keys_t = keys.astype(F32).T.astype(BF)
            dkey, dvalue = tile(h, 0, keys, values, keys_t)
            for shift in range(1, 4):
                more_key, more_value = tile(h, shift, keys, values, keys_t)
                dkey = dkey + more_key
                dvalue = dvalue + more_value
            dks[h] = dkey.astype(BF)
            dvs[h] = dvalue.astype(BF)
            return carry

        lax.fori_loop(0, heads, head, 0)

    @pl.when(whole == 0)
    def _():
        def head(h, carry):
            for shift in range(4):
                span = pl.ds(block_of(shift), share)
                keys = k_ref[0, h, span, :]
                values = v_ref[0, h, span, :]
                dkey, dvalue = tile(h, shift, keys, values, keys.astype(F32).T.astype(BF))
                dks[h, span, :] = dkey.astype(BF)
                dvs[h, span, :] = dvalue.astype(BF)
            return carry

        lax.fori_loop(0, heads, head, 0)

    for src, dst in ((dqs, dq_ref), (dks, dk_ref), (dvs, dv_ref)):
        for h in range(heads):
            dst[:, h * size : (h + 1) * size] = src[h]

    def out_rows(i, carry):
        span = pl.ds(pl.multiple_of(i * share, share), share)
        grad = nn(dq_ref[span, :], w_ref[0]) + nn(dk_ref[span, :], w_ref[1]) + nn(dv_ref[span, :], w_ref[2])
        part_ref[span, :] = grad.astype(BF)
        normed, _ = normalize(tok_ref[0, span, :].astype(F32))
        sums_ref[pl.ds(2 * i, 1), :] = jnp.sum(grad, axis=0, keepdims=True)
        sums_ref[pl.ds(2 * i + 1, 1), :] = jnp.sum(grad * normed, axis=0, keepdims=True)
        return carry

    lax.fori_loop(0, rows // share, out_rows, 0)
    bias_ref[...] = jnp.zeros_like(bias_ref)
    bias_ref[0:1, :] = jnp.sum(dq_ref[...].astype(F32), axis=0, keepdims=True)
    bias_ref[1:2, :] = jnp.sum(dv_ref[...].astype(F32), axis=0, keepdims=True)
    for which, ref in enumerate((dq_ref, dk_ref, dv_ref)):
        span = slice(which * local, (which + 1) * local)
        update = tn(ref[...], hid_ref[0])
        if last:
            wtmp[span] = (old_ref[span] + update).astype(BF)
        else:
            wout[span] = update
    if last:
        core = info_ref[2]
        half = 3 * local // 2
        for ref, place in ((wkeep, core), (wsend, 1 - core)):
            ref[:half] = wtmp[pl.ds(pl.multiple_of(place * half, half), half), :]
            ref[half:] = jnp.zeros((ref.shape[0] - half, ref.shape[1]), BF)


def attend_back(micro, info, query, key, value, lse, grads, qkv_weight, hidden, tokens, old=None, after=()):
    _, heads, rows, size = query.shape
    share = rows // 4
    local = heads * size
    width = qkv_weight.shape[2]
    last = old is not None
    full = pl.BlockSpec((1, heads, rows, size), lambda i, s: (micro, 0, 0, 0))
    row = pl.BlockSpec((1, rows, width), lambda i, s: (micro, 0, 0))

    def flat(*dims):
        return pl.BlockSpec(dims, lambda i, s: (0,) * len(dims))

    outs = [((rows, width), BF), ((8, width), F32), ((8, local), F32)]
    if last:
        outs += [((-(-3 * local // 128) * 64, width), BF)] * 2
    else:
        outs += [((3 * local, width), F32)]
    return pl.pallas_call(
        functools.partial(attend_back_kernel, last, len(after)),
        grid_spec=pltpu.PrefetchScalarGridSpec(
            num_scalar_prefetch=1,
            grid=(1,),
            in_specs=[full] * 3
            + [pl.BlockSpec((1, heads, rows), lambda i, s: (micro, 0, 0))]
            + [pl.BlockSpec((1, *grads[0].shape[1:]), lambda i, s: (micro, 0, 0))] * 4
            + [flat(*qkv_weight.shape), row, row]
            + ([flat(3 * local, width)] if last else [])
            + [ANY] * len(after),
            out_specs=[flat(*dims) for dims, _ in outs],
            scratch_shapes=[
                pltpu.VMEM((heads, 4, share, size), BF),
                pltpu.VMEM((heads, rows, size), BF),
                pltpu.VMEM((heads, rows, size), BF),
                pltpu.VMEM((heads, rows, size), BF),
                pltpu.VMEM((rows, local), BF),
                pltpu.VMEM((rows, local), BF),
                pltpu.VMEM((rows, local), BF),
                pltpu.VMEM((3 * local, width), BF),
            ],
        ),
        out_shape=[shape(dims, dtype) for dims, dtype in outs],
        compiler_params=params(),
        cost_estimate=cost(30),
        name="attend_back",
    )(info, query, key, value, lse, *grads, qkv_weight, hidden, tokens, *([old] if last else []), *after)


def finish_kernel(info_ref, grad_ref, tok_ref, mod_ref, gmid_ref, out_ref):
    normed, inverse = normalize(tok_ref[0].astype(F32))
    grad = grad_ref[...].astype(F32)
    out_ref[0] = gmid_ref[0] + norm_backward(grad * (1.0 + mod_ref[0, 1:2, :]), normed, inverse)


def finish(info, micro, grad, tokens, mod_blocks, gmid, blocks, old=None, after=()):
    _, share, width = gmid.shape
    more = ([] if old is None else [old]) + list(after)
    return pl.pallas_call(
        skipping(finish_kernel, 5, len(more)),
        grid_spec=pltpu.PrefetchScalarGridSpec(
            num_scalar_prefetch=1,
            grid=(1,),
            in_specs=[
                pl.BlockSpec((share, width), lambda i, s: (0, 0)),
                pl.BlockSpec((1, share, width), lambda i, s: (micro, s[0], 0)),
                pl.BlockSpec((1, 6, width), lambda i, s: (micro * blocks + s[0], 0, 0)),
                pl.BlockSpec((1, share, width), lambda i, s: (micro, 0, 0)),
            ]
            + [ANY] * len(more),
            out_specs=[pl.BlockSpec((1, share, width), lambda i, s: (micro, 0, 0))],
        ),
        out_shape=[shape(gmid.shape, F32)],
        input_output_aliases={} if old is None else {5: 0},
        compiler_params=params(),
        cost_estimate=cost(3),
        name="finish",
    )(info, grad, tokens, mod_blocks, gmid, *more)[0]


def in_order(row, quarter, piece):
    parts = [row[:, i * piece : (i + 1) * piece] for i in range(4)]
    out = []
    for j in range(4):
        source = jnp.bitwise_xor(quarter, j)
        value = parts[3]
        for i in range(3):
            value = jnp.where(source == i, parts[i], value)
        out.append(value)
    return jnp.concatenate(out, axis=1)


def ada_kernel(info, cond_ref, w_ref, bias_ref, units_ref, small_ref, act_ref):
    value = cond_ref[...].astype(F32)
    act = (value / (1.0 + jnp.exp(-value))).astype(BF)
    act_ref[...] = act
    count = act.shape[0]
    small_ref[...] = jnp.zeros_like(small_ref)
    small_ref[:count] = nt(act, w_ref[...]) + bias_ref[...]
    half = units_ref.shape[1] // 2
    mine = jnp.where(info[1] == 0, units_ref[:, :half], units_ref[:, half:])
    small_ref[count : count + 1, :half] = in_order(mine, info[2], half // 4)


def modulate_kernel(info, s0, s1, s2, s3, mod_ref, far_ref, near_ref, lanes, full):
    rank = info[0]
    for shift, ref in enumerate((s0, s1, s2, s3)):
        lanes[lax.rem(rank + 4 - shift, 4)] = ref[...]
    full[...] = jnp.concatenate([lanes[i] for i in range(4)], axis=1)
    width = mod_ref.shape[2]
    for i in range(mod_ref.shape[0]):
        segment = info[3 + i]
        slot = (i // 4) * 4 + jnp.minimum(segment, 3)
        row = full[pl.ds(slot, 1), :] * (segment < 4).astype(F32)
        for j in range(6):
            mod_ref[i, j : j + 1, :] = row[:, j * width : (j + 1) * width]
    half = far_ref.shape[2]
    for ref, order in ((far_ref, (s2, s1)), (near_ref, (s3, s0))):
        for i, source in enumerate(order):
            ref[i] = source[8:9, :half]


def pile_kernel(info, l0, l1, sums, far, near, out):
    rank = info[0]
    out[...] = jnp.zeros_like(out)
    for m, late in enumerate((l0, l1)):
        for slot in range(4):
            row = 6 * (4 * m + slot)
            for i in range(2):
                total = jnp.zeros((1, out.shape[1]), F32)
                for block in range(4):
                    inside = (info[3 + m * 4 + block] == slot).astype(F32)
                    total = total + inside * late[2 * block + i : 2 * block + i + 1, :]
                out[row + i : row + i + 1, :] = total
            inside = (info[3 + m * 4 + rank] == slot).astype(F32)
            out[row + 2 : row + 6, :] = inside * sums[m, 0:4, :]
    out[48:50, :] = sums[0, 4:6, :] + sums[1, 4:6, :]
    half = far.shape[2]
    for k, (ref, i) in enumerate(((near, 1), (far, 1), (far, 0), (near, 0))):
        out[pl.ds(50 + lax.rem(rank + 4 - k, 4), 1), :half] = ref[i]


def sum_kernel(a, b, out):
    out[...] = a[...] + b[...]


def slots_kernel(info, mine, got, b0, b1, act_ref, pay_ref, low_ref, full):
    rank = info[0]
    width = mine.shape[1]
    total = mine[...] + got[...]
    for row in range(8):
        for i in range(6):
            full[row : row + 1, i * width : (i + 1) * width] = total[6 * row + i : 6 * row + i + 1, :]
    columns = pay_ref.shape[1]
    half = columns - width
    pay_ref[...] = jnp.zeros_like(pay_ref)
    for i in range(4):

        @pl.when(rank == i)
        def _(i=i):
            own = full[:, i * columns : (i + 1) * columns]
            pay_ref[0:8, :] = own
            low_ref[...] = own.astype(BF)
            pay_ref[8:9, width:] = in_order(total[50 + i : 51 + i, :half], info[2], half // 4)

    pay_ref[8:9, :width] = total[48:49]
    pay_ref[9:10, :width] = total[49:50]
    both = b0[0:2, :] + b1[0:2, :]
    pay_ref[9:10, width:] = jnp.concatenate([both[0:1], both[1:2]], axis=1)
    pay_ref[10:18, :width] = act_ref[...].astype(F32)


def tail_kernel(info, pay_ref, ada_ref, ada_b, out_b, down_b, up_b, qv_b):
    width = out_b.shape[1]
    columns = pay_ref.shape[2]
    half = columns - width
    count = pay_ref.shape[0]
    mods = jnp.concatenate([pay_ref[i, 0:8, :] for i in range(count)], axis=0)
    acts = jnp.concatenate([pay_ref[i, 10:18, :width] for i in range(count)], axis=0)
    ada_ref[...] = tn(mods.astype(BF), acts.astype(BF))
    ada_b[...] = jnp.sum(mods, axis=0, keepdims=True)
    sums = [pay_ref[0, 8:10, :], pay_ref[1, 8:10, :]]
    for i in range(2, count):
        sums[i % 2] = sums[i % 2] + pay_ref[i, 8:10, :]
    total = sums[0] + sums[1]
    out_b[...] = total[0:1, :width]
    down_b[...] = total[1:2, :width]
    low = jnp.where(info[1] == 0, sums[0][0:1, width:], sums[1][0:1, width:])
    high = jnp.where(info[1] == 0, sums[1][0:1, width:], sums[0][0:1, width:])
    up_b[...] = jnp.concatenate([low, high], axis=1)
    qv_b[0:1, :] = total[1:2, width : width + half // 2]
    qv_b[1:2, :] = total[1:2, width + half // 2 :]


def pack_kernel(info, up_ref, down_ref, up_out, down_out, mine_ref, turned):
    turned[...] = up_ref[...].T
    half = up_out.shape[0]
    piece = half // 4
    for j in range(4):
        at = info[1] * half + jnp.bitwise_xor(info[2], j) * piece
        rows = pl.ds(pl.multiple_of(at, piece), piece)
        up = turned[rows, :]
        down = down_ref[rows, :]
        up_out[j * piece : (j + 1) * piece] = up
        down_out[j * piece : (j + 1) * piece] = down
        if j == 0:
            mine_ref[:piece] = up
            mine_ref[piece:] = down


def tick_kernel(out):
    out[...] = jnp.zeros_like(out)


def copy_kernel(*refs):
    count = len(refs) // 2
    for source, out in zip(refs[:count], refs[count:]):
        out[...] = source[...]


def stack_kernel(first, second, out):
    out[0] = first[...]
    out[1] = second[...]


def pack_rows(array):
    rows = array.shape[0] // 4
    return jnp.concatenate([array[i * rows : (i + 1) * rows] for i in range(4)], axis=1)


def unpack_rows(array):
    columns = array.shape[1] // 4
    return jnp.concatenate([array[:, i * columns : (i + 1) * columns] for i in range(4)], axis=0)


def plus(a, b):
    return a.astype(F32) + b.astype(F32)


def halve_kernel(uk, ur, dk, dr, u_keep, u_send, d_keep, d_send):
    for keep, got, mine, give in ((uk, ur, u_keep, u_send), (dk, dr, d_keep, d_send)):
        for i in range(keep.shape[0]):
            mine[i] = plus(keep[i, 0], got[i, 0]).astype(BF)
            give[i] = plus(keep[i, 1], got[i, 1]).astype(BF)


def quarter_kernel(uk, ur, dk, dr, first, second):
    piece = uk.shape[1]
    for i, out in enumerate((first, second)):
        out[:piece] = plus(uk[i], ur[i]).astype(BF)
        out[piece:] = plus(dk[i], dr[i]).astype(BF)


def mix_kernel(o_rows, info, uk, us, dk, ds, ok, og, u_keep, u_send, d_keep, d_send, room, sums):
    room[...] = jnp.zeros_like(room)
    for k in range(4):
        sums[...] = plus(ok[k], og[k])
        for i in range(4):
            room[k, jnp.bitwise_xor(info[2], i), :o_rows] = sums[i * o_rows : (i + 1) * o_rows].astype(BF)
    piece = uk.shape[2]
    wide = room.shape[2]
    for keep, send, mine, give, planes, near, far in (
        (uk, us, u_keep, u_send, (0, 1), (0, 1), (2, 3)),
        (dk, ds, d_keep, d_send, (2, 3), (0, 2), (1, 3)),
    ):
        for source, out, order in ((keep, mine, near), (send, give, far)):
            at = 0
            for place in range(2):
                for i in range(2):
                    out[at : at + piece] = source[i, place]
                    at += piece
                for k in planes:
                    out[at : at + wide] = room[k, order[place]]
                    at += wide


def halve_flat_kernel(uk, ur, dk, dr, u_keep, u_send, d_keep, d_send):
    for keep, got, mine, give in ((uk, ur, u_keep, u_send), (dk, dr, d_keep, d_send)):
        half = mine.shape[0]
        mine[...] = plus(keep[:half], got[:half]).astype(BF)
        give[...] = plus(keep[half:], got[half:]).astype(BF)


def last_kernel(uk, ur, dk, dr, third, o1, o2, own):
    wide = o1.shape[0]
    piece = (uk.shape[0] - 2 * wide) // 2
    up = plus(uk[...], ur[...]).astype(BF)
    down = plus(dk[...], dr[...]).astype(BF)
    for out, i in ((third, 0), (own, 1)):
        out[:piece] = up[i * piece : (i + 1) * piece]
        out[piece : 2 * piece] = down[i * piece : (i + 1) * piece]
    own[2 * piece :] = up[2 * piece : 2 * piece + wide]
    o1[...] = up[2 * piece + wide :]
    o2[...] = down[2 * piece : 2 * piece + wide]
    third[2 * piece :] = down[2 * piece + wide :]


def split_rows(total, bit, keep, send):
    half = total.shape[0] // 2
    keep[...] = total[pl.ds(pl.multiple_of(bit * half, half), half), :]
    send[...] = total[pl.ds(pl.multiple_of((1 - bit) * half, half), half), :]


def first_kernel(info, mine, got, keep, send, total):
    total[...] = plus(mine[...], got[...]).astype(BF)
    split_rows(total, jnp.bitwise_and(info[2], 1), keep, send)


def second_kernel(info, mine, got, keep, send, total):
    total[...] = plus(mine[...], got[...]).astype(BF)
    split_rows(total, info[2] >> 1, keep, send)


def merge_kernel(keep, got, own, first, second, third, o1, o2, out):
    at = keep.shape[0]
    out[:at] = plus(keep[...], got[...]).astype(BF)
    rows = first.shape[0]
    out[at : at + rows] = (plus(own[:rows], first[...]) + plus(second[...], third[:rows])).astype(BF)
    out[at + rows :] = (plus(own[rows:], o1[...]) + plus(o2[...], third[rows:])).astype(BF)


def order_kernel(o_rows, w_rows, info, b0, b1, b2, b3, halves, others, room):
    piece = halves.shape[1] // 4
    wide = room.shape[1]
    for j, ref in enumerate((b0, b1, b2, b3)):
        quarter = jnp.bitwise_xor(info[2], j)
        place = 2 * jnp.bitwise_and(quarter, 1) + (quarter >> 1)
        others[pl.ds(pl.multiple_of(place * w_rows, w_rows), w_rows), :] = ref[:w_rows]
        rows = pl.ds(pl.multiple_of(quarter * piece, piece), piece)
        halves[0, rows, :] = ref[w_rows : w_rows + piece]
        halves[1, rows, :] = ref[w_rows + piece : w_rows + 2 * piece]
        room[quarter] = ref[w_rows + 2 * piece :]
    outs = jnp.concatenate([room[i, :o_rows] for i in range(4)], axis=0)
    others[4 * w_rows :] = outs


def spread_kernel(info, own, other, own_o, other_o, up_out, down_out, qkv_out, out_out, turned, total):
    half = own.shape[1]
    here = pl.ds(pl.multiple_of(info[1] * half, half), half)
    there = pl.ds(pl.multiple_of((1 - info[1]) * half, half), half)
    turned[here, :] = own[0]
    turned[there, :] = other[0]
    down_out[here, :] = own[1].astype(F32)
    down_out[there, :] = other[1].astype(F32)
    rows = out_out.shape[0] // 2
    count = total.shape[0] // 2
    for ref, core in ((own_o, info[1]), (other_o, 1 - info[1])):
        out_out[pl.ds(pl.multiple_of(core * rows, rows), rows), :] = ref[ref.shape[0] - rows :].astype(F32)
        total[pl.ds(pl.multiple_of(core * count, count), count), :] = ref[:count]
    local = qkv_out.shape[1]
    for i in range(3):
        qkv_out[i] = total[i * local : (i + 1) * local].astype(F32)
    up_out[...] = turned[...].astype(F32).T


def turn(array, shift):
    count = lax.axis_size("tensor")
    return lax.ppermute(array, "tensor", [(i, (i + shift) % count) for i in range(count)])


def flip(array, axis):
    return lax.ppermute(array, axis, [(0, 1), (1, 0)])


def diagonal(array):
    return lax.ppermute(array, ("y", "x"), [(0, 3), (1, 2), (2, 1), (3, 0)])


def over_rest(array):
    count = lax.axis_size("rest")
    bit = 1
    while bit < count:
        other = lax.ppermute(array, "rest", [(i, i ^ bit) for i in range(count)])
        array = plus(array, other).astype(BF)
        bit *= 2
    return array


DP = ("rest", "y", "x", "core")


def local(
    tokens, conditioning, lengths, out_grad, ada_weight, ada_bias, qkv_weight, qv_bias,
    out_weight, out_bias, up_weight, up_bias, down_weight, down_bias,
):
    groups = lax.axis_size("tensor")
    rank = lax.axis_index("tensor")
    core = lax.axis_index("core")
    quarter = 2 * lax.axis_index("y") + lax.axis_index("x")
    micro, rows, width = tokens.shape
    share = rows // groups
    slots = lengths.shape[1]
    part = up_weight.shape[1]
    half = part // 2
    piece = half // 4
    columns = ada_weight.shape[1]
    local_width = qkv_weight.shape[2]
    ada_turned = ada_weight.T
    qkv_turned = qkv_weight.transpose(0, 2, 1)
    here = jnp.stack([rank, core, quarter]).astype(jnp.int32)

    boundary = jnp.cumsum(lengths, axis=1)
    starts = jnp.arange(groups, dtype=jnp.int32) * share
    segment = jnp.sum((boundary[:, None, :] <= starts[None, :, None]).astype(jnp.int32), axis=2)
    whole = (segment[:, groups - 1] == 0).astype(jnp.int32)
    own_valid = (lax.dynamic_index_in_dim(segment, rank, 1, False) < slots).astype(jnp.int32)
    info = jnp.concatenate([here, segment.reshape(-1)])

    small, cond_act = simple(
        ada_kernel,
        [shape((16, columns), F32), shape((micro * slots, width), BF)],
        [conditioning.reshape(micro * slots, width), ada_turned, ada_bias[None], up_bias[None]],
        info,
        name="ada", micros=0.01,
    )
    smalls = [small] + [turn(small, k) for k in (1, 2, 3)]

    up_near, down_near, mine = simple(
        pack_kernel,
        [shape((half, width), BF), shape((half, width), BF), shape((2 * piece, width), BF)],
        [up_weight, down_weight],
        info,
        after=(cond_act,),
        scratch=[pltpu.VMEM((part, width), BF)],
        name="pack", micros=0.01,
    )
    got = {k: turn(mine, k) for k in (2, 1, 3)}
    out_rows = lax.dynamic_slice_in_dim(out_weight, quarter * (local_width // 4), local_width // 4, 0)
    out_full = lax.all_gather(out_rows, ("tensor", "y", "x"), axis=0, tiled=True)
    out_full = out_full.reshape(groups, local_width, width)

    mod_blocks, bias_a, bias_b = simple(
        modulate_kernel,
        [
            shape((micro * groups, 6, width), F32),
            shape((2, 1, half), F32),
            shape((2, 1, half), F32),
        ],
        smalls,
        info,
        after=(mine,),
        scratch=[pltpu.VMEM((4, 16, columns), F32), pltpu.VMEM((16, 6 * width), F32)],
        name="modulate", micros=0.01,
    )
    hidden_one, query, key, value = project(tokens, mod_blocks, qkv_turned, qv_bias, groups)

    own_gate = lax.dynamic_index_in_dim(
        mod_blocks.reshape(micro, groups, 6, width), rank, 1, False
    )[:, 5:6]
    own_grad = lax.dynamic_slice_in_dim(out_grad, rank * share, share, 1).astype(F32)
    grad_mlp = own_grad * (own_valid.astype(F32)[:, None, None] * own_gate)
    own_g = grad_mlp.astype(BF).reshape(micro * share, width)
    other_g = flip(own_g, "core")

    *att, lse = attend(jnp.concatenate([rank[None], whole]), query, key, value, after=(other_g,))
    parts = [att[0], turn(att[1], 1), turn(att[2], 2), turn(att[3], 3)]

    (two,) = simple(
        stack_kernel, [shape((2, 2 * piece, width), BF)], [got[2], got[1]], after=(lse,), name="two", micros=0.01
    )
    two_parts = (two, flip(two, "x"), flip(two, "y"), diagonal(two))

    def release(arrays, after):
        return simple(
            copy_kernel, [shape(a.shape, a.dtype) for a in arrays], arrays, after=after, name="release"
        )

    attn, mid, hidden_two = middle(
        here, parts, out_full, out_bias[None], tokens, mod_blocks, groups,
    )
    own_x = hidden_two.reshape(micro * share, width)
    other_x = flip(own_x, "core")
    (third,) = release([got[3]], (mid,) + two_parts[1:])
    third_parts = (third, flip(third, "x"), flip(third, "y"), diagonal(third))
    *carry, uk_a, us_a, dk_a, ds_a, bsum_a = feed(
        own_x, other_x, own_g, other_g, [two_parts], bias_a, None
    )
    ur_a = flip(us_a, "y")
    dr_a = flip(ds_a, "x")
    mlp_own, mlp_send, gh_own, gh_send, uk_b, us_b, dk_b, ds_b, bsum_b = feed(
        own_x, other_x, own_g, other_g, [third_parts, (up_near, down_near)], bias_b, carry
    )
    gh_got = flip(gh_send, "core")
    mlp_got = flip(mlp_send, "core")
    piece_shapes = [shape((2, piece, width), BF)] * 4
    uk_a, us_a, dk_a, ds_a = simple(
        halve_kernel, piece_shapes, [uk_a, ur_a, dk_a, dr_a], after=(gh_own,), name="halve", micros=100
    )
    ur_a = flip(us_a, "x")
    dr_a = flip(ds_a, "y")
    layer_out, grad_mid, d0, d1, d2, d3, o_keep, o_send, sums = between(
        jnp.concatenate([here[:1], own_valid, here[1:2]]),
        (mlp_own, gh_own),
        (mlp_got, gh_got),
        mid, attn, out_grad, mod_blocks, down_bias[None], out_full, parts, groups,
        after=(uk_a,),
    )
    grads = [d0] + [turn(d, -k) for k, d in ((1, d1), (2, d2), (3, d3))]
    o_got = flip(o_send, "core")
    o_rows = o_keep.shape[1] // 4
    o_room = -(-o_rows // 16) * 16

    (tick,) = simple(tick_kernel, [shape((8, 128), F32)], [], after=(d0, ur_a, dr_a), name="tick", micros=100)

    side = 4 * piece + 4 * o_room
    u_keep, u_send, d_keep, d_send = simple(
        functools.partial(mix_kernel, o_rows),
        [shape((side, width), BF)] * 4,
        [uk_b, us_b, dk_b, ds_b, o_keep, o_got],
        info,
        after=(tick,),
        scratch=[pltpu.VMEM((4, 4, o_room, width), BF), pltpu.VMEM((4 * o_rows, width), F32)],
        name="mix",
    )
    u_got = flip(u_send, "y")
    d_got = flip(d_send, "x")
    block_shape = shape((2 * piece, width), BF)
    t2, t1 = simple(
        quarter_kernel,
        [block_shape] * 2,
        [uk_a, ur_a, dk_a, dr_a],
        after=(u_send, *grads[1:]),
        name="quarter",
    )
    token = (t1,)
    t2 = turn(t2, -2)
    t1 = turn(t1, -1)

    back_info = [jnp.stack([rank, whole[m], core]) for m in range(micro)]
    part_0, lsum_0, bias_0, old = attend_back(
        0, back_info[0], query, key, value, lse, grads, qkv_turned, hidden_one, tokens, after=token
    )
    share_0 = lax.psum_scatter(part_0, "tensor", scatter_dimension=0, tiled=True)
    half_shape = shape((side // 2, width), BF)
    u_keep, u_send, d_keep, d_send = simple(
        halve_flat_kernel,
        [half_shape] * 4,
        [u_keep, u_got, d_keep, d_got],
        after=(lsum_0, t1, t2),
        name="halve",
    )
    token = (u_keep,)
    u_got = flip(u_send, "x")
    d_got = flip(d_send, "y")
    part_1, lsum_1, bias_1, w_keep, w_send = attend_back(
        1, back_info[1], query, key, value, lse, grads, qkv_turned, hidden_one, tokens, old, after=token
    )
    w_got = flip(w_send, "core")
    def short(kernel, outs, operands, name, after=(), scratch=(), micros=3):
        return simple(
            kernel, outs, operands, info, after=after, scratch=scratch, name=name, micros=micros
        )

    def plain(kernel, outs, operands, name, after=(), micros=3):
        return simple(kernel, outs, operands, after=after, name=name, micros=micros)

    def rows_shape(count):
        return shape((count, width), BF)

    rows_all = w_keep.shape[0]
    keep, send = short(
        first_kernel,
        [rows_shape(rows_all // 2)] * 2,
        [w_keep, w_got],
        "first",
        scratch=[pltpu.VMEM((rows_all, width), BF)],
    )
    (pile,) = short(
        pile_kernel, [shape((56, width), F32)], [lsum_0, lsum_1, sums, bsum_a, bsum_b], "pile", (keep,)
    )
    pile_got = turn(pile, 2)
    o_shape = rows_shape(o_room)
    block_shape = rows_shape(2 * piece + o_room)
    t3, o1, o2, t0 = plain(
        last_kernel,
        [block_shape, o_shape, o_shape, block_shape],
        [u_keep, u_got, d_keep, d_got],
        "last",
        (pile, t1, t2),
    )
    token = (t3,)
    t3 = turn(t3, -3)
    o1 = turn(o1, -1)
    o2 = turn(o2, -2)
    tokens_grad = finish(here, 0, share_0, tokens, mod_blocks, grad_mid, groups, after=token)
    keep, send = short(
        second_kernel,
        [rows_shape(rows_all // 4)] * 2,
        [keep, flip(send, "x")],
        "second",
        (tokens_grad,),
        [pltpu.VMEM((rows_all // 2, width), BF)],
    )
    send_got = flip(send, "y")
    (pile,) = plain(
        sum_kernel, [shape(pile.shape, F32)], [pile, pile_got], "sum", (keep,), micros=40
    )
    pile_far = turn(pile, 1)
    (merged,) = plain(
        merge_kernel,
        [rows_shape(rows_all // 4 + 2 * piece + o_room)],
        [keep, send_got, t0, t1, t2, t3, o1, o2],
        "merge",
        (pile,),
        micros=0.1,
    )
    (part_1,) = release([part_1], (merged,))
    share_1 = lax.psum_scatter(part_1, "tensor", scatter_dimension=0, tiled=True)
    merged = over_rest(merged)
    all_four = [merged, flip(merged, "x"), flip(merged, "y"), diagonal(merged)]
    pay, mod_low = short(
        slots_kernel,
        [shape((24, columns), F32), shape((micro * slots, columns), BF)],
        [pile, pile_far, bias_0, bias_1, cond_act],
        "slots",
        (merged,),
        [pltpu.VMEM((micro * slots, 6 * width), F32)],
        micros=40,
    )
    pay_got = flip(pay, "core")
    cond_part = jnp.dot(mod_low, ada_turned, preferred_element_type=F32)

    cond_grad = cond_part + turn(cond_part, 2)
    cond_grad = cond_grad + turn(cond_grad, 1)

    def pair_kernel(mine, got, out):
        count = mine.shape[0]
        out[:count] = mine[...]
        out[count:] = got[...]

    def pair(mine, got, after=()):
        outs = [shape((2 * mine.shape[0], *mine.shape[1:]), F32)]
        return plain(pair_kernel, outs, [mine, got], "pair", after, micros=20)[0]

    pays = pair(pay[None], pay_got[None])
    pays = pair(pays, flip(pays, "x"))
    pays_got = flip(pays, "y")
    halves, others = short(
        functools.partial(order_kernel, o_rows, rows_all // 4),
        [shape((2, half, width), BF), rows_shape(rows_all + 4 * o_rows)],
        all_four,
        "order",
        (pays, cond_grad),
        [pltpu.VMEM((4, o_room, width), BF)],
        micros=0.1,
    )
    halves_got = flip(halves, "core")
    others_got = flip(others, "core")
    pays = pair(pays, pays_got, (halves,))
    if lax.axis_size("rest") > 1:
        pays = lax.all_gather(pays, "rest", axis=0, tiled=True)
    ada_weight_grad, ada_b, out_b, down_b, up_b, qv_bias_grad = short(
        tail_kernel,
        [
            shape(ada_turned.shape, F32),
            shape((1, columns), F32),
            shape((1, width), F32),
            shape((1, width), F32),
            shape((1, part), F32),
            shape(qv_bias.shape, F32),
        ],
        [pays],
        "tail",
    )
    up_weight_grad, down_weight_grad, qkv_weight_grad, out_weight_grad = short(
        spread_kernel,
        [
            shape(up_weight.shape, F32),
            shape(down_weight.shape, F32),
            shape(qkv_turned.shape, F32),
            shape(out_weight.shape, F32),
        ],
        [halves, halves_got, others, others_got],
        "spread",
        (ada_weight_grad,),
        [pltpu.VMEM((part, width), BF), pltpu.VMEM((3 * local_width, width), BF)],
    )
    cond_float = conditioning.astype(F32)
    sigmoid = jax.nn.sigmoid(cond_float)
    conditioning_grad = cond_grad.reshape(micro, slots, width) * (
        sigmoid * (1.0 + cond_float * (1.0 - sigmoid))
    )
    tokens_grad = finish(
        here, 1, share_1, tokens, mod_blocks, grad_mid, groups, tokens_grad, after=(up_weight_grad,)
    )

    return (
        layer_out,
        tokens_grad,
        conditioning_grad,
        ada_weight_grad.T,
        ada_b[0],
        qkv_weight_grad.transpose(0, 2, 1),
        qv_bias_grad,
        out_weight_grad,
        out_b[0],
        up_weight_grad,
        up_b[0],
        down_weight_grad,
        down_b[0],
    )


def solution(mesh):
    count, groups = mesh.devices.shape
    devices = mesh.devices.reshape(count // 8, 2, 2, 2, groups)
    fine = Mesh(devices, DP + ("tensor",))
    placed = (
        P(None, DP, None),
        P(None, DP, None),
        P(None, DP),
        P(None, DP, None),
        P(None, "tensor"),
        P("tensor"),
        P(None, None, "tensor"),
        P(None, "tensor"),
        P("tensor", None),
        P(),
        P(None, "tensor"),
        P("tensor"),
        P("tensor", None),
        P(),
    )
    return jax.shard_map(
        local,
        mesh=fine,
        in_specs=placed,
        out_specs=(
            P(None, DP + ("tensor",), None),
            P(None, DP + ("tensor",), None),
            P(None, DP, None),
            P(None, "tensor"),
            P("tensor"),
            P(None, None, "tensor"),
            P(None, "tensor"),
            P("tensor", None),
            P(),
            P(None, "tensor"),
            P("tensor"),
            P("tensor", None),
            P(),
        ),
        check_vma=False,
    )
```

time: 929 us -> 591 us (0.64)
  waiting for transfers between devices: 363 us -> 168 us
  blocking collectives: 97.7 us -> 0 us
  Pallas kernels: 192 us -> 279 us
  other arithmetic: 92.9 us -> 13.8 us
  local copies, waits for them, and re-layouts: 90 us -> 22.6 us
  starting transfers between devices: 42.5 us -> 83.3 us
  matrix products: 23.4 us -> 0.62 us
    unnamed x6 -> x3, waiting for transfers between devices: 107 us -> 0.05 us
    all_gather x3 -> x0, blocking collectives: 97.7 us -> none  [the longest x1 61.7 us: local(): gathered = lax.all_gather(small, 'tensor', axis=0)]
    pallas_call x12 -> x34, Pallas kernels: 192 us -> 279 us  [the longest x24 90.5 us: simple(): pl.pallas_call(body, grid_spec=pltpu.PrefetchScalarGridSpec(num_scalar_pr...]
    ppermute x20 -> x30, waiting for transfers between devices: 122 us -> 61.6 us  [the longest x27 37.4 us: flip(): return lax.ppermute(array, axis, [(0, 1), (1, 0)])]
    all_gather x2 -> x1, waiting for transfers between devices: 26.7 us -> 0.01 us  [local(): lax.all_gather(out_rows, ('tensor', 'y', 'x'), axis=0, tiled=True)]
    dot_general x6 -> x1, matrix products: 23.4 us -> 0.62 us  [local(): cond_part = jnp.dot(mod_low, ada_turned, preferred_element_type=F32)]
    ppermute x20 -> x30, starting transfers between devices: 14 us -> 35.3 us  [the longest x27 31.7 us: flip(): return lax.ppermute(array, axis, [(0, 1), (1, 0)])]
    ppermute x18 -> x21, starting transfers between devices: 28.1 us -> 47.9 us  [turn(): lax.ppermute(array, 'tensor', [(i, (i + shift) % count) for i in range(co...]
  transfers between devices with their start and end apart: 43 -> 54, of which waited for: 18 -> 25; matrix products, arithmetic and copies ran while one was open for 19% -> 4% of each run, Pallas kernels for 16% -> 46%
where the time goes in v2:
time: 591 us; the launch traced here: 581 us
  Pallas kernels  279 us (47%)
  waiting for transfers between devices  168 us (28%)
  starting transfers between devices  83.3 us (14%)
  local copies, waits for them, and re-layouts  22.6 us (4%)
  between operations  14.3 us (2%)
  other arithmetic  13.8 us (2%)
    ppermute x21, waiting for transfers between devices, turn(): lax.ppermute(array, 'tensor', [(i, (i + shift) % count) for i in range(co...  106 us
    pallas_call x24, Pallas kernels, simple(): pl.pallas_call(body, grid_spec=pltpu.PrefetchScalarGridSpec(num_scalar_pr...  90.5 us
    pallas_call x2, Pallas kernels, feed(): pl.pallas_call(functools.partial(feed_kernel, first, tuple((len(p) for p...  68.3 us
    pallas_call x2, Pallas kernels, attend_back(): pl.pallas_call(functools.partial(attend_back_kernel, last, len(after)), g...  55.5 us
    ppermute x21, starting transfers between devices, turn(): lax.ppermute(array, 'tensor', [(i, (i + shift) % count) for i in range(co...  47.9 us
    ppermute x27, waiting for transfers between devices, flip(): return lax.ppermute(array, axis, [(0, 1), (1, 0)])  37.4 us
    ppermute x27, starting transfers between devices, flip(): return lax.ppermute(array, axis, [(0, 1), (1, 0)])  31.7 us
    ppermute x3, waiting for transfers between devices, diagonal(): return lax.ppermute(array, ('y', 'x'), [(0, 3), (1, 2), (2, 1), (3, 0)])  24.2 us
  transfers between devices with their start and end apart: 54, of which 25 were waited for; matrix products, arithmetic and copies ran while one was open for 4% of the time, Pallas kernels for 46%

profile of v2, /device:TPU:10, one launch (start us, length us, event | category | flops | bytes accessed | tf_op | source)
XLA Modules:
  0.0 581.2 jit_solution(11425887285118147951)
XLA Ops:
  14.7 4.6 ada.1
  22.2 1.8 collective-permute-start.2
  24.2 5.8 pack.1
  31.4 3.2 collective-permute-done.1.refs_3_
  36.7 2.7 modulate.1
  42.1 2.0 collective-permute-start.9
  45.3 12.8 %project.1 = (bf16[2,1024,1152]{2,1,0:T(8,128)(2,1)}, bf16[2,4,1024,72]{3,2,1,0:T(8,128)(2,1)}, bf16[2,4,1024,72]{3,2,1,0:T(8,128)(2,1)}, bf16[2,4,1024,72]{3,2,1,0:T(8,128)(2,1)}) custom-call(bf16[2,1024,1152]{2,1,0:T(8,128)(2,1)} %refs_2_.5, f32[8,6,1152]{2,1,0:T(8,128)} %get-tuple-element.108.mod_ref.refs_8_.refs_3_, bf16[864,1152]{1,0:T(8,128)(2,1)} %bitcast.26, ...), custom_call_target="tpu_custom_call" | custom-call | flops 11500000 | bytes 1000 | tf_op jit(solution)/shard_map/project/pallas_call | solution.py:123
  59.2 17.1 %attend.1 = (bf16[2,64,1152]{2,1,0:T(8,128)(2,1)}, bf16[2,64,1152]{2,1,0:T(8,128)(2,1)}, bf16[2,64,1152]{2,1,0:T(8,128)(2,1)}, bf16[2,64,1152]{2,1,0:T(8,128)(2,1)}, f32[2,4,1024]{2,1,0:T(4,128)}) custom-call(s32[3]{0:T(128)} %pad_add_fusion.2.refs_0_, bf16[2,4,1024,72]{3,2,1,0:T(8,128)(2,1)} %get-tuple-element.109.refs_1_.q_ref, ...), custom_call_target="tpu_custom_call" | custom-call | flops 11500000 | bytes 1000 | tf_op jit(solution)/shard_map/attend/pallas_call | solution.py:185
  77.9 2.8 collective-permute-start.5
  82.3 31.7 %collective-permute-done.9.refs_0_ = bf16[288,1152]{1,0:T(8,128)(2,1)} collective-permute-done((bf16[288,1152]{1,0:T(8,128)(2,1)S(1)}, bf16[288,1152]{1,0:T(8,128)(2,1)}, u32[]{:S(2)}, u32[]{:S(2)}) %collective-permute-start.9) | collective-permute-done | bytes 663584 | tf_op jit(solution)/shard_map/ppermute | solution.py:931
  114.0 2.5 two.1.refs_4_
  118.4 7.2 %collective-permute-done.4.refs_2_.refs_12_ = bf16[2,64,1152]{2,1,0:T(8,128)(2,1)S(1)} collective-permute-done((bf16[2,64,1152]{2,1,0:T(8,128)(2,1)}, bf16[2,64,1152]{2,1,0:T(8,128)(2,1)S(1)}, u32[]{:S(2)}, u32[]{:S(2)}) %collective-permute-start.4) | collective-permute-done | bytes 294944 | tf_op jit(solution)/shard_map/ppermute | solution.py:931
  127.1 4.9 collective-permute-done.5.refs_3_.refs_13_
  131.9 1.9 collective-permute-done.6.refs_4_.refs_14_
  134.6 8.2 %middle.1 = (f32[2,256,1152]{2,1,0:T(8,128)}, f32[2,256,1152]{2,1,0:T(8,128)}, bf16[2,256,1152]{2,1,0:T(8,128)(2,1)}) custom-call(s32[3]{0:T(128)} %pad_add_fusion.1.refs_0_, bf16[2,64,1152]{2,1,0:T(8,128)(2,1)} %get-tuple-element.112.refs_1_.refs_11_, bf16[2,64,1152]{2,1,0:T(8,128)(2,1)} %copy-done.36, bf16[2,64,1152]{2,1,0:T(8,128)(2,1)} %copy-done.37, ...), custom_call_target="tpu_custom_call" | custom-call | flops 9200000000 | bytes 800000 | tf_op jit(solution)/shard_map/middle/pallas_call | solution.py:217
  147.2 12.9 %collective-permute-done.8.refs_0_ = bf16[288,1152]{1,0:T(8,128)(2,1)S(1)} collective-permute-done((bf16[288,1152]{1,0:T(8,128)(2,1)S(1)}, bf16[288,1152]{1,0:T(8,128)(2,1)S(1)}, u32[]{:S(2)}, u32[]{:S(2)}) %collective-permute-start.8) | collective-permute-done | bytes 663584 | tf_op jit(solution)/shard_map/ppermute | solution.py:931
  160.1 15.1 %collective-permute-done.12.refs_3_.refs_6_ = bf16[2,288,1152]{2,1,0:T(8,128)(2,1)} collective-permute-done((bf16[2,288,1152]{2,1,0:T(8,128)(2,1)}, bf16[2,288,1152]{2,1,0:T(8,128)(2,1)}, u32[]{:S(2)}, u32[]{:S(2)}) %collective-permute-start.12) | collective-permute-done | bytes 1327136 | tf_op jit(solution)/shard_map/ppermute | solution.py:935
  175.2 1.9 collective-permute-done.13.refs_4_.refs_7_
  177.1 2.0 release.2.refs_4_
  182.6 32.5 %feed.2 = (f32[512,1152]{1,0:T(8,128)}, f32[512,1152]{1,0:T(8,128)}, f32[512,1152]{1,0:T(8,128)}, f32[512,1152]{1,0:T(8,128)}, bf16[2,2,144,1152]{3,2,1,0:T(8,12...) custom-call(bf16[512,1152]{1,0:T(8,128)(2,1)} %bitcast.38, ...), custom_call_target="tpu_custom_call" | custom-call | flops 39099998208 | bytes 3400000 | tf_op jit(solution)/shard_map/feed/pallas_call | solution.py:352
  218.8 35.8 %feed.3 = (f32[512,1152]{1,0:T(8,128)}, f32[512,1152]{1,0:T(8,128)}, f32[512,1152]{1,0:T(8,128)}, f32[512,1152]{1,0:T(8,128)}, bf16[2,2,144,1152]{3,2,1,0:T(8,12...) custom-call(bf16[512,1152]{1,0:T(8,128)(2,1)} %bitcast.39, ...), custom_call_target="tpu_custom_call" | custom-call | flops 39099998208 | bytes 3400000 | tf_op jit(solution)/shard_map/feed/pallas_call | solution.py:352
  256.2 4.2 halve.2
  263.6 18.0 %between.1 = (bf16[2,256,1152]{2,1,0:T(8,128)(2,1)}, f32[2,256,1152]{2,1,0:T(8,128)}, bf16[2,64,1152]{2,1,0:T(8,128)(2,1)}, bf16[2,64,1152]{2,1,0:T(8,128)(2,1)}...) custom-call(s32[4]{0:T(128)} %pad_add_fusion.refs_0_, ...), custom_call_target="tpu_custom_call" | custom-call | flops 20700000256 | bytes 1800000 | tf_op jit(solution)/shard_map/between/pallas_call | solution.py:432
  281.7 4.4 collective-permute-start.21
  286.0 2.1 collective-permute-start.23
  290.7 7.7 %mix.1 = (bf16[768,1152]{1,0:T(8,128)(2,1)}, bf16[768,1152]{1,0:T(8,128)(2,1)}, bf16[768,1152]{1,0:T(8,128)(2,1)}, bf16[768,1152]{1,0:T(8,128)(2,1)}) custom-call(s32[11]{0:T(128)} %pad_add_fusion.3.refs_0_, bf16[2,2,144,1152]{3,2,1,0:T(8,128)(2,1)} %get-tuple-element.146.refs_1_, bf16[2,2,144,1152]{3,2,1,0:T(8,128)(2,1)} %get-tuple-element.147.refs_2_, ...), custom_call_target="tpu_custom_call" | custom-call | flops 3449999872 | bytes 300000 | tf_op jit(solution)/shard_map/mix/pallas_call | solution.py:69
  299.8 6.3 %collective-permute-done.22.refs_6_.g2 = bf16[2,64,1152]{2,1,0:T(8,128)(2,1)S(1)} collective-permute-done((bf16[2,64,1152]{2,1,0:T(8,128)(2,1)}, bf16[2,64,1152]{2,1,0:T(8,128)(2,1)S(1)}, u32[]{:S(2)}, u32[]{:S(2)}) %collective-permute-start.22) | collective-permute-done | bytes 294944 | tf_op jit(solution)/shard_map/ppermute | solution.py:931
  306.1 6.1 %collective-permute-done.23.refs_7_.g3 = bf16[2,64,1152]{2,1,0:T(8,128)(2,1)S(1)} collective-permute-done((bf16[2,64,1152]{2,1,0:T(8,128)(2,1)}, bf16[2,64,1152]{2,1,0:T(8,128)(2,1)S(1)}, u32[]{:S(2)}, u32[]{:S(2)}) %collective-permute-start.23) | collective-permute-done | bytes 294944 | tf_op jit(solution)/shard_map/ppermute | solution.py:931
  313.0 2.9 quarter.1
  315.9 3.8 collective-permute-start.30
  320.4 32.3 %attend_back.2 = (bf16[1024,1152]{1,0:T(8,128)(2,1)}, f32[8,1152]{1,0:T(8,128)}, f32[8,288]{1,0:T(8,128)}, f32[864,1152]{1,0:T(8,128)}) custom-call(s32[3]{0:T(128)} %add_add_fusion.1.info_ref, bf16[2,4,1024,72]{3,2,1,0:T(8,128)(2,1)} %get-tuple-element.109.refs_1_.q_ref, bf16[2,4,1024,72]{3,2,1,0:T(8,128)(2,1)} %get-tuple-element.110.refs_2_.k_ref, ...), custom_call_target="tpu_custom_call" | custom-call | flops 34500001792 | bytes 3000000 | tf_op jit(solution)/shard_map/attend_back/pallas_call | solution.py:593
  352.7 5.9 %collective-permute-done.30.refs_6_.refs_4_ = bf16[288,1152]{1,0:T(8,128)(2,1)S(1)} collective-permute-done((bf16[288,1152]{1,0:T(8,128)(2,1)}, bf16[288,1152]{1,0:T(8,128)(2,1)S(1)}, u32[]{:S(2)}, u32[]{:S(2)}) %collective-permute-start.30) | collective-permute-done | bytes 663584 | tf_op jit(solution)/shard_map/ppermute | solution.py:931
  360.0 5.1 halve.3
  365.1 23.2 %attend_back.3 = (bf16[1024,1152]{1,0:T(8,128)(2,1)}, f32[8,1152]{1,0:T(8,128)}, f32[8,288]{1,0:T(8,128)}, bf16[448,1152]{1,0:T(8,128)(2,1)}, bf16[448,1152]{1,0:T(8,128)(2,1)}) custom-call(s32[3]{0:T(128)} %add_add_fusion.info_ref, bf16[2,4,1024,72]{3,2,1,0:T(8,128)(2,1)} %get-tuple-element.109.refs_1_.q_ref, ...), custom_call_target="tpu_custom_call" | custom-call | flops 34500001792 | bytes 3000000 | tf_op jit(solution)/shard_map/attend_back/pallas_call | solution.py:593
  388.4 9.6 %collective-permute-start.33 = (bf16[384,1152]{1,0:T(8,128)(2,1)S(1)}, bf16[384,1152]{1,0:T(8,128)(2,1)S(1)}, u32[]{:S(2)}, u32[]{:S(2)}) collective-permute-start(bf16[384,1152]{1,0:T(8,128)(2,1)S(1)} %copy-done.28), channel_id=1, source_target_pairs={{0,8},{8,0},{1,9},{9,1},{2,10},{10,2},{3,11},{11,3},{4,12},{12,4},... | collective-permute-start | bytes 2654216 | tf_op jit(solution)/shard_map/ppermute | solution.py:935
  398.0 3.6 collective-permute-start.34
  402.5 3.7 first.1
  406.4 2.4 pile.1.refs_4_.refs_0_
  408.8 4.0 collective-permute-start.39
  412.7 5.7 collective-permute-done.33.refs_1_
  418.4 3.2 collective-permute-done.34.refs_3_
  421.6 3.5 last.1
  425.1 11.6 %collective-permute-start.36 = (bf16[336,1152]{1,0:T(8,128)(2,1)}, bf16[336,1152]{1,0:T(8,128)(2,1)S(1)}, u32[]{:S(2)}, u32[]{:S(2)}) collective-permute-start(bf16[336,1152]{1,0:T(8,128)(2,1)} %get-tuple-element.175.refs_5_), channel_id=1, source_target_pairs={{0,1},{1,2},{2,3},{3,0},{4,5},{5,6},{6,7},{7,4},{8,9},{9,10},{10,1... | collective-permute-start | bytes 2322440 | tf_op jit(solution)/shard_map/ppermute | solution.py:931
  436.7 4.1 finish.2.refs_3_.refs_5_
  440.8 2.9 second.1
  446.2 1.9 sum.1.refs_8_.refs_1_
  448.1 2.2 collective-permute-start.43
  452.0 2.4 collective-permute-start.38
  454.4 13.8 %collective-permute-done.37.refs_6_ = bf16[48,1152]{1,0:T(8,128)(2,1)S(1)} collective-permute-done((bf16[48,1152]{1,0:T(8,128)(2,1)S(1)}, bf16[48,1152]{1,0:T(8,128)(2,1)S(1)}, u32[]{:S(2)}, u32[]{:S(2)}) %collective-permute-start.37) | collective-permute-done | bytes 110624 | tf_op jit(solution)/shard_map/ppermute | solution.py:931
  469.2 3.4 merge.1.refs_1_.refs_6_
  473.3 2.9 slots.1
  484.6 3.2 release.3
  487.9 3.5 collective-permute-done.45.refs_1_
  491.4 2.0 pair.4.refs_5_.refs_0_
  496.7 4.3 collective-permute-done.46
  500.9 3.1 collective-permute-start.47
  504.1 4.9 collective-permute-done.47
  509.1 4.5 collective-permute-done.40.refs_2_
  513.5 22.3 %collective-permute-done.42.refs_4_ = bf16[448,1152]{1,0:T(8,128)(2,1)} collective-permute-done((bf16[448,1152]{1,0:T(8,128)(2,1)}, bf16[448,1152]{1,0:T(8,128)(2,1)}, u32[]{:S(2)}, u32[]{:S(2)}) %collective-permute-start.42) | collective-permute-done | bytes 1032224 | tf_op jit(solution)/shard_map/ppermute | solution.py:939
  535.8 5.1 order.1
  543.7 2.5 pair.5.refs_1_
  546.2 6.5 %tail.1 = (f32[1728,1152]{1,0:T(8,128)}, f32[1,1728]{1,0:T(1,128)}, f32[1,1152]{1,0:T(1,128)}, f32[1,1152]{1,0:T(1,128)}, f32[1,1152]{1,0:T(1,128)}, /*index=5*/f32[2,288]{1,0:T(2,128)}) custom-call(s32[11]{0:T(128)} %pad_add_fusion.3.refs_0_, f32[8,24,1728]{2,1,0:T(8,128)} %pair.5.refs_1_), custom_call_target="tpu_custom_call" | custom-call | flops 3449999872 | bytes 300000 | tf_op jit(solution)/shard_map/tail/pallas_call | solution.py:69
  559.5 10.7 %spread.1 = (f32[1152,1152]{1,0:T(8,128)}, f32[1152,1152]{1,0:T(8,128)}, f32[3,288,1152]{2,1,0:T(8,128)}, f32[288,1152]{1,0:T(8,128)}) custom-call(s32[11]{0:T(128)} %pad_add_fusion.3.refs_0_, bf16[2,576,1152]{2,1,0:T(8,128)(2,1)} %get-tuple-element.185.refs_2_.refs_1_, bf16[2,576,1152]{2,1,0:T(8,128)(2,1)} %copy-done.3, ...), custom_call_target="tpu_custom_call" | custom-call | flops 3449999872 | bytes 300000 | tf_op jit(solution)/shard_map/spread/pallas_call | solution.py:69
  570.2 4.2 finish.3
  (212 shorter events, 77.8 us)
Async XLA Ops:
  7.2 126.7 %all-gather.2.cloned.1.call-start = ((), (), s32[]{:S(2)}) async-start(), calls=%async_computation.2 | async-start | bytes 2820096 | tf_op jit(solution)/shard_map/all_gather | solution.py:1002
  9.0 427.8 %reduce-scatter.3.cloned.1.call-start = ((), (), s32[]{:S(2)}) async-start(), calls=%async_computation.3 | async-start | bytes 2949120 | tf_op jit(solution)/shard_map/reduce_scatter | solution.py:1106
  19.3 12.0 %collective-permute-start = (f32[16,1728]{1,0:T(8,128)}, f32[16,1728]{1,0:T(8,128)S(1)}, u32[]{:S(2)}, u32[]{:S(2)}) collective-permute-start(f32[16,1728]{1,0:T(8,128)} %get-tuple-element.105.refs_1_), channel_id=1, source_target_pairs={{0,1},{1,2},{2,3},{3,0},{4,5},{5,6},{6,7},{7,4},{8,9},{9,10},{10,1... | collective-permute-start | bytes 331784 | tf_op jit(solution)/shard_map/ppermute | solution.py:931
  20.9 13.6 %collective-permute-start.1 = (f32[16,1728]{1,0:T(8,128)}, f32[16,1728]{1,0:T(8,128)S(1)}, u32[]{:S(2)}, u32[]{:S(2)}) collective-permute-start(f32[16,1728]{1,0:T(8,128)} %get-tuple-element.105.refs_1_), channel_id=1, source_target_pairs={{0,2},{1,3},{2,0},{3,1},{4,6},{5,7},{6,4},{7,5},{8,10},{9,11},{10,... | collective-permute-start | bytes 331784 | tf_op jit(solution)/shard_map/ppermute | solution.py:931
  22.2 13.9 %collective-permute-start.2 = (f32[16,1728]{1,0:T(8,128)}, f32[16,1728]{1,0:T(8,128)S(1)}, u32[]{:S(2)}, u32[]{:S(2)}) collective-permute-start(f32[16,1728]{1,0:T(8,128)} %get-tuple-element.105.refs_1_), channel_id=1, source_target_pairs={{0,3},{1,0},{2,1},{3,2},{4,7},{5,4},{6,5},{7,6},{8,11},{9,8},{10,9... | collective-permute-start | bytes 331784 | tf_op jit(solution)/shard_map/ppermute | solution.py:931
  30.0 14.1 %copy-start.21 = (f32[2,288]{1,0:T(2,128)S(1)}, f32[2,288]{1,0:T(2,128)}, u32[]{:S(2)}) copy-start(f32[2,288]{1,0:T(2,128)} %param.21) | copy-start | bytes 6916
  41.9 16.2 %copy-start.4 = (bf16[2,256,1152]{2,1,0:T(8,128)(2,1)}, bf16[2,256,1152]{2,1,0:T(8,128)(2,1)S(1)}, u32[]{:S(2)}) copy-start(bf16[2,256,1152]{2,1,0:T(8,128)(2,1)S(1)} %multiply_convert_fusion) | copy-start | bytes 3538948
  41.9 16.2 %collective-permute-start.3 = (bf16[512,1152]{1,0:T(8,128)(2,1)S(1)}, bf16[512,1152]{1,0:T(8,128)(2,1)S(1)}, u32[]{:S(2)}, u32[]{:S(2)}) collective-permute-start(bf16[512,1152]{1,0:T(8,128)(2,1)S(1)} %bitcast.30), channel_id=1, source_target_pairs={{0,4},{4,0},{1,5},{5,1},{2,6},{6,2},{3,7},{7,3},{8,12},{12,8},{9,1... | collective-permute-start | bytes 3538952 | tf_op jit(solution)/shard_map/ppermute | solution.py:935
  42.0 40.3 %collective-permute-start.10 = (bf16[288,1152]{1,0:T(8,128)(2,1)S(1)}, bf16[288,1152]{1,0:T(8,128)(2,1)}, u32[]{:S(2)}, u32[]{:S(2)}) collective-permute-start(bf16[288,1152]{1,0:T(8,128)(2,1)S(1)} %copy-done.7), channel_id=1, source_target_pairs={{0,1},{1,2},{2,3},{3,0},{4,5},{5,6},{6,7},{7,4},{8,9},{9,10},{10,1... | collective-permute-start | bytes 1990664 | tf_op jit(solution)/shard_map/ppermute | solution.py:931
  42.1 71.9 %collective-permute-start.9 = (bf16[288,1152]{1,0:T(8,128)(2,1)S(1)}, bf16[288,1152]{1,0:T(8,128)(2,1)}, u32[]{:S(2)}, u32[]{:S(2)}) collective-permute-start(bf16[288,1152]{1,0:T(8,128)(2,1)S(1)} %copy-done.7), channel_id=1, source_target_pairs={{0,2},{1,3},{2,0},{3,1},{4,6},{5,7},{6,4},{7,5},{8,10},{9,11},{10,... | collective-permute-start | bytes 1990664 | tf_op jit(solution)/shard_map/ppermute | solution.py:931
  59.2 21.9 %copy-start.19 = (f32[1152]{0:T(1024)S(1)}, f32[1152]{0:T(1024)}, u32[]{:S(2)}) copy-start(f32[1152]{0:T(1024)} %param.23) | copy-start | bytes 13828
  76.3 49.3 %collective-permute-start.4 = (bf16[2,64,1152]{2,1,0:T(8,128)(2,1)}, bf16[2,64,1152]{2,1,0:T(8,128)(2,1)S(1)}, u32[]{:S(2)}, u32[]{:S(2)}) collective-permute-start(bf16[2,64,1152]{2,1,0:T(8,128)(2,1)} %get-tuple-element.113), channel_id=1, source_target_pairs={{0,1},{1,2},{2,3},{3,0},{4,5},{5,6},{6,7},{7,4},{8,9},{9,10},{10,1... | collective-permute-start | bytes 884744 | tf_op jit(solution)/shard_map/ppermute | solution.py:931
  77.9 54.0 %collective-permute-start.5 = (bf16[2,64,1152]{2,1,0:T(8,128)(2,1)}, bf16[2,64,1152]{2,1,0:T(8,128)(2,1)S(1)}, u32[]{:S(2)}, u32[]{:S(2)}) collective-permute-start(bf16[2,64,1152]{2,1,0:T(8,128)(2,1)} %get-tuple-element.114), channel_id=1, source_target_pairs={{0,2},{1,3},{2,0},{3,1},{4,6},{5,7},{6,4},{7,5},{8,10},{9,11},{10,... | collective-permute-start | bytes 884744 | tf_op jit(solution)/shard_map/ppermute | solution.py:931
  80.7 53.2 %collective-permute-start.6 = (bf16[2,64,1152]{2,1,0:T(8,128)(2,1)}, bf16[2,64,1152]{2,1,0:T(8,128)(2,1)S(1)}, u32[]{:S(2)}, u32[]{:S(2)}) collective-permute-start(bf16[2,64,1152]{2,1,0:T(8,128)(2,1)} %get-tuple-element.115), channel_id=1, source_target_pairs={{0,3},{1,0},{2,1},{3,2},{4,7},{5,4},{6,5},{7,6},{8,11},{9,8},{10,9... | collective-permute-start | bytes 884744 | tf_op jit(solution)/shard_map/ppermute | solution.py:931
  116.4 43.7 %collective-permute-start.11 = (bf16[2,288,1152]{2,1,0:T(8,128)(2,1)}, bf16[2,288,1152]{2,1,0:T(8,128)(2,1)S(1)}, u32[]{:S(2)}, u32[]{:S(2)}) collective-permute-start(bf16[2,288,1152]{2,1,0:T(8,128)(2,1)} %two.1.refs_4_), channel_id=1, source_target_pairs={{0,8},{8,0},{1,9},{9,1},{2,10},{10,2},{3,11},{11,3},{4,12},{12,4},... | collective-permute-start | bytes 3981320 | tf_op jit(solution)/shard_map/ppermute | solution.py:935
  116.9 58.3 %collective-permute-start.12 = (bf16[2,288,1152]{2,1,0:T(8,128)(2,1)}, bf16[2,288,1152]{2,1,0:T(8,128)(2,1)}, u32[]{:S(2)}, u32[]{:S(2)}) collective-permute-start(bf16[2,288,1152]{2,1,0:T(8,128)(2,1)} %two.1.refs_4_), channel_id=1, source_target_pairs={{0,16},{16,0},{1,17},{17,1},{2,18},{18,2},{3,19},{19,3},{4,20},{20... | collective-permute-start | bytes 3981320 | tf_op jit(solution)/shard_map/ppermute | solution.py:935
  125.6 51.5 %collective-permute-start.13 = (bf16[2,288,1152]{2,1,0:T(8,128)(2,1)}, bf16[2,288,1152]{2,1,0:T(8,128)(2,1)}, u32[]{:S(2)}, u32[]{:S(2)}) collective-permute-start(bf16[2,288,1152]{2,1,0:T(8,128)(2,1)} %two.1.refs_4_), channel_id=1, source_target_pairs={{0,24},{8,16},{16,8},{24,0},{1,25},{9,17},{17,9},{25,1},{2,26},{10... | collective-permute-start | bytes 3981320 | tf_op jit(solution)/shard_map/ppermute | solution.py:939
  142.8 39.8 %collective-permute-start.7 = (bf16[512,1152]{1,0:T(8,128)(2,1)}, bf16[512,1152]{1,0:T(8,128)(2,1)}, u32[]{:S(2)}, u32[]{:S(2)}) collective-permute-start(bf16[512,1152]{1,0:T(8,128)(2,1)} %bitcast.37), channel_id=1, source_target_pairs={{0,4},{4,0},{1,5},{5,1},{2,6},{6,2},{3,7},{7,3},{8,12},{12,8},{9,1... | collective-permute-start | bytes 3538952 | tf_op jit(solution)/shard_map/ppermute | solution.py:935
  142.9 17.2 %collective-permute-start.8 = (bf16[288,1152]{1,0:T(8,128)(2,1)S(1)}, bf16[288,1152]{1,0:T(8,128)(2,1)S(1)}, u32[]{:S(2)}, u32[]{:S(2)}) collective-permute-start(bf16[288,1152]{1,0:T(8,128)(2,1)S(1)} %copy-done.7), channel_id=1, source_target_pairs={{0,3},{1,0},{2,1},{3,2},{4,7},{5,4},{6,5},{7,6},{8,11},{9,8},{10,9... | collective-permute-start | bytes 1990664 | tf_op jit(solution)/shard_map/ppermute | solution.py:931
  160.1 17.0 %copy-start.35 = (bf16[288,1152]{1,0:T(8,128)(2,1)}, bf16[288,1152]{1,0:T(8,128)(2,1)S(1)}, u32[]{:S(2)}) copy-start(bf16[288,1152]{1,0:T(8,128)(2,1)S(1)} %collective-permute-done.8.refs_0_) | copy-start | bytes 1990660
  160.1 17.0 %copy-start.23 = (bf16[2,288,1152]{2,1,0:T(8,128)(2,1)}, bf16[2,288,1152]{2,1,0:T(8,128)(2,1)S(1)}, u32[]{:S(2)}) copy-start(bf16[2,288,1152]{2,1,0:T(8,128)(2,1)S(1)} %collective-permute-done.11.refs_2_.refs_5_) | copy-start | bytes 3981316
  179.1 38.4 %collective-permute-start.14 = (bf16[288,1152]{1,0:T(8,128)(2,1)}, bf16[288,1152]{1,0:T(8,128)(2,1)S(1)}, u32[]{:S(2)}, u32[]{:S(2)}) collective-permute-start(bf16[288,1152]{1,0:T(8,128)(2,1)} %release.2.refs_4_), channel_id=1, source_target_pairs={{0,8},{8,0},{1,9},{9,1},{2,10},{10,2},{3,11},{11,3},{4,12},{12,4},... | collective-permute-start | bytes 1990664 | tf_op jit(solution)/shard_map/ppermute | solution.py:935
  179.7 37.8 %collective-permute-start.15 = (bf16[288,1152]{1,0:T(8,128)(2,1)}, bf16[288,1152]{1,0:T(8,128)(2,1)S(1)}, u32[]{:S(2)}, u32[]{:S(2)}) collective-permute-start(bf16[288,1152]{1,0:T(8,128)(2,1)} %release.2.refs_4_), channel_id=1, source_target_pairs={{0,16},{16,0},{1,17},{17,1},{2,18},{18,2},{3,19},{19,3},{4,20},{20... | collective-permute-start | bytes 1990664 | tf_op jit(solution)/shard_map/ppermute | solution.py:935
  181.4 36.1 %collective-permute-start.16 = (bf16[288,1152]{1,0:T(8,128)(2,1)}, bf16[288,1152]{1,0:T(8,128)(2,1)S(1)}, u32[]{:S(2)}, u32[]{:S(2)}) collective-permute-start(bf16[288,1152]{1,0:T(8,128)(2,1)} %release.2.refs_4_), channel_id=1, source_target_pairs={{0,24},{8,16},{16,8},{24,0},{1,25},{9,17},{17,9},{25,1},{2,26},{10... | collective-permute-start | bytes 1990664 | tf_op jit(solution)/shard_map/ppermute | solution.py:939
  215.1 40.1 %collective-permute-start.19 = (bf16[2,2,144,1152]{3,2,1,0:T(8,128)(2,1)}, bf16[2,2,144,1152]{3,2,1,0:T(8,128)(2,1)S(1)}, u32[]{:S(2)}, u32[]{:S(2)}) collective-permute-start(bf16[2,2,144,1152]{3,2,1,0:T(8,128)(2,1)} %get-tuple-element.133), channel_id=1, source_target_pairs={{0,16},{16,0},{1,17},{17,1},{2,18},{18,2},{3,19},{19,3},{4,20},{20... | collective-permute-start | bytes 3981320 | tf_op jit(solution)/shard_map/ppermute | solution.py:935
  215.7 39.5 %collective-permute-start.20 = (bf16[2,2,144,1152]{3,2,1,0:T(8,128)(2,1)}, bf16[2,2,144,1152]{3,2,1,0:T(8,128)(2,1)}, u32[]{:S(2)}, u32[]{:S(2)}) collective-permute-start(bf16[2,2,144,1152]{3,2,1,0:T(8,128)(2,1)} %get-tuple-element.135), channel_id=1, source_target_pairs={{0,8},{8,0},{1,9},{9,1},{2,10},{10,2},{3,11},{11,3},{4,12},{12,4},... | collective-permute-start | bytes 3981320 | tf_op jit(solution)/shard_map/ppermute | solution.py:935
  254.6 7.6 %collective-permute-start.17 = (f32[512,1152]{1,0:T(8,128)}, f32[512,1152]{1,0:T(8,128)S(1)}, u32[]{:S(2)}, u32[]{:S(2)}) collective-permute-start(f32[512,1152]{1,0:T(8,128)} %get-tuple-element.128), channel_id=1, source_target_pairs={{0,4},{4,0},{1,5},{5,1},{2,6},{6,2},{3,7},{7,3},{8,12},{12,8},{9,1... | collective-permute-start | bytes 7077896 | tf_op jit(solution)/shard_map/ppermute | solution.py:935
  254.7 8.2 %collective-permute-start.18 = (f32[512,1152]{1,0:T(8,128)}, f32[512,1152]{1,0:T(8,128)}, u32[]{:S(2)}, u32[]{:S(2)}) collective-permute-start(f32[512,1152]{1,0:T(8,128)} %get-tuple-element.130), channel_id=1, source_target_pairs={{0,4},{4,0},{1,5},{5,1},{2,6},{6,2},{3,7},{7,3},{8,12},{12,8},{9,1... | collective-permute-start | bytes 7077896 | tf_op jit(solution)/shard_map/ppermute | solution.py:935
  260.4 25.6 %collective-permute-start.24 = (bf16[2,144,1152]{2,1,0:T(8,128)(2,1)}, bf16[2,144,1152]{2,1,0:T(8,128)(2,1)S(1)}, u32[]{:S(2)}, u32[]{:S(2)}) collective-permute-start(bf16[2,144,1152]{2,1,0:T(8,128)(2,1)} %get-tuple-element.143), channel_id=1, source_target_pairs={{0,8},{8,0},{1,9},{9,1},{2,10},{10,2},{3,11},{11,3},{4,12},{12,4},... | collective-permute-start | bytes 1990664 | tf_op jit(solution)/shard_map/ppermute | solution.py:935
  260.7 27.4 %collective-permute-start.25 = (bf16[2,144,1152]{2,1,0:T(8,128)(2,1)}, bf16[2,144,1152]{2,1,0:T(8,128)(2,1)S(1)}, u32[]{:S(2)}, u32[]{:S(2)}) collective-permute-start(bf16[2,144,1152]{2,1,0:T(8,128)(2,1)} %get-tuple-element.145), channel_id=1, source_target_pairs={{0,16},{16,0},{1,17},{17,1},{2,18},{18,2},{3,19},{19,3},{4,20},{20... | collective-permute-start | bytes 1990664 | tf_op jit(solution)/shard_map/ppermute | solution.py:935
  281.6 8.0 %collective-permute-start.26 = (bf16[4,144,1152]{2,1,0:T(8,128)(2,1)}, bf16[4,144,1152]{2,1,0:T(8,128)(2,1)S(1)}, u32[]{:S(2)}, u32[]{:S(2)}) collective-permute-start(bf16[4,144,1152]{2,1,0:T(8,128)(2,1)} %get-tuple-element.151), channel_id=1, source_target_pairs={{0,4},{4,0},{1,5},{5,1},{2,6},{6,2},{3,7},{7,3},{8,12},{12,8},{9,1... | collective-permute-start | bytes 3981320 | tf_op jit(solution)/shard_map/ppermute | solution.py:935
  281.7 18.1 %collective-permute-start.21 = (bf16[2,64,1152]{2,1,0:T(8,128)(2,1)}, bf16[2,64,1152]{2,1,0:T(8,128)(2,1)S(1)}, u32[]{:S(2)}, u32[]{:S(2)}) collective-permute-start(bf16[2,64,1152]{2,1,0:T(8,128)(2,1)} %get-tuple-element.139), channel_id=1, source_target_pairs={{0,3},{1,0},{2,1},{3,2},{4,7},{5,4},{6,5},{7,6},{8,11},{9,8},{10,9... | collective-permute-start | bytes 884744 | tf_op jit(solution)/shard_map/ppermute | solution.py:931
  286.0 20.1 %collective-permute-start.22 = (bf16[2,64,1152]{2,1,0:T(8,128)(2,1)}, bf16[2,64,1152]{2,1,0:T(8,128)(2,1)S(1)}, u32[]{:S(2)}, u32[]{:S(2)}) collective-permute-start(bf16[2,64,1152]{2,1,0:T(8,128)(2,1)} %get-tuple-element.140), channel_id=1, source_target_pairs={{0,2},{1,3},{2,0},{3,1},{4,6},{5,7},{6,4},{7,5},{8,10},{9,11},{10,... | collective-permute-start | bytes 884744 | tf_op jit(solution)/shard_map/ppermute | solution.py:931
  286.0 26.2 %collective-permute-start.23 = (bf16[2,64,1152]{2,1,0:T(8,128)(2,1)}, bf16[2,64,1152]{2,1,0:T(8,128)(2,1)S(1)}, u32[]{:S(2)}, u32[]{:S(2)}) collective-permute-start(bf16[2,64,1152]{2,1,0:T(8,128)(2,1)} %get-tuple-element.141), channel_id=1, source_target_pairs={{0,1},{1,2},{2,3},{3,0},{4,5},{5,6},{6,7},{7,4},{8,9},{9,10},{10,1... | collective-permute-start | bytes 884744 | tf_op jit(solution)/shard_map/ppermute | solution.py:931
  298.4 60.2 %collective-permute-start.27 = (bf16[768,1152]{1,0:T(8,128)(2,1)}, bf16[768,1152]{1,0:T(8,128)(2,1)}, u32[]{:S(2)}, u32[]{:S(2)}) collective-permute-start(bf16[768,1152]{1,0:T(8,128)(2,1)} %get-tuple-element.152.refs_4_), channel_id=1, source_target_pairs={{0,16},{16,0},{1,17},{17,1},{2,18},{18,2},{3,19},{19,3},{4,20},{20... | collective-permute-start | bytes 5308424 | tf_op jit(solution)/shard_map/ppermute | solution.py:935
  299.8 12.4 %copy-start.39 = (bf16[2,64,1152]{2,1,0:T(8,128)(2,1)}, bf16[2,64,1152]{2,1,0:T(8,128)(2,1)S(1)}, u32[]{:S(2)}) copy-start(bf16[2,64,1152]{2,1,0:T(8,128)(2,1)S(1)} %collective-permute-done.21.refs_5_.g1) | copy-start | bytes 884740
  315.9 36.8 %collective-permute-start.29 = (bf16[288,1152]{1,0:T(8,128)(2,1)}, bf16[288,1152]{1,0:T(8,128)(2,1)S(1)}, u32[]{:S(2)}, u32[]{:S(2)}) collective-permute-start(bf16[288,1152]{1,0:T(8,128)(2,1)} %get-tuple-element.153.refs_0_), channel_id=1, source_target_pairs={{0,3},{1,0},{2,1},{3,2},{4,7},{5,4},{6,5},{7,6},{8,11},{9,8},{10,9... | collective-permute-start | bytes 1990664 | tf_op jit(solution)/shard_map/ppermute | solution.py:931
  315.9 42.8 %collective-permute-start.30 = (bf16[288,1152]{1,0:T(8,128)(2,1)}, bf16[288,1152]{1,0:T(8,128)(2,1)S(1)}, u32[]{:S(2)}, u32[]{:S(2)}) collective-permute-start(bf16[288,1152]{1,0:T(8,128)(2,1)} %get-tuple-element.159), channel_id=1, source_target_pairs={{0,2},{1,3},{2,0},{3,1},{4,6},{5,7},{6,4},{7,5},{8,10},{9,11},{10,... | collective-permute-start | bytes 1990664 | tf_op jit(solution)/shard_map/ppermute | solution.py:931
  319.7 40.3 %collective-permute-start.28 = (bf16[768,1152]{1,0:T(8,128)(2,1)}, bf16[768,1152]{1,0:T(8,128)(2,1)}, u32[]{:S(2)}, u32[]{:S(2)}) collective-permute-start(bf16[768,1152]{1,0:T(8,128)(2,1)} %get-tuple-element.157), channel_id=1, source_target_pairs={{0,8},{8,0},{1,9},{9,1},{2,10},{10,2},{3,11},{11,3},{4,12},{12,4},... | collective-permute-start | bytes 5308424 | tf_op jit(solution)/shard_map/ppermute | solution.py:935
  352.6 217.5 %reduce-scatter.5.cloned.1.call-start = ((), (), s32[]{:S(2)}) async-start(), calls=%async_computation.4 | async-start | bytes 2949120 | tf_op jit(solution)/shard_map/reduce_scatter | solution.py:1181
  365.1 23.3 %copy-start.28 = (bf16[384,1152]{1,0:T(8,128)(2,1)S(1)}, bf16[384,1152]{1,0:T(8,128)(2,1)}, u32[]{:S(2)}) copy-start(bf16[384,1152]{1,0:T(8,128)(2,1)} %get-tuple-element.168) | copy-start | bytes 2654212
  365.1 32.9 %copy-start.27 = (bf16[384,1152]{1,0:T(8,128)(2,1)S(1)}, bf16[384,1152]{1,0:T(8,128)(2,1)}, u32[]{:S(2)}) copy-start(bf16[384,1152]{1,0:T(8,128)(2,1)} %get-tuple-element.170) | copy-start | bytes 2654212
  388.3 13.2 %collective-permute-start.31 = (bf16[448,1152]{1,0:T(8,128)(2,1)}, bf16[448,1152]{1,0:T(8,128)(2,1)S(1)}, u32[]{:S(2)}, u32[]{:S(2)}) collective-permute-start(bf16[448,1152]{1,0:T(8,128)(2,1)} %get-tuple-element.163), channel_id=1, source_target_pairs={{0,4},{4,0},{1,5},{5,1},{2,6},{6,2},{3,7},{7,3},{8,12},{12,8},{9,1... | collective-permute-start | bytes 3096584 | tf_op jit(solution)/shard_map/ppermute | solution.py:935
  388.4 30.1 %collective-permute-start.33 = (bf16[384,1152]{1,0:T(8,128)(2,1)S(1)}, bf16[384,1152]{1,0:T(8,128)(2,1)S(1)}, u32[]{:S(2)}, u32[]{:S(2)}) collective-permute-start(bf16[384,1152]{1,0:T(8,128)(2,1)S(1)} %copy-done.28), channel_id=1, source_target_pairs={{0,8},{8,0},{1,9},{9,1},{2,10},{10,2},{3,11},{11,3},{4,12},{12,4},... | collective-permute-start | bytes 2654216 | tf_op jit(solution)/shard_map/ppermute | solution.py:935
  398.0 23.6 %collective-permute-start.34 = (bf16[384,1152]{1,0:T(8,128)(2,1)S(1)}, bf16[384,1152]{1,0:T(8,128)(2,1)}, u32[]{:S(2)}, u32[]{:S(2)}) collective-permute-start(bf16[384,1152]{1,0:T(8,128)(2,1)S(1)} %copy-done.27), channel_id=1, source_target_pairs={{0,16},{16,0},{1,17},{17,1},{2,18},{18,2},{3,19},{19,3},{4,20},{20... | collective-permute-start | bytes 2654216 | tf_op jit(solution)/shard_map/ppermute | solution.py:935
  406.3 34.6 %collective-permute-start.32 = (bf16[224,1152]{1,0:T(8,128)(2,1)}, bf16[224,1152]{1,0:T(8,128)(2,1)}, u32[]{:S(2)}, u32[]{:S(2)}) collective-permute-start(bf16[224,1152]{1,0:T(8,128)(2,1)} %get-tuple-element.165), channel_id=1, source_target_pairs={{0,8},{8,0},{1,9},{9,1},{2,10},{10,2},{3,11},{11,3},{4,12},{12,4},... | collective-permute-start | bytes 1548296 | tf_op jit(solution)/shard_map/ppermute | solution.py:935
  408.8 36.7 %collective-permute-start.39 = (f32[56,1152]{1,0:T(8,128)}, f32[56,1152]{1,0:T(8,128)S(1)}, u32[]{:S(2)}, u32[]{:S(2)}) collective-permute-start(f32[56,1152]{1,0:T(8,128)} %pile.1.refs_4_.refs_0_), channel_id=1, source_target_pairs={{0,2},{1,3},{2,0},{3,1},{4,6},{5,7},{6,4},{7,5},{8,10},{9,11},{10,... | collective-permute-start | bytes 774152 | tf_op jit(solution)/shard_map/ppermute | solution.py:931
  425.1 43.0 %collective-permute-start.36 = (bf16[336,1152]{1,0:T(8,128)(2,1)}, bf16[336,1152]{1,0:T(8,128)(2,1)S(1)}, u32[]{:S(2)}, u32[]{:S(2)}) collective-permute-start(bf16[336,1152]{1,0:T(8,128)(2,1)} %get-tuple-element.175.refs_5_), channel_id=1, source_target_pairs={{0,1},{1,2},{2,3},{3,0},{4,5},{5,6},{6,7},{7,4},{8,9},{9,10},{10,1... | collective-permute-start | bytes 2322440 | tf_op jit(solution)/shard_map/ppermute | solution.py:931
  443.8 24.4 %collective-permute-start.35 = (bf16[112,1152]{1,0:T(8,128)(2,1)}, bf16[112,1152]{1,0:T(8,128)(2,1)S(1)}, u32[]{:S(2)}, u32[]{:S(2)}) collective-permute-start(bf16[112,1152]{1,0:T(8,128)(2,1)} %get-tuple-element.177), channel_id=1, source_target_pairs={{0,16},{16,0},{1,17},{17,1},{2,18},{18,2},{3,19},{19,3},{4,20},{20... | collective-permute-start | bytes 774152 | tf_op jit(solution)/shard_map/ppermute | solution.py:935
  448.1 24.5 %collective-permute-start.43 = (f32[56,1152]{1,0:T(8,128)}, f32[56,1152]{1,0:T(8,128)S(1)}, u32[]{:S(2)}, u32[]{:S(2)}) collective-permute-start(f32[56,1152]{1,0:T(8,128)} %sum.1.refs_8_.refs_1_), channel_id=1, source_target_pairs={{0,1},{1,2},{2,3},{3,0},{4,5},{5,6},{6,7},{7,4},{8,9},{9,10},{10,1... | collective-permute-start | bytes 774152 | tf_op jit(solution)/shard_map/ppermute | solution.py:931
  450.3 17.9 %collective-permute-start.37 = (bf16[48,1152]{1,0:T(8,128)(2,1)S(1)}, bf16[48,1152]{1,0:T(8,128)(2,1)S(1)}, u32[]{:S(2)}, u32[]{:S(2)}) collective-permute-start(bf16[48,1152]{1,0:T(8,128)(2,1)S(1)} %copy-done.46), channel_id=1, source_target_pairs={{0,3},{1,0},{2,1},{3,2},{4,7},{5,4},{6,5},{7,6},{8,11},{9,8},{10,9... | collective-permute-start | bytes 331784 | tf_op jit(solution)/shard_map/ppermute | solution.py:931
  452.0 16.1 %collective-permute-start.38 = (bf16[48,1152]{1,0:T(8,128)(2,1)S(1)}, bf16[48,1152]{1,0:T(8,128)(2,1)S(1)}, u32[]{:S(2)}, u32[]{:S(2)}) collective-permute-start(bf16[48,1152]{1,0:T(8,128)(2,1)S(1)} %copy-done.45), channel_id=1, source_target_pairs={{0,2},{1,3},{2,0},{3,1},{4,6},{5,7},{6,4},{7,5},{8,10},{9,11},{10,... | collective-permute-start | bytes 331784 | tf_op jit(solution)/shard_map/ppermute | solution.py:931
  476.2 1.6 collective-permute-start.44
  480.2 11.2 %collective-permute-start.45 = (f32[2,24,1728]{2,1,0:T(8,128)}, f32[2,24,1728]{2,1,0:T(8,128)}, u32[]{:S(2)}, u32[]{:S(2)}) collective-permute-start(f32[2,24,1728]{2,1,0:T(8,128)} %pair.3.refs_0_), channel_id=1, source_target_pairs={{0,8},{8,0},{1,9},{9,1},{2,10},{10,2},{3,11},{11,3},{4,12},{12,4},... | collective-permute-start | bytes 995336 | tf_op jit(solution)/shard_map/ppermute | solution.py:935
  480.8 32.8 %collective-permute-start.40 = (bf16[448,1152]{1,0:T(8,128)(2,1)}, bf16[448,1152]{1,0:T(8,128)(2,1)}, u32[]{:S(2)}, u32[]{:S(2)}) collective-permute-start(bf16[448,1152]{1,0:T(8,128)(2,1)} %merge.1.refs_1_.refs_6_), channel_id=1, source_target_pairs={{0,8},{8,0},{1,9},{9,1},{2,10},{10,2},{3,11},{11,3},{4,12},{12,4},... | collective-permute-start | bytes 3096584 | tf_op jit(solution)/shard_map/ppermute | solution.py:935
  482.2 31.3 %collective-permute-start.41 = (bf16[448,1152]{1,0:T(8,128)(2,1)}, bf16[448,1152]{1,0:T(8,128)(2,1)}, u32[]{:S(2)}, u32[]{:S(2)}) collective-permute-start(bf16[448,1152]{1,0:T(8,128)(2,1)} %merge.1.refs_1_.refs_6_), channel_id=1, source_target_pairs={{0,16},{16,0},{1,17},{17,1},{2,18},{18,2},{3,19},{19,3},{4,20},{20... | collective-permute-start | bytes 3096584 | tf_op jit(solution)/shard_map/ppermute | solution.py:935
  483.7 52.2 %collective-permute-start.42 = (bf16[448,1152]{1,0:T(8,128)(2,1)}, bf16[448,1152]{1,0:T(8,128)(2,1)}, u32[]{:S(2)}, u32[]{:S(2)}) collective-permute-start(bf16[448,1152]{1,0:T(8,128)(2,1)} %merge.1.refs_1_.refs_6_), channel_id=1, source_target_pairs={{0,24},{8,16},{16,8},{24,0},{1,25},{9,17},{17,9},{25,1},{2,26},{10... | collective-permute-start | bytes 3096584 | tf_op jit(solution)/shard_map/ppermute | solution.py:939
  493.4 50.3 %collective-permute-start.50 = (f32[4,24,1728]{2,1,0:T(8,128)}, f32[4,24,1728]{2,1,0:T(8,128)}, u32[]{:S(2)}, u32[]{:S(2)}) collective-permute-start(f32[4,24,1728]{2,1,0:T(8,128)} %pair.4.refs_5_.refs_0_), channel_id=1, source_target_pairs={{0,16},{16,0},{1,17},{17,1},{2,18},{18,2},{3,19},{19,3},{4,20},{20... | collective-permute-start | bytes 1990664 | tf_op jit(solution)/shard_map/ppermute | solution.py:935
  495.5 5.5 collective-permute-start.46
  500.9 8.1 %collective-permute-start.47 = (f32[8,1152]{1,0:T(8,128)S(1)}, f32[8,1152]{1,0:T(8,128)S(1)}, u32[]{:S(2)}, u32[]{:S(2)}) collective-permute-start(f32[8,1152]{1,0:T(8,128)S(1)} %add.35), channel_id=1, source_target_pairs={{0,1},{1,2},{2,3},{3,0},{4,5},{5,6},{6,7},{7,4},{8,9},{9,10},{10,1... | collective-permute-start | bytes 110600 | tf_op jit(solution)/shard_map/ppermute | solution.py:931
  509.0 26.8 %copy-start.10 = (f32[8,1152]{1,0:T(8,128)}, f32[8,1152]{1,0:T(8,128)S(1)}, u32[]{:S(2)}) copy-start(f32[8,1152]{1,0:T(8,128)S(1)} %add.36.refs_6_) | copy-start | bytes 110596
  509.0 31.9 %copy-start.17 = (bf16[2,4,1152]{2,1,0:T(4,128)(2,1)S(1)}, bf16[2,4,1152]{2,1,0:T(4,128)(2,1)}, u32[]{:S(2)}) copy-start(bf16[2,4,1152]{2,1,0:T(4,128)(2,1)} %param.15) | copy-start | bytes 55300
  540.9 17.0 %collective-permute-start.48 = (bf16[2,576,1152]{2,1,0:T(8,128)(2,1)}, bf16[2,576,1152]{2,1,0:T(8,128)(2,1)S(1)}, u32[]{:S(2)}, u32[]{:S(2)}) collective-permute-start(bf16[2,576,1152]{2,1,0:T(8,128)(2,1)} %get-tuple-element.185.refs_2_.refs_1_), channel_id=1, source_target_pairs={{0,4},{4,0},{1,5},{5,1},{2,6},{6,2},{3,7},{7,3},{8,12},{12,8},{9,1... | collective-permute-start | bytes 7962632 | tf_op jit(solution)/shard_map/ppermute | solution.py:935
  541.6 16.3 %collective-permute-start.49 = (bf16[592,1152]{1,0:T(8,128)(2,1)}, bf16[592,1152]{1,0:T(8,128)(2,1)}, u32[]{:S(2)}, u32[]{:S(2)}) collective-permute-start(bf16[592,1152]{1,0:T(8,128)(2,1)} %get-tuple-element.186.refs_3_), channel_id=1, source_target_pairs={{0,4},{4,0},{1,5},{5,1},{2,6},{6,2},{3,7},{7,3},{8,12},{12,8},{9,1... | collective-permute-start | bytes 4091912 | tf_op jit(solution)/shard_map/ppermute | solution.py:935
  (37 other events, 104.6 us)
Sparse Core Ops, SparseCore 0:
  11.3 111.7 all-gather.1
  352.8 48.2 reduce-scatter.2
  488.0 50.7 reduce-scatter.4

commit v3 on v2

--- a/solution.py
+++ b/solution.py
@@ -286,9 +286,11 @@
                     us[...] = block[0][...]
                     ds[...] = block[1][...]
                     return
-                for j, ref in enumerate(block):
-                    us[j * piece : (j + 1) * piece] = ref[:piece]
-                    ds[j * piece : (j + 1) * piece] = ref[piece:]
+                for j in range(4):
+                    up = block[j]
+                    down = block[-1] if j == 3 else block[j]
+                    us[j * piece : (j + 1) * piece] = up[:piece]
+                    ds[j * piece : (j + 1) * piece] = down[down.shape[0] - piece :]
 
             index += 1
 
@@ -471,7 +473,7 @@
 
 
 def attend_back_kernel(
-    last, count, info_ref, q_ref, k_ref, v_ref, lse_ref, g0, g1, g2, g3, w_ref, hid_ref, tok_ref, *refs
+    micro, last, count, info_ref, q_ref, k_ref, v_ref, lse_ref, g0, g1, g2, g3, w_ref, hid_ref, tok_ref, *refs
 ):
     if last:
         old_ref, refs = refs[0], refs[1:]
@@ -483,7 +485,16 @@
     else:
         sums_ref, bias_ref, wout = refs[:3]
         refs = refs[3:]
-    dos, dqs, dks, dvs, dq_ref, dk_ref, dv_ref, wtmp = refs
+    dos, dqs, dks, dvs, dq_ref, dk_ref, dv_ref, wtmp, w_here, hid_here, tok_here, sems, *old_here = refs
+    copies = [
+        pltpu.make_async_copy(source, here, sems.at[i])
+        for i, (source, here) in enumerate(
+            [(w_ref, w_here), (tok_ref.at[micro], tok_here), (hid_ref.at[micro], hid_here)]
+            + ([(old_ref, old_here[0])] if last else [])
+        )
+    ]
+    for copy in copies:
+        copy.start()
     _, heads, rows, size = q_ref.shape
     share = rows // 4
     local = heads * size
@@ -506,8 +517,8 @@
         probs = jnp.exp2(nt(keys, query) * factor - lse)
         dprobs = nt(values, grad)
         inner = jnp.sum(probs * dprobs, axis=0, keepdims=True)
-        dscores = (probs * (dprobs - inner) * scale).astype(BF)
-        dqs[h, pl.ds(block_of(shift), share), :] = nn(keys_t, dscores).T.astype(BF)
+        dscores = (probs * (dprobs - inner)).astype(BF)
+        dqs[h, pl.ds(block_of(shift), share), :] = (nn(keys_t, dscores) * scale).T.astype(BF)
         return nn(dscores, query), nn(probs.astype(BF), grad)
 
     @pl.when(whole == 1)
@@ -521,7 +532,7 @@
                 more_key, more_value = tile(h, shift, keys, values, keys_t)
                 dkey = dkey + more_key
                 dvalue = dvalue + more_value
-            dks[h] = dkey.astype(BF)
+            dks[h] = (dkey * scale).astype(BF)
             dvs[h] = dvalue.astype(BF)
             return carry
 
@@ -535,7 +546,7 @@
                 keys = k_ref[0, h, span, :]
                 values = v_ref[0, h, span, :]
                 dkey, dvalue = tile(h, shift, keys, values, keys.astype(F32).T.astype(BF))
-                dks[h, span, :] = dkey.astype(BF)
+                dks[h, span, :] = (dkey * scale).astype(BF)
                 dvs[h, span, :] = dvalue.astype(BF)
             return carry
 
@@ -545,11 +556,14 @@
         for h in range(heads):
             dst[:, h * size : (h + 1) * size] = src[h]
 
+    copies[0].wait()
+    copies[1].wait()
+
     def out_rows(i, carry):
         span = pl.ds(pl.multiple_of(i * share, share), share)
-        grad = nn(dq_ref[span, :], w_ref[0]) + nn(dk_ref[span, :], w_ref[1]) + nn(dv_ref[span, :], w_ref[2])
+        grad = nn(dq_ref[span, :], w_here[0]) + nn(dk_ref[span, :], w_here[1]) + nn(dv_ref[span, :], w_here[2])
         part_ref[span, :] = grad.astype(BF)
-        normed, _ = normalize(tok_ref[0, span, :].astype(F32))
+        normed, _ = normalize(tok_here[span, :].astype(F32))
         sums_ref[pl.ds(2 * i, 1), :] = jnp.sum(grad, axis=0, keepdims=True)
         sums_ref[pl.ds(2 * i + 1, 1), :] = jnp.sum(grad * normed, axis=0, keepdims=True)
         return carry
@@ -558,11 +572,13 @@
     bias_ref[...] = jnp.zeros_like(bias_ref)
     bias_ref[0:1, :] = jnp.sum(dq_ref[...].astype(F32), axis=0, keepdims=True)
     bias_ref[1:2, :] = jnp.sum(dv_ref[...].astype(F32), axis=0, keepdims=True)
+    for copy in copies[2:]:
+        copy.wait()
     for which, ref in enumerate((dq_ref, dk_ref, dv_ref)):
         span = slice(which * local, (which + 1) * local)
-        update = tn(ref[...], hid_ref[0])
+        update = tn(ref[...], hid_here[...])
         if last:
-            wtmp[span] = (old_ref[span] + update).astype(BF)
+            wtmp[span] = (old_here[0][span] + update).astype(BF)
         else:
             wout[span] = update
     if last:
@@ -580,8 +596,6 @@
     width = qkv_weight.shape[2]
     last = old is not None
     full = pl.BlockSpec((1, heads, rows, size), lambda i, s: (micro, 0, 0, 0))
-    row = pl.BlockSpec((1, rows, width), lambda i, s: (micro, 0, 0))
-
     def flat(*dims):
         return pl.BlockSpec(dims, lambda i, s: (0,) * len(dims))
 
@@ -591,16 +605,14 @@
     else:
         outs += [((3 * local, width), F32)]
     return pl.pallas_call(
-        functools.partial(attend_back_kernel, last, len(after)),
+        functools.partial(attend_back_kernel, micro, last, len(after)),
         grid_spec=pltpu.PrefetchScalarGridSpec(
             num_scalar_prefetch=1,
             grid=(1,),
             in_specs=[full] * 3
             + [pl.BlockSpec((1, heads, rows), lambda i, s: (micro, 0, 0))]
             + [pl.BlockSpec((1, *grads[0].shape[1:]), lambda i, s: (micro, 0, 0))] * 4
-            + [flat(*qkv_weight.shape), row, row]
-            + ([flat(3 * local, width)] if last else [])
-            + [ANY] * len(after),
+            + [ANY] * (3 + int(last) + len(after)),
             out_specs=[flat(*dims) for dims, _ in outs],
             scratch_shapes=[
                 pltpu.VMEM((heads, 4, share, size), BF),
@@ -611,7 +623,12 @@
                 pltpu.VMEM((rows, local), BF),
                 pltpu.VMEM((rows, local), BF),
                 pltpu.VMEM((3 * local, width), BF),
-            ],
+                pltpu.VMEM(qkv_weight.shape, BF),
+                pltpu.VMEM((rows, width), BF),
+                pltpu.VMEM((rows, width), BF),
+                pltpu.SemaphoreType.DMA((4,)),
+            ]
+            + ([pltpu.VMEM((3 * local, width), F32)] if last else []),
         ),
         out_shape=[shape(dims, dtype) for dims, dtype in outs],
         compiler_params=params(),
@@ -744,23 +761,23 @@
 
 
 def tail_kernel(info, pay_ref, ada_ref, ada_b, out_b, down_b, up_b, qv_b):
-    width = out_b.shape[1]
+    width = out_b.shape[0]
     columns = pay_ref.shape[2]
     half = columns - width
     count = pay_ref.shape[0]
     mods = jnp.concatenate([pay_ref[i, 0:8, :] for i in range(count)], axis=0)
     acts = jnp.concatenate([pay_ref[i, 10:18, :width] for i in range(count)], axis=0)
     ada_ref[...] = tn(mods.astype(BF), acts.astype(BF))
-    ada_b[...] = jnp.sum(mods, axis=0, keepdims=True)
+    ada_b[...] = jnp.sum(mods, axis=0)
     sums = [pay_ref[0, 8:10, :], pay_ref[1, 8:10, :]]
     for i in range(2, count):
         sums[i % 2] = sums[i % 2] + pay_ref[i, 8:10, :]
     total = sums[0] + sums[1]
-    out_b[...] = total[0:1, :width]
-    down_b[...] = total[1:2, :width]
+    out_b[...] = total[0, :width]
+    down_b[...] = total[1, :width]
     low = jnp.where(info[1] == 0, sums[0][0:1, width:], sums[1][0:1, width:])
     high = jnp.where(info[1] == 0, sums[1][0:1, width:], sums[0][0:1, width:])
-    up_b[...] = jnp.concatenate([low, high], axis=1)
+    up_b[...] = jnp.concatenate([low, high], axis=1)[0]
     qv_b[0:1, :] = total[1:2, width : width + half // 2]
     qv_b[1:2, :] = total[1:2, width + half // 2 :]
 
@@ -804,6 +821,12 @@
 def unpack_rows(array):
     columns = array.shape[1] // 4
     return jnp.concatenate([array[:, i * columns : (i + 1) * columns] for i in range(4)], axis=0)
+
+
+def corner_kernel(x_ref, y_ref, up_out, down_out):
+    piece = up_out.shape[1]
+    up_out[...] = x_ref[:, :piece]
+    down_out[...] = y_ref[:, piece:]
 
 
 def plus(a, b):
@@ -926,6 +949,33 @@
     up_out[...] = turned[...].astype(F32).T
 
 
+def spread(info, operands, outs, after):
+    up, down, qkv, out = outs
+    width = up[0]
+    tile = 384 if width % 384 == 0 else width
+    return pl.pallas_call(
+        skipping(spread_kernel, 5, len(after)),
+        grid_spec=pltpu.PrefetchScalarGridSpec(
+            num_scalar_prefetch=1,
+            grid=(width // tile,),
+            in_specs=[pl.BlockSpec((*a.shape[:2], tile), lambda i, s: (0, 0, i)) for a in operands[:2]]
+            + [pl.BlockSpec((a.shape[0], tile), lambda i, s: (0, i)) for a in operands[2:]]
+            + [ANY] * len(after),
+            out_specs=[
+                pl.BlockSpec((tile, up[1]), lambda i, s: (i, 0)),
+                pl.BlockSpec((down[0], tile), lambda i, s: (0, i)),
+                pl.BlockSpec((*qkv[:2], tile), lambda i, s: (0, 0, i)),
+                pl.BlockSpec((out[0], tile), lambda i, s: (0, i)),
+            ],
+            scratch_shapes=[pltpu.VMEM((up[1], tile), BF), pltpu.VMEM((3 * qkv[1], tile), BF)],
+        ),
+        out_shape=[shape(dims, F32) for dims in outs],
+        compiler_params=params(),
+        cost_estimate=cost(6),
+        name="spread",
+    )(info, *operands, *after)
+
+
 def turn(array, shift):
     count = lax.axis_size("tensor")
     return lax.ppermute(array, "tensor", [(i, (i + shift) % count) for i in range(count)])
@@ -1025,25 +1075,39 @@
     own_g = grad_mlp.astype(BF).reshape(micro * share, width)
     other_g = flip(own_g, "core")
 
-    *att, lse = attend(jnp.concatenate([rank[None], whole]), query, key, value, after=(other_g,))
+    (two,) = simple(
+        stack_kernel,
+        [shape((2, 2 * piece, width), BF)],
+        [got[2], got[1]],
+        after=(query,),
+        name="two",
+        micros=0.01,
+    )
+    *att, lse = attend(
+        jnp.concatenate([rank[None], whole]), query, key, value, after=(two, other_g)
+    )
     parts = [att[0], turn(att[1], 1), turn(att[2], 2), turn(att[3], 3)]
-
-    (two,) = simple(
-        stack_kernel, [shape((2, 2 * piece, width), BF)], [got[2], got[1]], after=(lse,), name="two", micros=0.01
-    )
-    two_parts = (two, flip(two, "x"), flip(two, "y"), diagonal(two))
-
-    def release(arrays, after):
+    two_parts = (two, flip(two, "x"), flip(two, "y"))
+
+    def release(arrays, after, micros=3):
         return simple(
-            copy_kernel, [shape(a.shape, a.dtype) for a in arrays], arrays, after=after, name="release"
+            copy_kernel, [shape(a.shape, a.dtype) for a in arrays], arrays, after=after, name="release", micros=micros
         )
 
+    corner = simple(
+        corner_kernel,
+        [shape((2, piece, width), BF)] * 2,
+        two_parts[1:],
+        after=(lse,),
+        name="corner",
+    )
+    two_parts = (*two_parts, flip(corner[0], "y"), flip(corner[1], "x"))
     attn, mid, hidden_two = middle(
-        here, parts, out_full, out_bias[None], tokens, mod_blocks, groups,
+        here, parts, out_full, out_bias[None], tokens, mod_blocks, groups, after=(corner[0],)
     )
     own_x = hidden_two.reshape(micro * share, width)
     other_x = flip(own_x, "core")
-    (third,) = release([got[3]], (mid,) + two_parts[1:])
+    (third,) = release([got[3]], (mid,) + two_parts[3:], 100)
     third_parts = (third, flip(third, "x"), flip(third, "y"), diagonal(third))
     *carry, uk_a, us_a, dk_a, ds_a, bsum_a = feed(
         own_x, other_x, own_g, other_g, [two_parts], bias_a, None
@@ -1109,7 +1173,7 @@
         halve_flat_kernel,
         [half_shape] * 4,
         [u_keep, u_got, d_keep, d_got],
-        after=(lsum_0, t1, t2),
+        after=(lsum_0,),
         name="halve",
     )
     token = (u_keep,)
@@ -1130,18 +1194,10 @@
     def rows_shape(count):
         return shape((count, width), BF)
 
-    rows_all = w_keep.shape[0]
-    keep, send = short(
-        first_kernel,
-        [rows_shape(rows_all // 2)] * 2,
-        [w_keep, w_got],
-        "first",
-        scratch=[pltpu.VMEM((rows_all, width), BF)],
-    )
-    (pile,) = short(
-        pile_kernel, [shape((56, width), F32)], [lsum_0, lsum_1, sums, bsum_a, bsum_b], "pile", (keep,)
-    )
-    pile_got = turn(pile, 2)
+    (tick,) = simple(
+        tick_kernel, [shape((8, 128), F32)], [], after=(lsum_1, t1, t2), name="tick", micros=100
+    )
+
     o_shape = rows_shape(o_room)
     block_shape = rows_shape(2 * piece + o_room)
     t3, o1, o2, t0 = plain(
@@ -1149,13 +1205,27 @@
         [block_shape, o_shape, o_shape, block_shape],
         [u_keep, u_got, d_keep, d_got],
         "last",
-        (pile, t1, t2),
+        (tick,),
+        micros=60,
     )
     token = (t3,)
     t3 = turn(t3, -3)
     o1 = turn(o1, -1)
     o2 = turn(o2, -2)
-    tokens_grad = finish(here, 0, share_0, tokens, mod_blocks, grad_mid, groups, after=token)
+    rows_all = w_keep.shape[0]
+    keep, send = short(
+        first_kernel,
+        [rows_shape(rows_all // 2)] * 2,
+        [w_keep, w_got],
+        "first",
+        token,
+        [pltpu.VMEM((rows_all, width), BF)],
+    )
+    (pile,) = short(
+        pile_kernel, [shape((56, width), F32)], [lsum_0, lsum_1, sums, bsum_a, bsum_b], "pile", (keep,)
+    )
+    pile_got = turn(pile, 2)
+    tokens_grad = finish(here, 0, share_0, tokens, mod_blocks, grad_mid, groups, after=(*token, pile))
     keep, send = short(
         second_kernel,
         [rows_shape(rows_all // 4)] * 2,
@@ -1165,18 +1235,19 @@
         [pltpu.VMEM((rows_all // 2, width), BF)],
     )
     send_got = flip(send, "y")
-    (pile,) = plain(
-        sum_kernel, [shape(pile.shape, F32)], [pile, pile_got], "sum", (keep,), micros=40
-    )
-    pile_far = turn(pile, 1)
+    (tick,) = plain(tick_kernel, [shape((8, 128), F32)], [], "tick", (keep, o1, o2), micros=60)
     (merged,) = plain(
         merge_kernel,
         [rows_shape(rows_all // 4 + 2 * piece + o_room)],
         [keep, send_got, t0, t1, t2, t3, o1, o2],
         "merge",
-        (pile,),
+        (tick,),
         micros=0.1,
     )
+    (pile,) = plain(
+        sum_kernel, [shape(pile.shape, F32)], [pile, pile_got], "sum", (merged,), micros=30
+    )
+    pile_far = turn(pile, 1)
     (part_1,) = release([part_1], (merged,))
     share_1 = lax.psum_scatter(part_1, "tensor", scatter_dimension=0, tiled=True)
     merged = over_rest(merged)
@@ -1188,7 +1259,7 @@
         "slots",
         (merged,),
         [pltpu.VMEM((micro * slots, 6 * width), F32)],
-        micros=40,
+        micros=0.1,
     )
     pay_got = flip(pay, "core")
     cond_part = jnp.dot(mod_low, ada_turned, preferred_element_type=F32)
@@ -1203,7 +1274,7 @@
 
     def pair(mine, got, after=()):
         outs = [shape((2 * mine.shape[0], *mine.shape[1:]), F32)]
-        return plain(pair_kernel, outs, [mine, got], "pair", after, micros=20)[0]
+        return plain(pair_kernel, outs, [mine, got], "pair", after, micros=0.1)[0]
 
     pays = pair(pay[None], pay_got[None])
     pays = pair(pays, flip(pays, "x"))
@@ -1219,58 +1290,50 @@
     )
     halves_got = flip(halves, "core")
     others_got = flip(others, "core")
-    pays = pair(pays, pays_got, (halves,))
+    tokens_grad = finish(
+        here, 1, share_1, tokens, mod_blocks, grad_mid, groups, tokens_grad, after=(halves,)
+    )
+    up_weight_grad, down_weight_grad, qkv_weight_grad, out_weight_grad = spread(
+        info,
+        [halves, halves_got, others, others_got],
+        [up_weight.shape, down_weight.shape, qkv_turned.shape, out_weight.shape],
+        (tokens_grad,),
+    )
+    pays = pair(pays, pays_got, (up_weight_grad,))
     if lax.axis_size("rest") > 1:
         pays = lax.all_gather(pays, "rest", axis=0, tiled=True)
     ada_weight_grad, ada_b, out_b, down_b, up_b, qv_bias_grad = short(
         tail_kernel,
         [
             shape(ada_turned.shape, F32),
-            shape((1, columns), F32),
-            shape((1, width), F32),
-            shape((1, width), F32),
-            shape((1, part), F32),
+            shape((columns,), F32),
+            shape((width,), F32),
+            shape((width,), F32),
+            shape((part,), F32),
             shape(qv_bias.shape, F32),
         ],
         [pays],
         "tail",
     )
-    up_weight_grad, down_weight_grad, qkv_weight_grad, out_weight_grad = short(
-        spread_kernel,
-        [
-            shape(up_weight.shape, F32),
-            shape(down_weight.shape, F32),
-            shape(qkv_turned.shape, F32),
-            shape(out_weight.shape, F32),
-        ],
-        [halves, halves_got, others, others_got],
-        "spread",
-        (ada_weight_grad,),
-        [pltpu.VMEM((part, width), BF), pltpu.VMEM((3 * local_width, width), BF)],
-    )
     cond_float = conditioning.astype(F32)
     sigmoid = jax.nn.sigmoid(cond_float)
     conditioning_grad = cond_grad.reshape(micro, slots, width) * (
         sigmoid * (1.0 + cond_float * (1.0 - sigmoid))
     )
-    tokens_grad = finish(
-        here, 1, share_1, tokens, mod_blocks, grad_mid, groups, tokens_grad, after=(up_weight_grad,)
-    )
-
     return (
         layer_out,
         tokens_grad,
         conditioning_grad,
         ada_weight_grad.T,
-        ada_b[0],
+        ada_b,
         qkv_weight_grad.transpose(0, 2, 1),
         qv_bias_grad,
         out_weight_grad,
-        out_b[0],
+        out_b,
         up_weight_grad,
-        up_b[0],
+        up_b,
         down_weight_grad,
-        down_b[0],
+        down_b,
     )
 
 

time: 591 us -> 532 us (0.900)
  waiting for transfers between devices: 168 us -> 118 us
  starting transfers between devices: 83.3 us -> 68.5 us
  Pallas kernels: 279 us -> 290 us
    ppermute x3 -> x2, waiting for transfers between devices: 24.2 us -> 0.01 us  [diagonal(): return lax.ppermute(array, ('y', 'x'), [(0, 3), (1, 2), (2, 1), (3, 0)])]
    ppermute x21, starting transfers between devices: 47.9 us -> 28.7 us  [turn(): lax.ppermute(array, 'tensor', [(i, (i + shift) % count) for i in range(co...]
    ppermute x21, waiting for transfers between devices: 106 us -> 89.3 us  [turn(): lax.ppermute(array, 'tensor', [(i, (i + shift) % count) for i in range(co...]
    pallas_call x2 -> x3, Pallas kernels: 55.5 us -> 69.6 us  [the longest x2 60 us: attend_back(): pl.pallas_call(functools.partial(attend_back_kernel, micro, last, len(aft...]
    ppermute x27 -> x29, waiting for transfers between devices: 37.4 us -> 23.7 us  [flip(): return lax.ppermute(array, axis, [(0, 1), (1, 0)])]
    pallas_call x24 -> x26, Pallas kernels: 90.5 us -> 84.6 us  [simple(): pl.pallas_call(body, grid_spec=pltpu.PrefetchScalarGridSpec(num_scalar_pr...]
    unnamed x95 -> x83, local copies, waits for them, and re-layouts: 14.7 us -> 17.5 us
    ppermute x27 -> x29, starting transfers between devices: 31.7 us -> 34.5 us  [flip(): return lax.ppermute(array, axis, [(0, 1), (1, 0)])]
  transfers between devices with their start and end apart: 54 -> 55, of which waited for: 25 -> 19; matrix products, arithmetic and copies ran while one was open for 4% -> 3% of each run, Pallas kernels for 46% -> 53%
where the time goes in v3:
time: 532 us; the launch traced here: 527 us
  Pallas kernels  290 us (55%)
  waiting for transfers between devices  118 us (22%)
  starting transfers between devices  68.5 us (13%)
  local copies, waits for them, and re-layouts  25.5 us (5%)
  between operations  14.4 us (3%)
  other arithmetic  9.24 us (2%)
    ppermute x21, waiting for transfers between devices, turn(): lax.ppermute(array, 'tensor', [(i, (i + shift) % count) for i in range(co...  89.3 us
    pallas_call x26, Pallas kernels, simple(): pl.pallas_call(body, grid_spec=pltpu.PrefetchScalarGridSpec(num_scalar_pr...  84.6 us
    pallas_call x2, Pallas kernels, feed(): pl.pallas_call(functools.partial(feed_kernel, first, tuple((len(p) for p...  68.1 us
    pallas_call x2, Pallas kernels, attend_back(): pl.pallas_call(functools.partial(attend_back_kernel, micro, last, len(aft...  60 us
    ppermute x29, starting transfers between devices, flip(): return lax.ppermute(array, axis, [(0, 1), (1, 0)])  34.5 us
    ppermute x21, starting transfers between devices, turn(): lax.ppermute(array, 'tensor', [(i, (i + shift) % count) for i in range(co...  28.7 us
    ppermute x29, waiting for transfers between devices, flip(): return lax.ppermute(array, axis, [(0, 1), (1, 0)])  23.7 us
    pallas_call x1, Pallas kernels, attend(): pl.pallas_call(skipping(attend_kernel, 4, len(after)), grid_spec=pltpu.Pr...  20.3 us
  transfers between devices with their start and end apart: 55, of which 19 were waited for; matrix products, arithmetic and copies ran while one was open for 3% of the time, Pallas kernels for 53%

profile of v3, /device:TPU:10, one launch (start us, length us, event | category | flops | bytes accessed | tf_op | source)
XLA Modules:
  0.0 527.0 jit_solution(9568737409790326479)
XLA Ops:
  14.8 4.6 ada.1
  19.4 1.6 collective-permute-start
  22.2 1.8 collective-permute-start.2
  24.0 5.9 %pack.1 = (bf16[576,1152]{1,0:T(8,128)(2,1)}, bf16[576,1152]{1,0:T(8,128)(2,1)}, bf16[288,1152]{1,0:T(8,128)(2,1)}) custom-call(s32[11]{0:T(128)} %pad_add_fusion.3.refs_0_, bf16[1152,1152]{1,0:T(8,128)(2,1)} %refs_1_.1, bf16[1152,1152]{1,0:T(8,128)(2,1)} %refs_2_.3, bf16[8,1152]{1,0:T(8,128)(2,1)} %get-tuple-element.108.refs_3_.refs_5_), custom_call_target="tpu_custom_call" | custom-call | flops 11500000 | bytes 1000 | tf_op jit(solution)/shard_map/pack/pallas_call | solution.py:69
  30.2 2.5 collective-permute-start.4
  33.6 15.4 %collective-permute-done.1.refs_3_ = f32[16,1728]{1,0:T(8,128)S(1)} collective-permute-done((f32[16,1728]{1,0:T(8,128)}, f32[16,1728]{1,0:T(8,128)S(1)}, u32[]{:S(2)}, u32[]{:S(2)}) %collective-permute-start.1) | collective-permute-done | bytes 110624 | tf_op jit(solution)/shard_map/ppermute | solution.py:981
  49.1 15.6 %collective-permute-done.2.refs_4_ = f32[16,1728]{1,0:T(8,128)S(1)} collective-permute-done((f32[16,1728]{1,0:T(8,128)}, f32[16,1728]{1,0:T(8,128)S(1)}, u32[]{:S(2)}, u32[]{:S(2)}) %collective-permute-start.2) | collective-permute-done | bytes 110624 | tf_op jit(solution)/shard_map/ppermute | solution.py:981
  65.3 2.9 modulate.1
  69.1 12.9 %project.1 = (bf16[2,1024,1152]{2,1,0:T(8,128)(2,1)}, bf16[2,4,1024,72]{3,2,1,0:T(8,128)(2,1)}, bf16[2,4,1024,72]{3,2,1,0:T(8,128)(2,1)}, bf16[2,4,1024,72]{3,2,1,0:T(8,128)(2,1)}) custom-call(bf16[2,1024,1152]{2,1,0:T(8,128)(2,1)} %refs_2_.5, f32[8,6,1152]{2,1,0:T(8,128)} %get-tuple-element.110.mod_ref.refs_8_.refs_3_, bf16[864,1152]{1,0:T(8,128)(2,1)} %bitcast.25, ...), custom_call_target="tpu_custom_call" | custom-call | flops 11500000 | bytes 1000 | tf_op jit(solution)/shard_map/project/pallas_call | solution.py:123
  82.1 2.2 collective-permute-done.4.refs_1_
  85.2 2.5 two.1.refs_4_
  87.7 1.6 collective-permute-start.10
  91.3 3.5 collective-permute-start.12
  102.0 20.3 %attend.1 = (bf16[2,64,1152]{2,1,0:T(8,128)(2,1)}, bf16[2,64,1152]{2,1,0:T(8,128)(2,1)}, bf16[2,64,1152]{2,1,0:T(8,128)(2,1)}, bf16[2,64,1152]{2,1,0:T(8,128)(2,1)}, f32[2,4,1024]{2,1,0:T(4,128)}) custom-call(s32[3]{0:T(128)} %pad_add_fusion.2.refs_0_, bf16[2,4,1024,72]{3,2,1,0:T(8,128)(2,1)} %get-tuple-element.111.refs_2_.refs_1_.q_ref, ...), custom_call_target="tpu_custom_call" | custom-call | flops 11500000 | bytes 1000 | tf_op jit(solution)/shard_map/attend/pallas_call | solution.py:185
  122.8 2.4 collective-permute-start.7
  126.6 2.8 corner.1
  130.0 2.8 collective-permute-done.6.refs_2_.refs_12_
  132.8 16.1 %collective-permute-done.7.refs_3_.refs_13_ = bf16[2,64,1152]{2,1,0:T(8,128)(2,1)S(1)} collective-permute-done((bf16[2,64,1152]{2,1,0:T(8,128)(2,1)}, bf16[2,64,1152]{2,1,0:T(8,128)(2,1)S(1)}, u32[]{:S(2)}, u32[]{:S(2)}) %collective-permute-start.7) | collective-permute-done | bytes 294944 | tf_op jit(solution)/shard_map/ppermute | solution.py:981
  148.9 2.8 collective-permute-done.8.refs_4_.refs_14_
  152.4 8.0 %middle.1 = (f32[2,256,1152]{2,1,0:T(8,128)}, f32[2,256,1152]{2,1,0:T(8,128)}, bf16[2,256,1152]{2,1,0:T(8,128)(2,1)}) custom-call(s32[3]{0:T(128)} %pad_add_fusion.1.refs_0_, bf16[2,64,1152]{2,1,0:T(8,128)(2,1)} %get-tuple-element.114.refs_1_.refs_11_, bf16[2,64,1152]{2,1,0:T(8,128)(2,1)} %copy-done.36, bf16[2,64,1152]{2,1,0:T(8,128)(2,1)} %copy-done.37, ...), custom_call_target="tpu_custom_call" | custom-call | flops 9200000000 | bytes 800000 | tf_op jit(solution)/shard_map/middle/pallas_call | solution.py:217
  161.6 2.0 release.2.refs_4_
  163.6 3.5 collective-permute-start.17
  168.1 32.5 %feed.2 = (f32[512,1152]{1,0:T(8,128)}, f32[512,1152]{1,0:T(8,128)}, f32[512,1152]{1,0:T(8,128)}, f32[512,1152]{1,0:T(8,128)}, bf16[2,2,144,1152]{3,2,1,0:T(8,12...) custom-call(bf16[512,1152]{1,0:T(8,128)(2,1)} %bitcast.37, ...), custom_call_target="tpu_custom_call" | custom-call | flops 39099998208 | bytes 3400000 | tf_op jit(solution)/shard_map/feed/pallas_call | solution.py:354
  202.0 35.6 %feed.3 = (f32[512,1152]{1,0:T(8,128)}, f32[512,1152]{1,0:T(8,128)}, f32[512,1152]{1,0:T(8,128)}, f32[512,1152]{1,0:T(8,128)}, bf16[2,2,144,1152]{3,2,1,0:T(8,12...) custom-call(bf16[512,1152]{1,0:T(8,128)(2,1)} %bitcast.38, ...), custom_call_target="tpu_custom_call" | custom-call | flops 39099998208 | bytes 3400000 | tf_op jit(solution)/shard_map/feed/pallas_call | solution.py:354
  239.3 4.2 halve.2
  245.1 1.9 collective-permute-start.26
  248.5 18.0 %between.1 = (bf16[2,256,1152]{2,1,0:T(8,128)(2,1)}, f32[2,256,1152]{2,1,0:T(8,128)}, bf16[2,64,1152]{2,1,0:T(8,128)(2,1)}, bf16[2,64,1152]{2,1,0:T(8,128)(2,1)}...) custom-call(s32[4]{0:T(128)} %pad_add_fusion.refs_0_, ...), custom_call_target="tpu_custom_call" | custom-call | flops 20700000256 | bytes 1800000 | tf_op jit(solution)/shard_map/between/pallas_call | solution.py:434
  267.7 2.4 collective-permute-start.24
  272.7 7.7 %mix.1 = (bf16[768,1152]{1,0:T(8,128)(2,1)}, bf16[768,1152]{1,0:T(8,128)(2,1)}, bf16[768,1152]{1,0:T(8,128)(2,1)}, bf16[768,1152]{1,0:T(8,128)(2,1)}) custom-call(s32[11]{0:T(128)} %pad_add_fusion.3.refs_0_, bf16[2,2,144,1152]{3,2,1,0:T(8,128)(2,1)} %get-tuple-element.150.refs_1_, bf16[2,2,144,1152]{3,2,1,0:T(8,128)(2,1)} %get-tuple-element.151.refs_2_, ...), custom_call_target="tpu_custom_call" | custom-call | flops 3449999872 | bytes 300000 | tf_op jit(solution)/shard_map/mix/pallas_call | solution.py:69
  282.0 7.3 %collective-permute-done.22.refs_5_.g1 = bf16[2,64,1152]{2,1,0:T(8,128)(2,1)S(1)} collective-permute-done((bf16[2,64,1152]{2,1,0:T(8,128)(2,1)}, bf16[2,64,1152]{2,1,0:T(8,128)(2,1)S(1)}, u32[]{:S(2)}, u32[]{:S(2)}) %collective-permute-start.22) | collective-permute-done | bytes 294944 | tf_op jit(solution)/shard_map/ppermute | solution.py:981
  289.3 4.3 collective-permute-done.24.refs_7_.g3
  293.6 2.9 quarter.1
  296.5 3.7 collective-permute-start.33
  300.5 30.5 %attend_back.2 = (bf16[1024,1152]{1,0:T(8,128)(2,1)}, f32[8,1152]{1,0:T(8,128)}, f32[8,288]{1,0:T(8,128)}, f32[864,1152]{1,0:T(8,128)}) custom-call(s32[3]{0:T(128)} %add_add_fusion.1.info_ref, bf16[2,4,1024,72]{3,2,1,0:T(8,128)(2,1)} %get-tuple-element.111.refs_2_.refs_1_.q_ref, bf16[2,4,1024,72]{3,2,1,0:T(8,128)(2,1)} %get-tuple-element.112.refs_2_.k_ref, ...), custom_call_target="tpu_custom_call" | custom-call | flops 34500001792 | bytes 3000000 | tf_op jit(solution)/shard_map/attend_back/pallas_call | solution.py:607
  332.2 5.1 halve.3
  337.3 29.5 %attend_back.3 = (bf16[1024,1152]{1,0:T(8,128)(2,1)}, f32[8,1152]{1,0:T(8,128)}, f32[8,288]{1,0:T(8,128)}, bf16[448,1152]{1,0:T(8,128)(2,1)}, bf16[448,1152]{1,0:T(8,128)(2,1)}) custom-call(s32[3]{0:T(128)} %add_add_fusion.info_ref, bf16[2,4,1024,72]{3,2,1,0:T(8,128)(2,1)} %get-tuple-element.111.refs_2_.refs_1_.q_ref, ...), custom_call_target="tpu_custom_call" | custom-call | flops 34500001792 | bytes 3000000 | tf_op jit(solution)/shard_map/attend_back/pallas_call | solution.py:607
  368.6 3.5 last.1
  372.2 2.6 collective-permute-start.39
  374.9 3.1 collective-permute-start.37
  377.9 3.7 first.1
  382.4 2.4 pile.1.refs_6_.refs_0_
  385.7 5.1 reduce-scatter.3.cloned.1.call-done.refs_1_
  390.8 4.1 finish.2.refs_3_.refs_5_
  396.0 2.9 second.1
  398.9 20.7 %collective-permute-start.36 = (bf16[112,1152]{1,0:T(8,128)(2,1)}, bf16[112,1152]{1,0:T(8,128)(2,1)S(1)}, u32[]{:S(2)}, u32[]{:S(2)}) collective-permute-start(bf16[112,1152]{1,0:T(8,128)(2,1)} %get-tuple-element.181), channel_id=1, source_target_pairs={{0,16},{16,0},{1,17},{17,1},{2,18},{18,2},{3,19},{19,3},{4,20},{20... | collective-permute-start | bytes 774152 | tf_op jit(solution)/shard_map/ppermute | solution.py:985
  420.9 5.4 %collective-permute-done.36.refs_1_ = bf16[112,1152]{1,0:T(8,128)(2,1)S(1)} collective-permute-done((bf16[112,1152]{1,0:T(8,128)(2,1)}, bf16[112,1152]{1,0:T(8,128)(2,1)S(1)}, u32[]{:S(2)}, u32[]{:S(2)}) %collective-permute-start.36) | collective-permute-done | bytes 258080 | tf_op jit(solution)/shard_map/ppermute | solution.py:985
  427.0 3.4 merge.1.refs_1_.refs_2_.refs_6_
  430.4 1.7 collective-permute-start.41
  432.1 1.7 collective-permute-start.42
  433.8 3.2 release.3
  437.1 1.9 sum.1.refs_1_
  439.1 12.1 %collective-permute-done.44.refs_2_ = f32[56,1152]{1,0:T(8,128)} collective-permute-done((f32[56,1152]{1,0:T(8,128)}, f32[56,1152]{1,0:T(8,128)}, u32[]{:S(2)}, u32[]{:S(2)}) %collective-permute-start.44) | collective-permute-done | bytes 258080 | tf_op jit(solution)/shard_map/ppermute | solution.py:981
  451.2 2.9 slots.1
  454.1 1.7 collective-permute-done.45
  455.8 1.8 pair.3.refs_0_
  459.2 5.7 %collective-permute-done.47 = f32[8,1152]{1,0:T(8,128)S(1)} collective-permute-done((f32[8,1152]{1,0:T(8,128)S(1)}, f32[8,1152]{1,0:T(8,128)S(1)}, u32[]{:S(2)}, u32[]{:S(2)}) %collective-permute-start.47) | collective-permute-done | bytes 36896 | tf_op jit(solution)/shard_map/ppermute | solution.py:981
  465.0 4.9 collective-permute-done.48
  470.5 13.9 %collective-permute-done.46.refs_1_ = f32[2,24,1728]{2,1,0:T(8,128)} collective-permute-done((f32[2,24,1728]{2,1,0:T(8,128)}, f32[2,24,1728]{2,1,0:T(8,128)}, u32[]{:S(2)}, u32[]{:S(2)}) %collective-permute-start.46) | collective-permute-done | bytes 331808 | tf_op jit(solution)/shard_map/ppermute | solution.py:985
  484.5 2.0 pair.4.refs_5_.refs_0_
  486.5 5.2 order.1
  494.3 4.1 finish.3.refs_5_
  499.5 9.7 %spread.1 = (f32[1152,1152]{1,0:T(8,128)}, f32[1152,1152]{1,0:T(8,128)}, f32[3,288,1152]{2,1,0:T(8,128)}, f32[288,1152]{1,0:T(8,128)}) custom-call(s32[11]{0:T(128)} %pad_add_fusion.3.refs_0_, bf16[2,576,1152]{2,1,0:T(8,128)(2,1)} %get-tuple-element.189.refs_6_.refs_1_, bf16[2,576,1152]{2,1,0:T(8,128)(2,1)} %collective-permute-done.50.refs_2_, ...), custom_call_target="tpu_custom_call" | custom-call | flops 6899999744 | bytes 600000 | tf_op jit(solution)/shard_map/spread/pallas_call | solution.py:956
  511.1 2.5 pair.5.refs_1_
  513.6 6.6 %tail.1 = (f32[1728,1152]{1,0:T(8,128)}, f32[1728]{0:T(1024)}, f32[1152]{0:T(1024)}, f32[1152]{0:T(1024)}, f32[1152]{0:T(1024)}, /*index=5*/f32[2,288]{1,0:T(2,128)}) custom-call(s32[11]{0:T(128)} %pad_add_fusion.3.refs_0_, f32[8,24,1728]{2,1,0:T(8,128)} %pair.5.refs_1_), custom_call_target="tpu_custom_call" | custom-call | flops 3449999872 | bytes 300000 | tf_op jit(solution)/shard_map/tail/pallas_call | solution.py:69
  (201 shorter events, 54.3 us)
Async XLA Ops:
  7.2 144.5 %all-gather.2.cloned.1.call-start = ((), (), s32[]{:S(2)}) async-start(), calls=%async_computation.2 | async-start | bytes 2820096 | tf_op jit(solution)/shard_map/all_gather | solution.py:1052
  9.0 381.9 %reduce-scatter.3.cloned.1.call-start = ((), (), s32[]{:S(2)}) async-start(), calls=%async_computation.3 | async-start | bytes 2949120 | tf_op jit(solution)/shard_map/reduce_scatter | solution.py:1170
  19.4 14.2 %collective-permute-start = (f32[16,1728]{1,0:T(8,128)}, f32[16,1728]{1,0:T(8,128)S(1)}, u32[]{:S(2)}, u32[]{:S(2)}) collective-permute-start(f32[16,1728]{1,0:T(8,128)} %get-tuple-element.107.refs_1_), channel_id=1, source_target_pairs={{0,1},{1,2},{2,3},{3,0},{4,5},{5,6},{6,7},{7,4},{8,9},{9,10},{10,1... | collective-permute-start | bytes 331784 | tf_op jit(solution)/shard_map/ppermute | solution.py:981
  20.9 28.1 %collective-permute-start.1 = (f32[16,1728]{1,0:T(8,128)}, f32[16,1728]{1,0:T(8,128)S(1)}, u32[]{:S(2)}, u32[]{:S(2)}) collective-permute-start(f32[16,1728]{1,0:T(8,128)} %get-tuple-element.107.refs_1_), channel_id=1, source_target_pairs={{0,2},{1,3},{2,0},{3,1},{4,6},{5,7},{6,4},{7,5},{8,10},{9,11},{10,... | collective-permute-start | bytes 331784 | tf_op jit(solution)/shard_map/ppermute | solution.py:981
  22.2 42.5 %collective-permute-start.2 = (f32[16,1728]{1,0:T(8,128)}, f32[16,1728]{1,0:T(8,128)S(1)}, u32[]{:S(2)}, u32[]{:S(2)}) collective-permute-start(f32[16,1728]{1,0:T(8,128)} %get-tuple-element.107.refs_1_), channel_id=1, source_target_pairs={{0,3},{1,0},{2,1},{3,2},{4,7},{5,4},{6,5},{7,6},{8,11},{9,8},{10,9... | collective-permute-start | bytes 331784 | tf_op jit(solution)/shard_map/ppermute | solution.py:981
  24.0 8.7 %copy-start.23 = (f32[2,288]{1,0:T(2,128)S(1)}, f32[2,288]{1,0:T(2,128)}, u32[]{:S(2)}) copy-start(f32[2,288]{1,0:T(2,128)} %param.21) | copy-start | bytes 6916
  29.9 52.2 %collective-permute-start.3 = (bf16[288,1152]{1,0:T(8,128)(2,1)}, bf16[288,1152]{1,0:T(8,128)(2,1)S(1)}, u32[]{:S(2)}, u32[]{:S(2)}) collective-permute-start(bf16[288,1152]{1,0:T(8,128)(2,1)} %get-tuple-element.109.refs_5_), channel_id=1, source_target_pairs={{0,2},{1,3},{2,0},{3,1},{4,6},{5,7},{6,4},{7,5},{8,10},{9,11},{10,... | collective-permute-start | bytes 1990664 | tf_op jit(solution)/shard_map/ppermute | solution.py:981
  30.2 54.2 %collective-permute-start.4 = (bf16[288,1152]{1,0:T(8,128)(2,1)}, bf16[288,1152]{1,0:T(8,128)(2,1)S(1)}, u32[]{:S(2)}, u32[]{:S(2)}) collective-permute-start(bf16[288,1152]{1,0:T(8,128)(2,1)} %get-tuple-element.109.refs_5_), channel_id=1, source_target_pairs={{0,1},{1,2},{2,3},{3,0},{4,5},{5,6},{6,7},{7,4},{8,9},{9,10},{10,1... | collective-permute-start | bytes 1990664 | tf_op jit(solution)/shard_map/ppermute | solution.py:981
  33.6 31.1 %copy-start.15 = (f32[16,1728]{1,0:T(8,128)}, f32[16,1728]{1,0:T(8,128)S(1)}, u32[]{:S(2)}) copy-start(f32[16,1728]{1,0:T(8,128)S(1)} %collective-permute-done.refs_2_) | copy-start | bytes 331780
  49.1 15.6 %copy-start.16 = (f32[16,1728]{1,0:T(8,128)}, f32[16,1728]{1,0:T(8,128)S(1)}, u32[]{:S(2)}) copy-start(f32[16,1728]{1,0:T(8,128)S(1)} %collective-permute-done.1.refs_3_) | copy-start | bytes 331780
  87.7 7.2 %copy-start.21 = (f32[1152]{0:T(1024)S(1)}, f32[1152]{0:T(1024)}, u32[]{:S(2)}) copy-start(f32[1152]{0:T(1024)} %param.23) | copy-start | bytes 13828
  87.7 7.8 %copy-start.22 = (f32[1152]{0:T(1024)S(1)}, f32[1152]{0:T(1024)}, u32[]{:S(2)}) copy-start(f32[1152]{0:T(1024)} %param.27) | copy-start | bytes 13828
  87.7 38.4 %collective-permute-start.10 = (bf16[2,288,1152]{2,1,0:T(8,128)(2,1)}, bf16[2,288,1152]{2,1,0:T(8,128)(2,1)}, u32[]{:S(2)}, u32[]{:S(2)}) collective-permute-start(bf16[2,288,1152]{2,1,0:T(8,128)(2,1)} %two.1.refs_4_), channel_id=1, source_target_pairs={{0,16},{16,0},{1,17},{17,1},{2,18},{18,2},{3,19},{19,3},{4,20},{20... | collective-permute-start | bytes 3981320 | tf_op jit(solution)/shard_map/ppermute | solution.py:985
  89.3 37.3 %collective-permute-start.9 = (bf16[2,288,1152]{2,1,0:T(8,128)(2,1)}, bf16[2,288,1152]{2,1,0:T(8,128)(2,1)}, u32[]{:S(2)}, u32[]{:S(2)}) collective-permute-start(bf16[2,288,1152]{2,1,0:T(8,128)(2,1)} %two.1.refs_4_), channel_id=1, source_target_pairs={{0,8},{8,0},{1,9},{9,1},{2,10},{10,2},{3,11},{11,3},{4,12},{12,4},... | collective-permute-start | bytes 3981320 | tf_op jit(solution)/shard_map/ppermute | solution.py:985
  91.2 38.2 %copy-start.5 = (bf16[2,256,1152]{2,1,0:T(8,128)(2,1)}, bf16[2,256,1152]{2,1,0:T(8,128)(2,1)S(1)}, u32[]{:S(2)}) copy-start(bf16[2,256,1152]{2,1,0:T(8,128)(2,1)S(1)} %multiply_convert_fusion) | copy-start | bytes 3538948
  91.3 9.7 %collective-permute-start.5 = (bf16[512,1152]{1,0:T(8,128)(2,1)S(1)}, bf16[512,1152]{1,0:T(8,128)(2,1)S(1)}, u32[]{:S(2)}, u32[]{:S(2)}) collective-permute-start(bf16[512,1152]{1,0:T(8,128)(2,1)S(1)} %bitcast.29), channel_id=1, source_target_pairs={{0,4},{4,0},{1,5},{5,1},{2,6},{6,2},{3,7},{7,3},{8,12},{12,8},{9,1... | collective-permute-start | bytes 3538952 | tf_op jit(solution)/shard_map/ppermute | solution.py:985
  91.3 69.1 %collective-permute-start.12 = (bf16[288,1152]{1,0:T(8,128)(2,1)S(1)}, bf16[288,1152]{1,0:T(8,128)(2,1)}, u32[]{:S(2)}, u32[]{:S(2)}) collective-permute-start(bf16[288,1152]{1,0:T(8,128)(2,1)S(1)} %copy-done.10), channel_id=1, source_target_pairs={{0,3},{1,0},{2,1},{3,2},{4,7},{5,4},{6,5},{7,6},{8,11},{9,8},{10,9... | collective-permute-start | bytes 1990664 | tf_op jit(solution)/shard_map/ppermute | solution.py:981
  122.3 10.5 %collective-permute-start.6 = (bf16[2,64,1152]{2,1,0:T(8,128)(2,1)}, bf16[2,64,1152]{2,1,0:T(8,128)(2,1)S(1)}, u32[]{:S(2)}, u32[]{:S(2)}) collective-permute-start(bf16[2,64,1152]{2,1,0:T(8,128)(2,1)} %get-tuple-element.115), channel_id=1, source_target_pairs={{0,1},{1,2},{2,3},{3,0},{4,5},{5,6},{6,7},{7,4},{8,9},{9,10},{10,1... | collective-permute-start | bytes 884744 | tf_op jit(solution)/shard_map/ppermute | solution.py:981
  122.8 26.1 %collective-permute-start.7 = (bf16[2,64,1152]{2,1,0:T(8,128)(2,1)}, bf16[2,64,1152]{2,1,0:T(8,128)(2,1)S(1)}, u32[]{:S(2)}, u32[]{:S(2)}) collective-permute-start(bf16[2,64,1152]{2,1,0:T(8,128)(2,1)} %get-tuple-element.116), channel_id=1, source_target_pairs={{0,2},{1,3},{2,0},{3,1},{4,6},{5,7},{6,4},{7,5},{8,10},{9,11},{10,... | collective-permute-start | bytes 884744 | tf_op jit(solution)/shard_map/ppermute | solution.py:981
  126.0 25.6 %collective-permute-start.8 = (bf16[2,64,1152]{2,1,0:T(8,128)(2,1)}, bf16[2,64,1152]{2,1,0:T(8,128)(2,1)S(1)}, u32[]{:S(2)}, u32[]{:S(2)}) collective-permute-start(bf16[2,64,1152]{2,1,0:T(8,128)(2,1)} %get-tuple-element.117), channel_id=1, source_target_pairs={{0,3},{1,0},{2,1},{3,2},{4,7},{5,4},{6,5},{7,6},{8,11},{9,8},{10,9... | collective-permute-start | bytes 884744 | tf_op jit(solution)/shard_map/ppermute | solution.py:981
  129.4 31.0 %collective-permute-start.13 = (bf16[2,144,1152]{2,1,0:T(8,128)(2,1)}, bf16[2,144,1152]{2,1,0:T(8,128)(2,1)S(1)}, u32[]{:S(2)}, u32[]{:S(2)}) collective-permute-start(bf16[2,144,1152]{2,1,0:T(8,128)(2,1)} %get-tuple-element.119.refs_9_), channel_id=1, source_target_pairs={{0,16},{16,0},{1,17},{17,1},{2,18},{18,2},{3,19},{19,3},{4,20},{20... | collective-permute-start | bytes 1990664 | tf_op jit(solution)/shard_map/ppermute | solution.py:985
  132.8 18.8 %copy-start.36 = (bf16[2,64,1152]{2,1,0:T(8,128)(2,1)}, bf16[2,64,1152]{2,1,0:T(8,128)(2,1)S(1)}, u32[]{:S(2)}) copy-start(bf16[2,64,1152]{2,1,0:T(8,128)(2,1)S(1)} %collective-permute-done.6.refs_2_.refs_12_) | copy-start | bytes 884740
  132.8 27.6 %collective-permute-start.14 = (bf16[2,144,1152]{2,1,0:T(8,128)(2,1)}, bf16[2,144,1152]{2,1,0:T(8,128)(2,1)S(1)}, u32[]{:S(2)}, u32[]{:S(2)}) collective-permute-start(bf16[2,144,1152]{2,1,0:T(8,128)(2,1)} %get-tuple-element.122), channel_id=1, source_target_pairs={{0,8},{8,0},{1,9},{9,1},{2,10},{10,2},{3,11},{11,3},{4,12},{12,4},... | collective-permute-start | bytes 1990664 | tf_op jit(solution)/shard_map/ppermute | solution.py:985
  160.4 6.7 %collective-permute-start.11 = (bf16[512,1152]{1,0:T(8,128)(2,1)}, bf16[512,1152]{1,0:T(8,128)(2,1)S(1)}, u32[]{:S(2)}, u32[]{:S(2)}) collective-permute-start(bf16[512,1152]{1,0:T(8,128)(2,1)} %bitcast.36), channel_id=1, source_target_pairs={{0,4},{4,0},{1,5},{5,1},{2,6},{6,2},{3,7},{7,3},{8,12},{12,8},{9,1... | collective-permute-start | bytes 3538952 | tf_op jit(solution)/shard_map/ppermute | solution.py:985
  163.6 37.6 %collective-permute-start.15 = (bf16[288,1152]{1,0:T(8,128)(2,1)}, bf16[288,1152]{1,0:T(8,128)(2,1)S(1)}, u32[]{:S(2)}, u32[]{:S(2)}) collective-permute-start(bf16[288,1152]{1,0:T(8,128)(2,1)} %release.2.refs_4_), channel_id=1, source_target_pairs={{0,8},{8,0},{1,9},{9,1},{2,10},{10,2},{3,11},{11,3},{4,12},{12,4},... | collective-permute-start | bytes 1990664 | tf_op jit(solution)/shard_map/ppermute | solution.py:985
  163.6 37.6 %collective-permute-start.16 = (bf16[288,1152]{1,0:T(8,128)(2,1)}, bf16[288,1152]{1,0:T(8,128)(2,1)}, u32[]{:S(2)}, u32[]{:S(2)}) collective-permute-start(bf16[288,1152]{1,0:T(8,128)(2,1)} %release.2.refs_4_), channel_id=1, source_target_pairs={{0,16},{16,0},{1,17},{17,1},{2,18},{18,2},{3,19},{19,3},{4,20},{20... | collective-permute-start | bytes 1990664 | tf_op jit(solution)/shard_map/ppermute | solution.py:985
  163.6 37.6 %collective-permute-start.17 = (bf16[288,1152]{1,0:T(8,128)(2,1)}, bf16[288,1152]{1,0:T(8,128)(2,1)}, u32[]{:S(2)}, u32[]{:S(2)}) collective-permute-start(bf16[288,1152]{1,0:T(8,128)(2,1)} %release.2.refs_4_), channel_id=1, source_target_pairs={{0,24},{8,16},{16,8},{24,0},{1,25},{9,17},{17,9},{25,1},{2,26},{10... | collective-permute-start | bytes 1990664 | tf_op jit(solution)/shard_map/ppermute | solution.py:989
  200.5 37.7 %collective-permute-start.20 = (bf16[2,2,144,1152]{3,2,1,0:T(8,128)(2,1)}, bf16[2,2,144,1152]{3,2,1,0:T(8,128)(2,1)S(1)}, u32[]{:S(2)}, u32[]{:S(2)}) collective-permute-start(bf16[2,2,144,1152]{3,2,1,0:T(8,128)(2,1)} %get-tuple-element.137), channel_id=1, source_target_pairs={{0,16},{16,0},{1,17},{17,1},{2,18},{18,2},{3,19},{19,3},{4,20},{20... | collective-permute-start | bytes 3981320 | tf_op jit(solution)/shard_map/ppermute | solution.py:985
  200.6 37.7 %collective-permute-start.21 = (bf16[2,2,144,1152]{3,2,1,0:T(8,128)(2,1)}, bf16[2,2,144,1152]{3,2,1,0:T(8,128)(2,1)}, u32[]{:S(2)}, u32[]{:S(2)}) collective-permute-start(bf16[2,2,144,1152]{3,2,1,0:T(8,128)(2,1)} %get-tuple-element.139), channel_id=1, source_target_pairs={{0,8},{8,0},{1,9},{9,1},{2,10},{10,2},{3,11},{11,3},{4,12},{12,4},... | collective-permute-start | bytes 3981320 | tf_op jit(solution)/shard_map/ppermute | solution.py:985
  237.7 9.4 %collective-permute-start.18 = (f32[512,1152]{1,0:T(8,128)}, f32[512,1152]{1,0:T(8,128)S(1)}, u32[]{:S(2)}, u32[]{:S(2)}) collective-permute-start(f32[512,1152]{1,0:T(8,128)} %get-tuple-element.132), channel_id=1, source_target_pairs={{0,4},{4,0},{1,5},{5,1},{2,6},{6,2},{3,7},{7,3},{8,12},{12,8},{9,1... | collective-permute-start | bytes 7077896 | tf_op jit(solution)/shard_map/ppermute | solution.py:985
  237.8 9.3 %collective-permute-start.19 = (f32[512,1152]{1,0:T(8,128)}, f32[512,1152]{1,0:T(8,128)}, u32[]{:S(2)}, u32[]{:S(2)}) collective-permute-start(f32[512,1152]{1,0:T(8,128)} %get-tuple-element.134), channel_id=1, source_target_pairs={{0,4},{4,0},{1,5},{5,1},{2,6},{6,2},{3,7},{7,3},{8,12},{12,8},{9,1... | collective-permute-start | bytes 7077896 | tf_op jit(solution)/shard_map/ppermute | solution.py:985
  243.6 24.1 %collective-permute-start.25 = (bf16[2,144,1152]{2,1,0:T(8,128)(2,1)}, bf16[2,144,1152]{2,1,0:T(8,128)(2,1)S(1)}, u32[]{:S(2)}, u32[]{:S(2)}) collective-permute-start(bf16[2,144,1152]{2,1,0:T(8,128)(2,1)} %get-tuple-element.147), channel_id=1, source_target_pairs={{0,8},{8,0},{1,9},{9,1},{2,10},{10,2},{3,11},{11,3},{4,12},{12,4},... | collective-permute-start | bytes 1990664 | tf_op jit(solution)/shard_map/ppermute | solution.py:985
  245.1 25.0 %collective-permute-start.26 = (bf16[2,144,1152]{2,1,0:T(8,128)(2,1)}, bf16[2,144,1152]{2,1,0:T(8,128)(2,1)S(1)}, u32[]{:S(2)}, u32[]{:S(2)}) collective-permute-start(bf16[2,144,1152]{2,1,0:T(8,128)(2,1)} %get-tuple-element.149), channel_id=1, source_target_pairs={{0,16},{16,0},{1,17},{17,1},{2,18},{18,2},{3,19},{19,3},{4,20},{20... | collective-permute-start | bytes 1990664 | tf_op jit(solution)/shard_map/ppermute | solution.py:985
  266.5 5.1 collective-permute-start.27
  266.6 22.7 %collective-permute-start.22 = (bf16[2,64,1152]{2,1,0:T(8,128)(2,1)}, bf16[2,64,1152]{2,1,0:T(8,128)(2,1)S(1)}, u32[]{:S(2)}, u32[]{:S(2)}) collective-permute-start(bf16[2,64,1152]{2,1,0:T(8,128)(2,1)} %get-tuple-element.143), channel_id=1, source_target_pairs={{0,3},{1,0},{2,1},{3,2},{4,7},{5,4},{6,5},{7,6},{8,11},{9,8},{10,9... | collective-permute-start | bytes 884744 | tf_op jit(solution)/shard_map/ppermute | solution.py:981
  266.6 22.7 %collective-permute-start.23 = (bf16[2,64,1152]{2,1,0:T(8,128)(2,1)}, bf16[2,64,1152]{2,1,0:T(8,128)(2,1)S(1)}, u32[]{:S(2)}, u32[]{:S(2)}) collective-permute-start(bf16[2,64,1152]{2,1,0:T(8,128)(2,1)} %get-tuple-element.144), channel_id=1, source_target_pairs={{0,2},{1,3},{2,0},{3,1},{4,6},{5,7},{6,4},{7,5},{8,10},{9,11},{10,... | collective-permute-start | bytes 884744 | tf_op jit(solution)/shard_map/ppermute | solution.py:981
  267.7 25.9 %collective-permute-start.24 = (bf16[2,64,1152]{2,1,0:T(8,128)(2,1)}, bf16[2,64,1152]{2,1,0:T(8,128)(2,1)}, u32[]{:S(2)}, u32[]{:S(2)}) collective-permute-start(bf16[2,64,1152]{2,1,0:T(8,128)(2,1)} %get-tuple-element.145), channel_id=1, source_target_pairs={{0,1},{1,2},{2,3},{3,0},{4,5},{5,6},{6,7},{7,4},{8,9},{9,10},{10,1... | collective-permute-start | bytes 884744 | tf_op jit(solution)/shard_map/ppermute | solution.py:981
  280.4 50.6 %collective-permute-start.28 = (bf16[768,1152]{1,0:T(8,128)(2,1)}, bf16[768,1152]{1,0:T(8,128)(2,1)S(1)}, u32[]{:S(2)}, u32[]{:S(2)}) collective-permute-start(bf16[768,1152]{1,0:T(8,128)(2,1)} %get-tuple-element.156.refs_4_), channel_id=1, source_target_pairs={{0,16},{16,0},{1,17},{17,1},{2,18},{18,2},{3,19},{19,3},{4,20},{20... | collective-permute-start | bytes 5308424 | tf_op jit(solution)/shard_map/ppermute | solution.py:985
  280.5 50.6 %collective-permute-start.29 = (bf16[768,1152]{1,0:T(8,128)(2,1)}, bf16[768,1152]{1,0:T(8,128)(2,1)}, u32[]{:S(2)}, u32[]{:S(2)}) collective-permute-start(bf16[768,1152]{1,0:T(8,128)(2,1)} %get-tuple-element.161), channel_id=1, source_target_pairs={{0,8},{8,0},{1,9},{9,1},{2,10},{10,2},{3,11},{11,3},{4,12},{12,4},... | collective-permute-start | bytes 5308424 | tf_op jit(solution)/shard_map/ppermute | solution.py:985
  296.5 70.4 %collective-permute-start.33 = (bf16[288,1152]{1,0:T(8,128)(2,1)}, bf16[288,1152]{1,0:T(8,128)(2,1)S(1)}, u32[]{:S(2)}, u32[]{:S(2)}) collective-permute-start(bf16[288,1152]{1,0:T(8,128)(2,1)} %get-tuple-element.157.refs_0_), channel_id=1, source_target_pairs={{0,3},{1,0},{2,1},{3,2},{4,7},{5,4},{6,5},{7,6},{8,11},{9,8},{10,9... | collective-permute-start | bytes 1990664 | tf_op jit(solution)/shard_map/ppermute | solution.py:981
  300.2 66.7 %collective-permute-start.34 = (bf16[288,1152]{1,0:T(8,128)(2,1)}, bf16[288,1152]{1,0:T(8,128)(2,1)S(1)}, u32[]{:S(2)}, u32[]{:S(2)}) collective-permute-start(bf16[288,1152]{1,0:T(8,128)(2,1)} %get-tuple-element.171), channel_id=1, source_target_pairs={{0,2},{1,3},{2,0},{3,1},{4,6},{5,7},{6,4},{7,5},{8,10},{9,11},{10,... | collective-permute-start | bytes 1990664 | tf_op jit(solution)/shard_map/ppermute | solution.py:981
  331.0 163.4 %reduce-scatter.5.cloned.1.call-start = ((), (), s32[]{:S(2)}) async-start(), calls=%async_computation.4 | async-start | bytes 2949120 | tf_op jit(solution)/shard_map/reduce_scatter | solution.py:1252
  337.3 31.3 %collective-permute-start.31 = (bf16[384,1152]{1,0:T(8,128)(2,1)}, bf16[384,1152]{1,0:T(8,128)(2,1)}, u32[]{:S(2)}, u32[]{:S(2)}) collective-permute-start(bf16[384,1152]{1,0:T(8,128)(2,1)} %get-tuple-element.167), channel_id=1, source_target_pairs={{0,8},{8,0},{1,9},{9,1},{2,10},{10,2},{3,11},{11,3},{4,12},{12,4},... | collective-permute-start | bytes 2654216 | tf_op jit(solution)/shard_map/ppermute | solution.py:985
  337.3 31.3 %collective-permute-start.32 = (bf16[384,1152]{1,0:T(8,128)(2,1)}, bf16[384,1152]{1,0:T(8,128)(2,1)}, u32[]{:S(2)}, u32[]{:S(2)}) collective-permute-start(bf16[384,1152]{1,0:T(8,128)(2,1)} %get-tuple-element.169), channel_id=1, source_target_pairs={{0,16},{16,0},{1,17},{17,1},{2,18},{18,2},{3,19},{19,3},{4,20},{20... | collective-permute-start | bytes 2654216 | tf_op jit(solution)/shard_map/ppermute | solution.py:985
  366.8 11.1 %collective-permute-start.30 = (bf16[448,1152]{1,0:T(8,128)(2,1)}, bf16[448,1152]{1,0:T(8,128)(2,1)}, u32[]{:S(2)}, u32[]{:S(2)}) collective-permute-start(bf16[448,1152]{1,0:T(8,128)(2,1)} %get-tuple-element.166), channel_id=1, source_target_pairs={{0,4},{4,0},{1,5},{5,1},{2,6},{6,2},{3,7},{7,3},{8,12},{12,8},{9,1... | collective-permute-start | bytes 3096584 | tf_op jit(solution)/shard_map/ppermute | solution.py:985
  372.1 47.5 %collective-permute-start.38 = (bf16[48,1152]{1,0:T(8,128)(2,1)}, bf16[48,1152]{1,0:T(8,128)(2,1)S(1)}, u32[]{:S(2)}, u32[]{:S(2)}) collective-permute-start(bf16[48,1152]{1,0:T(8,128)(2,1)} %get-tuple-element.183), channel_id=1, source_target_pairs={{0,3},{1,0},{2,1},{3,2},{4,7},{5,4},{6,5},{7,6},{8,11},{9,8},{10,9... | collective-permute-start | bytes 331784 | tf_op jit(solution)/shard_map/ppermute | solution.py:981
  372.2 47.4 %collective-permute-start.39 = (bf16[48,1152]{1,0:T(8,128)(2,1)}, bf16[48,1152]{1,0:T(8,128)(2,1)S(1)}, u32[]{:S(2)}, u32[]{:S(2)}) collective-permute-start(bf16[48,1152]{1,0:T(8,128)(2,1)} %get-tuple-element.184), channel_id=1, source_target_pairs={{0,2},{1,3},{2,0},{3,1},{4,6},{5,7},{6,4},{7,5},{8,10},{9,11},{10,... | collective-permute-start | bytes 331784 | tf_op jit(solution)/shard_map/ppermute | solution.py:981
  374.9 46.0 %collective-permute-start.37 = (bf16[336,1152]{1,0:T(8,128)(2,1)}, bf16[336,1152]{1,0:T(8,128)(2,1)S(1)}, u32[]{:S(2)}, u32[]{:S(2)}) collective-permute-start(bf16[336,1152]{1,0:T(8,128)(2,1)} %get-tuple-element.172.refs_3_.refs_5_), channel_id=1, source_target_pairs={{0,1},{1,2},{2,3},{3,0},{4,5},{5,6},{6,7},{7,4},{8,9},{9,10},{10,1... | collective-permute-start | bytes 2322440 | tf_op jit(solution)/shard_map/ppermute | solution.py:981
  381.6 13.5 %collective-permute-start.35 = (bf16[224,1152]{1,0:T(8,128)(2,1)}, bf16[224,1152]{1,0:T(8,128)(2,1)S(1)}, u32[]{:S(2)}, u32[]{:S(2)}) collective-permute-start(bf16[224,1152]{1,0:T(8,128)(2,1)} %get-tuple-element.174), channel_id=1, source_target_pairs={{0,8},{8,0},{1,9},{9,1},{2,10},{10,2},{3,11},{11,3},{4,12},{12,4},... | collective-permute-start | bytes 1548296 | tf_op jit(solution)/shard_map/ppermute | solution.py:985
  384.8 52.3 %collective-permute-start.43 = (f32[56,1152]{1,0:T(8,128)}, f32[56,1152]{1,0:T(8,128)}, u32[]{:S(2)}, u32[]{:S(2)}) collective-permute-start(f32[56,1152]{1,0:T(8,128)} %pile.1.refs_6_.refs_0_), channel_id=1, source_target_pairs={{0,2},{1,3},{2,0},{3,1},{4,6},{5,7},{6,4},{7,5},{8,10},{9,11},{10,... | collective-permute-start | bytes 774152 | tf_op jit(solution)/shard_map/ppermute | solution.py:981
  398.9 27.4 %collective-permute-start.36 = (bf16[112,1152]{1,0:T(8,128)(2,1)}, bf16[112,1152]{1,0:T(8,128)(2,1)S(1)}, u32[]{:S(2)}, u32[]{:S(2)}) collective-permute-start(bf16[112,1152]{1,0:T(8,128)(2,1)} %get-tuple-element.181), channel_id=1, source_target_pairs={{0,16},{16,0},{1,17},{17,1},{2,18},{18,2},{3,19},{19,3},{4,20},{20... | collective-permute-start | bytes 774152 | tf_op jit(solution)/shard_map/ppermute | solution.py:985
  430.4 56.1 %collective-permute-start.40 = (bf16[448,1152]{1,0:T(8,128)(2,1)}, bf16[448,1152]{1,0:T(8,128)(2,1)}, u32[]{:S(2)}, u32[]{:S(2)}) collective-permute-start(bf16[448,1152]{1,0:T(8,128)(2,1)} %merge.1.refs_1_.refs_2_.refs_6_), channel_id=1, source_target_pairs={{0,8},{8,0},{1,9},{9,1},{2,10},{10,2},{3,11},{11,3},{4,12},{12,4},... | collective-permute-start | bytes 3096584 | tf_op jit(solution)/shard_map/ppermute | solution.py:985
  430.4 56.1 %collective-permute-start.41 = (bf16[448,1152]{1,0:T(8,128)(2,1)}, bf16[448,1152]{1,0:T(8,128)(2,1)}, u32[]{:S(2)}, u32[]{:S(2)}) collective-permute-start(bf16[448,1152]{1,0:T(8,128)(2,1)} %merge.1.refs_1_.refs_2_.refs_6_), channel_id=1, source_target_pairs={{0,16},{16,0},{1,17},{17,1},{2,18},{18,2},{3,19},{19,3},{4,20},{20... | collective-permute-start | bytes 3096584 | tf_op jit(solution)/shard_map/ppermute | solution.py:985
  432.1 54.4 %collective-permute-start.42 = (bf16[448,1152]{1,0:T(8,128)(2,1)}, bf16[448,1152]{1,0:T(8,128)(2,1)}, u32[]{:S(2)}, u32[]{:S(2)}) collective-permute-start(bf16[448,1152]{1,0:T(8,128)(2,1)} %merge.1.refs_1_.refs_2_.refs_6_), channel_id=1, source_target_pairs={{0,24},{8,16},{16,8},{24,0},{1,25},{9,17},{17,9},{25,1},{2,26},{10... | collective-permute-start | bytes 3096584 | tf_op jit(solution)/shard_map/ppermute | solution.py:989
  437.1 20.7 %copy-start.2 = (bf16[1152,1728]{0,1:T(8,128)(2,1)S(1)}, bf16[1152,1728]{0,1:T(8,128)(2,1)}, u32[]{:S(2)}) copy-start(bf16[1152,1728]{0,1:T(8,128)(2,1)} %param.18) | copy-start | bytes 11943940
  439.1 12.1 %collective-permute-start.44 = (f32[56,1152]{1,0:T(8,128)}, f32[56,1152]{1,0:T(8,128)}, u32[]{:S(2)}, u32[]{:S(2)}) collective-permute-start(f32[56,1152]{1,0:T(8,128)} %sum.1.refs_1_), channel_id=1, source_target_pairs={{0,1},{1,2},{2,3},{3,0},{4,5},{5,6},{6,7},{7,4},{8,9},{9,10},{10,1... | collective-permute-start | bytes 774152 | tf_op jit(solution)/shard_map/ppermute | solution.py:981
  454.0 1.7 collective-permute-start.45
  457.6 26.9 %collective-permute-start.46 = (f32[2,24,1728]{2,1,0:T(8,128)}, f32[2,24,1728]{2,1,0:T(8,128)}, u32[]{:S(2)}, u32[]{:S(2)}) collective-permute-start(f32[2,24,1728]{2,1,0:T(8,128)} %pair.3.refs_0_), channel_id=1, source_target_pairs={{0,8},{8,0},{1,9},{9,1},{2,10},{10,2},{3,11},{11,3},{4,12},{12,4},... | collective-permute-start | bytes 995336 | tf_op jit(solution)/shard_map/ppermute | solution.py:985
  459.2 5.8 %collective-permute-start.47 = (f32[8,1152]{1,0:T(8,128)S(1)}, f32[8,1152]{1,0:T(8,128)S(1)}, u32[]{:S(2)}, u32[]{:S(2)}) collective-permute-start(f32[8,1152]{1,0:T(8,128)S(1)} %fusion.10), channel_id=1, source_target_pairs={{0,2},{1,3},{2,0},{3,1},{4,6},{5,7},{6,4},{7,5},{8,10},{9,11},{10,... | collective-permute-start | bytes 110600 | tf_op jit(solution)/shard_map/ppermute | solution.py:981
  465.0 4.9 collective-permute-start.48
  491.7 7.2 %collective-permute-start.50 = (bf16[2,576,1152]{2,1,0:T(8,128)(2,1)}, bf16[2,576,1152]{2,1,0:T(8,128)(2,1)}, u32[]{:S(2)}, u32[]{:S(2)}) collective-permute-start(bf16[2,576,1152]{2,1,0:T(8,128)(2,1)} %get-tuple-element.189.refs_6_.refs_1_), channel_id=1, source_target_pairs={{0,4},{4,0},{1,5},{5,1},{2,6},{6,2},{3,7},{7,3},{8,12},{12,8},{9,1... | collective-permute-start | bytes 7962632 | tf_op jit(solution)/shard_map/ppermute | solution.py:985
  491.7 6.7 %collective-permute-start.51 = (bf16[592,1152]{1,0:T(8,128)(2,1)}, bf16[592,1152]{1,0:T(8,128)(2,1)S(1)}, u32[]{:S(2)}, u32[]{:S(2)}) collective-permute-start(bf16[592,1152]{1,0:T(8,128)(2,1)} %get-tuple-element.190.refs_3_), channel_id=1, source_target_pairs={{0,4},{4,0},{1,5},{5,1},{2,6},{6,2},{3,7},{7,3},{8,12},{12,8},{9,1... | collective-permute-start | bytes 4091912 | tf_op jit(solution)/shard_map/ppermute | solution.py:985
  492.9 17.3 %collective-permute-start.49 = (f32[4,24,1728]{2,1,0:T(8,128)S(1)}, f32[4,24,1728]{2,1,0:T(8,128)S(1)}, u32[]{:S(2)}, u32[]{:S(2)}) collective-permute-start(f32[4,24,1728]{2,1,0:T(8,128)S(1)} %copy-done.3), channel_id=1, source_target_pairs={{0,16},{16,0},{1,17},{17,1},{2,18},{18,2},{3,19},{19,3},{4,20},{20... | collective-permute-start | bytes 1990664 | tf_op jit(solution)/shard_map/ppermute | solution.py:985
  513.6 6.6 %copy-start.1 = (bf16[288,1152]{1,0:T(8,128)(2,1)S(1)}, bf16[288,1152]{1,0:T(8,128)(2,1)}, u32[]{:S(2)}) copy-start(bf16[288,1152]{1,0:T(8,128)(2,1)} %param.22) | copy-start | bytes 1990660
  (32 other events, 63.5 us)
Sparse Core Ops, SparseCore 0:
  10.7 108.2 all-gather.1
  331.1 59.7 reduce-scatter.2
  437.2 48.7 reduce-scatter.4

commit v4 on v3

--- a/solution.py
+++ b/solution.py
@@ -681,21 +681,25 @@
 
 
 def ada_kernel(info, cond_ref, w_ref, bias_ref, units_ref, small_ref, act_ref):
-    value = cond_ref[...].astype(F32)
+    value = jnp.concatenate([cond_ref[m].astype(F32) for m in range(cond_ref.shape[0])], axis=0)
     act = (value / (1.0 + jnp.exp(-value))).astype(BF)
     act_ref[...] = act
-    count = act.shape[0]
-    small_ref[...] = jnp.zeros_like(small_ref)
-    small_ref[:count] = nt(act, w_ref[...]) + bias_ref[...]
-    half = units_ref.shape[1] // 2
-    mine = jnp.where(info[1] == 0, units_ref[:, :half], units_ref[:, half:])
-    small_ref[count : count + 1, :half] = in_order(mine, info[2], half // 4)
+    count, columns = act.shape[0], w_ref.shape[0]
+    small_ref[:, :columns] = nt(act, w_ref[...]) + bias_ref[...][None]
+    units = units_ref[...][None]
+    half = units.shape[1] // 2
+    mine = jnp.where(info[1] == 0, units[:, :half], units[:, half:])
+    mine = in_order(mine, info[2], half // 4)
+    each = half // count
+    for i in range(count):
+        small_ref[i : i + 1, columns:] = mine[:, i * each : (i + 1) * each]
 
 
 def modulate_kernel(info, s0, s1, s2, s3, mod_ref, far_ref, near_ref, lanes, full):
     rank = info[0]
+    count, columns = lanes.shape[1:]
     for shift, ref in enumerate((s0, s1, s2, s3)):
-        lanes[lax.rem(rank + 4 - shift, 4)] = ref[...]
+        lanes[lax.rem(rank + 4 - shift, 4)] = ref[:, :columns]
     full[...] = jnp.concatenate([lanes[i] for i in range(4)], axis=1)
     width = mod_ref.shape[2]
     for i in range(mod_ref.shape[0]):
@@ -704,10 +708,9 @@
         row = full[pl.ds(slot, 1), :] * (segment < 4).astype(F32)
         for j in range(6):
             mod_ref[i, j : j + 1, :] = row[:, j * width : (j + 1) * width]
-    half = far_ref.shape[2]
     for ref, order in ((far_ref, (s2, s1)), (near_ref, (s3, s0))):
         for i, source in enumerate(order):
-            ref[i] = source[8:9, :half]
+            ref[i] = jnp.concatenate([source[j : j + 1, columns:] for j in range(count)], axis=1)
 
 
 def pile_kernel(info, l0, l1, sums, far, near, out):
@@ -1031,8 +1034,8 @@
 
     small, cond_act = simple(
         ada_kernel,
-        [shape((16, columns), F32), shape((micro * slots, width), BF)],
-        [conditioning.reshape(micro * slots, width), ada_turned, ada_bias[None], up_bias[None]],
+        [shape((micro * slots, columns + half // (micro * slots)), F32), shape((micro * slots, width), BF)],
+        [conditioning, ada_turned, ada_bias, up_bias],
         info,
         name="ada", micros=0.01,
     )
@@ -1047,7 +1050,7 @@
         scratch=[pltpu.VMEM((part, width), BF)],
         name="pack", micros=0.01,
     )
-    got = {k: turn(mine, k) for k in (2, 1, 3)}
+    got = {k: turn(mine, k) for k in (2, 1)}
     out_rows = lax.dynamic_slice_in_dim(out_weight, quarter * (local_width // 4), local_width // 4, 0)
     out_full = lax.all_gather(out_rows, ("tensor", "y", "x"), axis=0, tiled=True)
     out_full = out_full.reshape(groups, local_width, width)
@@ -1062,7 +1065,10 @@
         smalls,
         info,
         after=(mine,),
-        scratch=[pltpu.VMEM((4, 16, columns), F32), pltpu.VMEM((16, 6 * width), F32)],
+        scratch=[
+            pltpu.VMEM((4, micro * slots, columns), F32),
+            pltpu.VMEM((micro * slots, 6 * width), F32),
+        ],
         name="modulate", micros=0.01,
     )
     hidden_one, query, key, value = project(tokens, mod_blocks, qkv_turned, qv_bias, groups)
@@ -1075,30 +1081,30 @@
     own_g = grad_mlp.astype(BF).reshape(micro * share, width)
     other_g = flip(own_g, "core")
 
+    def release(arrays, after, micros=3):
+        return simple(
+            copy_kernel, [shape(a.shape, a.dtype) for a in arrays], arrays, after=after, name="release", micros=micros
+        )
+
+    *att, lse = attend(jnp.concatenate([rank[None], whole]), query, key, value)
     (two,) = simple(
         stack_kernel,
         [shape((2, 2 * piece, width), BF)],
         [got[2], got[1]],
-        after=(query,),
+        after=(lse,),
         name="two",
         micros=0.01,
     )
-    *att, lse = attend(
-        jnp.concatenate([rank[None], whole]), query, key, value, after=(two, other_g)
-    )
-    parts = [att[0], turn(att[1], 1), turn(att[2], 2), turn(att[3], 3)]
     two_parts = (two, flip(two, "x"), flip(two, "y"))
-
-    def release(arrays, after, micros=3):
-        return simple(
-            copy_kernel, [shape(a.shape, a.dtype) for a in arrays], arrays, after=after, name="release", micros=micros
-        )
+    sent = release([*att[1:], mine], (two, other_g), 0.01)
+    parts = [att[0], turn(sent[0], 1), turn(sent[1], 2), turn(sent[2], 3)]
+    got[3] = turn(sent[3], 3)
 
     corner = simple(
         corner_kernel,
         [shape((2, piece, width), BF)] * 2,
         two_parts[1:],
-        after=(lse,),
+        after=(sent[0],),
         name="corner",
     )
     two_parts = (*two_parts, flip(corner[0], "y"), flip(corner[1], "x"))
@@ -1225,17 +1231,17 @@
         pile_kernel, [shape((56, width), F32)], [lsum_0, lsum_1, sums, bsum_a, bsum_b], "pile", (keep,)
     )
     pile_got = turn(pile, 2)
-    tokens_grad = finish(here, 0, share_0, tokens, mod_blocks, grad_mid, groups, after=(*token, pile))
     keep, send = short(
         second_kernel,
         [rows_shape(rows_all // 4)] * 2,
         [keep, flip(send, "x")],
         "second",
-        (tokens_grad,),
+        (*token, pile),
         [pltpu.VMEM((rows_all // 2, width), BF)],
     )
+    tokens_grad = finish(here, 0, share_0, tokens, mod_blocks, grad_mid, groups, after=(keep,))
     send_got = flip(send, "y")
-    (tick,) = plain(tick_kernel, [shape((8, 128), F32)], [], "tick", (keep, o1, o2), micros=60)
+    (tick,) = plain(tick_kernel, [shape((8, 128), F32)], [], "tick", (keep, tokens_grad, o1, o2), micros=60)
     (merged,) = plain(
         merge_kernel,
         [rows_shape(rows_all // 4 + 2 * piece + o_room)],

time: 532 us -> 519 us (0.976)
  Pallas kernels: 290 us -> 279 us
    ppermute x21, waiting for transfers between devices: 89.3 us -> 61.4 us  [turn(): lax.ppermute(array, 'tensor', [(i, (i + shift) % count) for i in range(co...]
    ppermute x29, waiting for transfers between devices: 23.7 us -> 44.4 us  [flip(): return lax.ppermute(array, axis, [(0, 1), (1, 0)])]
    reduce_scatter x1, waiting for transfers between devices: 5.12 us -> 16 us  [local(): lax.psum_scatter(part_0, 'tensor', scatter_dimension=0, tiled=True)]
    ppermute x29, starting transfers between devices: 34.5 us -> 24.1 us  [flip(): return lax.ppermute(array, axis, [(0, 1), (1, 0)])]
    pallas_call x2, Pallas kernels: 60 us -> 50.4 us  [attend_back(): pl.pallas_call(functools.partial(attend_back_kernel, micro, last, len(aft...]
    ppermute x21, starting transfers between devices: 28.7 us -> 34.9 us  [turn(): lax.ppermute(array, 'tensor', [(i, (i + shift) % count) for i in range(co...]
    pallas_call x26 -> x27, Pallas kernels: 84.6 us -> 86.8 us  [simple(): pl.pallas_call(body, grid_spec=pltpu.PrefetchScalarGridSpec(num_scalar_pr...]
    unnamed x83 -> x89, local copies, waits for them, and re-layouts: 17.5 us -> 19.2 us
  transfers between devices with their start and end apart: 55 -> 55, of which waited for: 19 -> 15; matrix products, arithmetic and copies ran while one was open for 3% -> 3% of each run, Pallas kernels for 53% -> 53%
where the time goes in v4:
time: 519 us; the launch traced here: 514 us
  Pallas kernels  279 us (54%)
  waiting for transfers between devices  122 us (24%)
  starting transfers between devices  64.5 us (12%)
  local copies, waits for them, and re-layouts  23.3 us (4%)
  between operations  14.5 us (3%)
  other arithmetic  9.17 us (2%)
    pallas_call x27, Pallas kernels, simple(): pl.pallas_call(body, grid_spec=pltpu.PrefetchScalarGridSpec(num_scalar_pr...  86.8 us
    pallas_call x2, Pallas kernels, feed(): pl.pallas_call(functools.partial(feed_kernel, first, tuple((len(p) for p...  68 us
    ppermute x21, waiting for transfers between devices, turn(): lax.ppermute(array, 'tensor', [(i, (i + shift) % count) for i in range(co...  61.4 us
    pallas_call x2, Pallas kernels, attend_back(): pl.pallas_call(functools.partial(attend_back_kernel, micro, last, len(aft...  50.4 us
    ppermute x29, waiting for transfers between devices, flip(): return lax.ppermute(array, axis, [(0, 1), (1, 0)])  44.4 us
    ppermute x21, starting transfers between devices, turn(): lax.ppermute(array, 'tensor', [(i, (i + shift) % count) for i in range(co...  34.9 us
    ppermute x29, starting transfers between devices, flip(): return lax.ppermute(array, axis, [(0, 1), (1, 0)])  24.1 us
    unnamed x89, local copies, waits for them, and re-layouts  19.2 us
  transfers between devices with their start and end apart: 55, of which 15 were waited for; matrix products, arithmetic and copies ran while one was open for 3% of the time, Pallas kernels for 53%

profile of v4, /device:TPU:10, one launch (start us, length us, event | category | flops | bytes accessed | tf_op | source)
XLA Modules:
  0.0 514.1 jit_solution(18315700182371049322)
XLA Ops:
  10.8 4.6 ada.1
  15.3 1.6 collective-permute-start
  18.2 1.8 collective-permute-start.2
  20.0 5.9 %pack.1 = (bf16[576,1152]{1,0:T(8,128)(2,1)}, bf16[576,1152]{1,0:T(8,128)(2,1)}, bf16[288,1152]{1,0:T(8,128)(2,1)}) custom-call(s32[11]{0:T(128)} %pad_add_fusion.3.refs_0_, bf16[1152,1152]{1,0:T(8,128)(2,1)} %refs_1_.3, bf16[1152,1152]{1,0:T(8,128)(2,1)} %refs_2_.3, bf16[8,1152]{1,0:T(8,128)(2,1)} %get-tuple-element.112.refs_3_.refs_5_), custom_call_target="tpu_custom_call" | custom-call | flops 11500000 | bytes 1000 | tf_op jit(solution)/shard_map/pack/pallas_call | solution.py:69
  26.3 2.4 collective-permute-start.4
  31.4 2.5 modulate.1
  34.9 12.9 %project.1 = (bf16[2,1024,1152]{2,1,0:T(8,128)(2,1)}, bf16[2,4,1024,72]{3,2,1,0:T(8,128)(2,1)}, bf16[2,4,1024,72]{3,2,1,0:T(8,128)(2,1)}, bf16[2,4,1024,72]{3,2,1,0:T(8,128)(2,1)}) custom-call(bf16[2,1024,1152]{2,1,0:T(8,128)(2,1)} %refs_2_.5, f32[8,6,1152]{2,1,0:T(8,128)} %get-tuple-element.114.mod_ref.refs_8_.refs_3_, bf16[864,1152]{1,0:T(8,128)(2,1)} %bitcast.25, ...), custom_call_target="tpu_custom_call" | custom-call | flops 11500000 | bytes 1000 | tf_op jit(solution)/shard_map/project/pallas_call | solution.py:123
  47.7 17.4 %attend.1 = (bf16[2,64,1152]{2,1,0:T(8,128)(2,1)}, bf16[2,64,1152]{2,1,0:T(8,128)(2,1)}, bf16[2,64,1152]{2,1,0:T(8,128)(2,1)}, bf16[2,64,1152]{2,1,0:T(8,128)(2,1)}, f32[2,4,1024]{2,1,0:T(4,128)}) custom-call(s32[3]{0:T(128)} %pad_add_fusion.2.refs_0_, bf16[2,4,1024,72]{3,2,1,0:T(8,128)(2,1)} %get-tuple-element.115.refs_1_.q_ref, ...), custom_call_target="tpu_custom_call" | custom-call | flops 11500000 | bytes 1000 | tf_op jit(solution)/shard_map/attend/pallas_call | solution.py:185
  65.2 12.3 %collective-permute-done.4.refs_1_ = bf16[288,1152]{1,0:T(8,128)(2,1)S(1)} collective-permute-done((bf16[288,1152]{1,0:T(8,128)(2,1)}, bf16[288,1152]{1,0:T(8,128)(2,1)S(1)}, u32[]{:S(2)}, u32[]{:S(2)}) %collective-permute-start.4) | collective-permute-done | bytes 663584 | tf_op jit(solution)/shard_map/ppermute | solution.py:984
  78.3 2.5 two.1.refs_4_
  90.9 2.5 release.3
  93.4 2.7 collective-permute-start.6
  96.2 3.8 collective-permute-start.7
  99.9 21.2 %collective-permute-done.10.refs_1_.refs_6_ = bf16[2,288,1152]{2,1,0:T(8,128)(2,1)} collective-permute-done((bf16[2,288,1152]{2,1,0:T(8,128)(2,1)}, bf16[2,288,1152]{2,1,0:T(8,128)(2,1)}, u32[]{:S(2)}, u32[]{:S(2)}) %collective-permute-start.10) | collective-permute-done | bytes 1327136 | tf_op jit(solution)/shard_map/ppermute | solution.py:988
  121.1 3.4 collective-permute-start.12
  124.6 2.8 corner.1
  128.3 14.8 %collective-permute-done.7.refs_3_.refs_13_ = bf16[2,64,1152]{2,1,0:T(8,128)(2,1)S(1)} collective-permute-done((bf16[2,64,1152]{2,1,0:T(8,128)(2,1)}, bf16[2,64,1152]{2,1,0:T(8,128)(2,1)S(1)}, u32[]{:S(2)}, u32[]{:S(2)}) %collective-permute-start.7) | collective-permute-done | bytes 294944 | tf_op jit(solution)/shard_map/ppermute | solution.py:984
  144.0 8.0 %middle.1 = (f32[2,256,1152]{2,1,0:T(8,128)}, f32[2,256,1152]{2,1,0:T(8,128)}, bf16[2,256,1152]{2,1,0:T(8,128)(2,1)}) custom-call(s32[3]{0:T(128)} %pad_add_fusion.1.refs_0_, bf16[2,64,1152]{2,1,0:T(8,128)(2,1)} %get-tuple-element.118.refs_1_.refs_11_, bf16[2,64,1152]{2,1,0:T(8,128)(2,1)} %copy-done.37, bf16[2,64,1152]{2,1,0:T(8,128)(2,1)} %copy-done.38, ...), custom_call_target="tpu_custom_call" | custom-call | flops 9200000000 | bytes 800000 | tf_op jit(solution)/shard_map/middle/pallas_call | solution.py:217
  153.4 2.0 release.4.refs_4_
  157.1 1.9 collective-permute-start.17
  160.0 32.4 %feed.2 = (f32[512,1152]{1,0:T(8,128)}, f32[512,1152]{1,0:T(8,128)}, f32[512,1152]{1,0:T(8,128)}, f32[512,1152]{1,0:T(8,128)}, bf16[2,2,144,1152]{3,2,1,0:T(8,12...) custom-call(bf16[512,1152]{1,0:T(8,128)(2,1)} %bitcast.37, ...), custom_call_target="tpu_custom_call" | custom-call | flops 39099998208 | bytes 3400000 | tf_op jit(solution)/shard_map/feed/pallas_call | solution.py:354
  192.5 1.6 collective-permute-start.21
  195.0 35.6 %feed.3 = (f32[512,1152]{1,0:T(8,128)}, f32[512,1152]{1,0:T(8,128)}, f32[512,1152]{1,0:T(8,128)}, f32[512,1152]{1,0:T(8,128)}, bf16[2,2,144,1152]{3,2,1,0:T(8,12...) custom-call(bf16[512,1152]{1,0:T(8,128)(2,1)} %bitcast.38, ...), custom_call_target="tpu_custom_call" | custom-call | flops 39099998208 | bytes 3400000 | tf_op jit(solution)/shard_map/feed/pallas_call | solution.py:354
  232.2 4.2 halve.2
  236.9 1.9 collective-permute-start.26
  240.3 18.0 %between.1 = (bf16[2,256,1152]{2,1,0:T(8,128)(2,1)}, f32[2,256,1152]{2,1,0:T(8,128)}, bf16[2,64,1152]{2,1,0:T(8,128)(2,1)}, bf16[2,64,1152]{2,1,0:T(8,128)(2,1)}...) custom-call(s32[4]{0:T(128)} %pad_add_fusion.refs_0_, ...), custom_call_target="tpu_custom_call" | custom-call | flops 20700000256 | bytes 1800000 | tf_op jit(solution)/shard_map/between/pallas_call | solution.py:434
  258.5 3.4 collective-permute-start.23
  261.8 2.8 collective-permute-start.24
  267.2 7.7 %mix.1 = (bf16[768,1152]{1,0:T(8,128)(2,1)}, bf16[768,1152]{1,0:T(8,128)(2,1)}, bf16[768,1152]{1,0:T(8,128)(2,1)}, bf16[768,1152]{1,0:T(8,128)(2,1)}) custom-call(s32[11]{0:T(128)} %pad_add_fusion.3.refs_0_, bf16[2,2,144,1152]{3,2,1,0:T(8,128)(2,1)} %get-tuple-element.158.refs_1_, bf16[2,2,144,1152]{3,2,1,0:T(8,128)(2,1)} %get-tuple-element.159.refs_2_, ...), custom_call_target="tpu_custom_call" | custom-call | flops 3449999872 | bytes 300000 | tf_op jit(solution)/shard_map/mix/pallas_call | solution.py:69
  276.5 5.6 %collective-permute-done.23.refs_6_.g2 = bf16[2,64,1152]{2,1,0:T(8,128)(2,1)S(1)} collective-permute-done((bf16[2,64,1152]{2,1,0:T(8,128)(2,1)}, bf16[2,64,1152]{2,1,0:T(8,128)(2,1)S(1)}, u32[]{:S(2)}, u32[]{:S(2)}) %collective-permute-start.23) | collective-permute-done | bytes 294944 | tf_op jit(solution)/shard_map/ppermute | solution.py:984
  282.2 5.8 %collective-permute-done.24.refs_7_.g3 = bf16[2,64,1152]{2,1,0:T(8,128)(2,1)} collective-permute-done((bf16[2,64,1152]{2,1,0:T(8,128)(2,1)}, bf16[2,64,1152]{2,1,0:T(8,128)(2,1)}, u32[]{:S(2)}, u32[]{:S(2)}) %collective-permute-start.24) | collective-permute-done | bytes 294944 | tf_op jit(solution)/shard_map/ppermute | solution.py:984
  287.9 2.9 quarter.1
  292.1 2.7 collective-permute-start.34
  294.8 30.5 %attend_back.2 = (bf16[1024,1152]{1,0:T(8,128)(2,1)}, f32[8,1152]{1,0:T(8,128)}, f32[8,288]{1,0:T(8,128)}, f32[864,1152]{1,0:T(8,128)}) custom-call(s32[3]{0:T(128)} %add_add_fusion.1.info_ref, bf16[2,4,1024,72]{3,2,1,0:T(8,128)(2,1)} %get-tuple-element.115.refs_1_.q_ref, bf16[2,4,1024,72]{3,2,1,0:T(8,128)(2,1)} %get-tuple-element.116.refs_2_.k_ref, ...), custom_call_target="tpu_custom_call" | custom-call | flops 34500001792 | bytes 3000000 | tf_op jit(solution)/shard_map/attend_back/pallas_call | solution.py:607
  326.5 5.1 halve.3
  333.3 19.9 %attend_back.3 = (bf16[1024,1152]{1,0:T(8,128)(2,1)}, f32[8,1152]{1,0:T(8,128)}, f32[8,288]{1,0:T(8,128)}, bf16[448,1152]{1,0:T(8,128)(2,1)}, bf16[448,1152]{1,0:T(8,128)(2,1)}) custom-call(s32[3]{0:T(128)} %add_add_fusion.info_ref, bf16[2,4,1024,72]{3,2,1,0:T(8,128)(2,1)} %get-tuple-element.115.refs_1_.q_ref, ...), custom_call_target="tpu_custom_call" | custom-call | flops 34500001792 | bytes 3000000 | tf_op jit(solution)/shard_map/attend_back/pallas_call | solution.py:607
  354.9 3.5 last.1
  358.5 3.9 first.1
  362.9 2.2 collective-permute-start.38
  365.1 1.9 collective-permute-start.39
  367.0 2.4 pile.1.refs_4_.refs_0_
  370.4 6.3 %collective-permute-done.35.refs_2_ = bf16[224,1152]{1,0:T(8,128)(2,1)S(1)} collective-permute-done((bf16[224,1152]{1,0:T(8,128)(2,1)}, bf16[224,1152]{1,0:T(8,128)(2,1)S(1)}, u32[]{:S(2)}, u32[]{:S(2)}) %collective-permute-start.35) | collective-permute-done | bytes 516128 | tf_op jit(solution)/shard_map/ppermute | solution.py:988
  377.5 2.9 second.1
  380.4 10.2 %collective-permute-start.36 = (bf16[112,1152]{1,0:T(8,128)(2,1)}, bf16[112,1152]{1,0:T(8,128)(2,1)S(1)}, u32[]{:S(2)}, u32[]{:S(2)}) collective-permute-start(bf16[112,1152]{1,0:T(8,128)(2,1)} %get-tuple-element.187), channel_id=1, source_target_pairs={{0,16},{16,0},{1,17},{17,1},{2,18},{18,2},{3,19},{19,3},{4,20},{20... | collective-permute-start | bytes 774152 | tf_op jit(solution)/shard_map/ppermute | solution.py:988
  390.6 16.0 %reduce-scatter.3.cloned.1.call-done.refs_1_ = bf16[256,1152]{1,0:T(8,128)(2,1)} async-done(((bf16[1024,1152]{1,0:T(8,128)(2,1)}), bf16[256,1152]{1,0:T(8,128)(2,1)}) %reduce-scatter.3.cloned.1.call-update) | async-done | bytes 589840 | tf_op jit(solution)/shard_map/reduce_scatter | solution.py:1176
  406.6 4.1 finish.2.refs_1_.refs_5_
  413.5 3.4 merge.1.refs_1_.refs_2_.refs_6_
  417.0 3.5 collective-permute-start.42
  420.4 3.2 release.5
  423.7 1.9 sum.1.refs_1_
  425.7 13.2 %collective-permute-done.44.refs_2_ = f32[56,1152]{1,0:T(8,128)} collective-permute-done((f32[56,1152]{1,0:T(8,128)}, f32[56,1152]{1,0:T(8,128)}, u32[]{:S(2)}, u32[]{:S(2)}) %collective-permute-start.44) | collective-permute-done | bytes 258080 | tf_op jit(solution)/shard_map/ppermute | solution.py:984
  438.9 2.9 slots.1
  441.8 1.7 collective-permute-done.45
  443.5 1.8 pair.3.refs_0_
  447.0 5.7 %collective-permute-done.47 = f32[8,1152]{1,0:T(8,128)S(1)} collective-permute-done((f32[8,1152]{1,0:T(8,128)S(1)}, f32[8,1152]{1,0:T(8,128)S(1)}, u32[]{:S(2)}, u32[]{:S(2)}) %collective-permute-start.47) | collective-permute-done | bytes 36896 | tf_op jit(solution)/shard_map/ppermute | solution.py:984
  452.8 2.2 collective-permute-start.48
  455.0 3.9 collective-permute-done.48
  459.5 12.1 %collective-permute-done.46.refs_1_ = f32[2,24,1728]{2,1,0:T(8,128)} collective-permute-done((f32[2,24,1728]{2,1,0:T(8,128)}, f32[2,24,1728]{2,1,0:T(8,128)}, u32[]{:S(2)}, u32[]{:S(2)}) %collective-permute-start.46) | collective-permute-done | bytes 331808 | tf_op jit(solution)/shard_map/ppermute | solution.py:988
  471.6 2.0 pair.4.refs_5_.refs_0_
  473.6 5.2 %order.1 = (bf16[2,576,1152]{2,1,0:T(8,128)(2,1)}, bf16[592,1152]{1,0:T(8,128)(2,1)}) custom-call(s32[11]{0:T(128)} %pad_add_fusion.3.refs_0_, bf16[448,1152]{1,0:T(8,128)(2,1)} %merge.1.refs_1_.refs_2_.refs_6_, bf16[448,1152]{1,0:T(8,128)(2,1)} %collective-permute-done.40.refs_2_, bf16[448,1152]{1,0:T(8,128)(2,1)} %collective-permute-done.41.refs_3_, ...), custom_call_target="tpu_custom_call" | custom-call | flops 115000000 | bytes 10000 | tf_op jit(solution)/shard_map/order/pallas_call | solution.py:69
  480.0 4.1 finish.3.refs_5_
  486.7 9.7 %spread.1 = (f32[1152,1152]{1,0:T(8,128)}, f32[1152,1152]{1,0:T(8,128)}, f32[3,288,1152]{2,1,0:T(8,128)}, f32[288,1152]{1,0:T(8,128)}) custom-call(s32[11]{0:T(128)} %pad_add_fusion.3.refs_0_, bf16[2,576,1152]{2,1,0:T(8,128)(2,1)} %get-tuple-element.197.refs_6_.refs_1_, bf16[2,576,1152]{2,1,0:T(8,128)(2,1)} %collective-permute-done.50.refs_2_, ...), custom_call_target="tpu_custom_call" | custom-call | flops 6899999744 | bytes 600000 | tf_op jit(solution)/shard_map/spread/pallas_call | solution.py:959
  498.2 2.5 pair.5.refs_1_
  500.7 6.6 %tail.1 = (f32[1728,1152]{1,0:T(8,128)}, f32[1728]{0:T(1024)}, f32[1152]{0:T(1024)}, f32[1152]{0:T(1024)}, f32[1152]{0:T(1024)}, /*index=5*/f32[2,288]{1,0:T(2,128)}) custom-call(s32[11]{0:T(128)} %pad_add_fusion.3.refs_0_, f32[8,24,1728]{2,1,0:T(8,128)} %pair.5.refs_1_), custom_call_target="tpu_custom_call" | custom-call | flops 3449999872 | bytes 300000 | tf_op jit(solution)/shard_map/tail/pallas_call | solution.py:69
  (205 shorter events, 53.3 us)
Async XLA Ops:
  7.2 136.0 %all-gather.2.cloned.1.call-start = ((), (), s32[]{:S(2)}) async-start(), calls=%async_computation.2 | async-start | bytes 2820096 | tf_op jit(solution)/shard_map/all_gather | solution.py:1055
  9.0 397.6 %reduce-scatter.3.cloned.1.call-start = ((), (), s32[]{:S(2)}) async-start(), calls=%async_computation.3 | async-start | bytes 2949120 | tf_op jit(solution)/shard_map/reduce_scatter | solution.py:1176
  15.3 14.8 %collective-permute-start = (f32[8,1800]{1,0:T(8,128)}, f32[8,1800]{1,0:T(8,128)S(1)}, u32[]{:S(2)}, u32[]{:S(2)}) collective-permute-start(f32[8,1800]{1,0:T(8,128)} %get-tuple-element.111.refs_1_), channel_id=1, source_target_pairs={{0,1},{1,2},{2,3},{3,0},{4,5},{5,6},{6,7},{7,4},{8,9},{9,10},{10,1... | collective-permute-start | bytes 172808 | tf_op jit(solution)/shard_map/ppermute | solution.py:984
  16.9 13.2 %collective-permute-start.1 = (f32[8,1800]{1,0:T(8,128)}, f32[8,1800]{1,0:T(8,128)S(1)}, u32[]{:S(2)}, u32[]{:S(2)}) collective-permute-start(f32[8,1800]{1,0:T(8,128)} %get-tuple-element.111.refs_1_), channel_id=1, source_target_pairs={{0,2},{1,3},{2,0},{3,1},{4,6},{5,7},{6,4},{7,5},{8,10},{9,11},{10,... | collective-permute-start | bytes 172808 | tf_op jit(solution)/shard_map/ppermute | solution.py:984
  18.2 12.0 %collective-permute-start.2 = (f32[8,1800]{1,0:T(8,128)}, f32[8,1800]{1,0:T(8,128)S(1)}, u32[]{:S(2)}, u32[]{:S(2)}) collective-permute-start(f32[8,1800]{1,0:T(8,128)} %get-tuple-element.111.refs_1_), channel_id=1, source_target_pairs={{0,3},{1,0},{2,1},{3,2},{4,7},{5,4},{6,5},{7,6},{8,11},{9,8},{10,9... | collective-permute-start | bytes 172808 | tf_op jit(solution)/shard_map/ppermute | solution.py:984
  20.0 8.7 %copy-start.22 = (f32[2,288]{1,0:T(2,128)S(1)}, f32[2,288]{1,0:T(2,128)}, u32[]{:S(2)}) copy-start(f32[2,288]{1,0:T(2,128)} %param.21) | copy-start | bytes 6916
  25.9 39.3 %collective-permute-start.3 = (bf16[288,1152]{1,0:T(8,128)(2,1)}, bf16[288,1152]{1,0:T(8,128)(2,1)S(1)}, u32[]{:S(2)}, u32[]{:S(2)}) collective-permute-start(bf16[288,1152]{1,0:T(8,128)(2,1)} %get-tuple-element.113.refs_5_.refs_3_), channel_id=1, source_target_pairs={{0,2},{1,3},{2,0},{3,1},{4,6},{5,7},{6,4},{7,5},{8,10},{9,11},{10,... | collective-permute-start | bytes 1990664 | tf_op jit(solution)/shard_map/ppermute | solution.py:984
  26.3 51.2 %collective-permute-start.4 = (bf16[288,1152]{1,0:T(8,128)(2,1)}, bf16[288,1152]{1,0:T(8,128)(2,1)S(1)}, u32[]{:S(2)}, u32[]{:S(2)}) collective-permute-start(bf16[288,1152]{1,0:T(8,128)(2,1)} %get-tuple-element.113.refs_5_.refs_3_), channel_id=1, source_target_pairs={{0,1},{1,2},{2,3},{3,0},{4,5},{5,6},{6,7},{7,4},{8,9},{9,10},{10,1... | collective-permute-start | bytes 1990664 | tf_op jit(solution)/shard_map/ppermute | solution.py:984
  65.2 12.3 %copy-start.8 = (bf16[288,1152]{1,0:T(8,128)(2,1)}, bf16[288,1152]{1,0:T(8,128)(2,1)S(1)}, u32[]{:S(2)}) copy-start(bf16[288,1152]{1,0:T(8,128)(2,1)S(1)} %collective-permute-done.3.refs_0_) | copy-start | bytes 1990660
  78.3 6.7 %copy-start.21 = (f32[1152]{0:T(1024)S(1)}, f32[1152]{0:T(1024)}, u32[]{:S(2)}) copy-start(f32[1152]{0:T(1024)} %param.27) | copy-start | bytes 13828
  80.8 40.4 %collective-permute-start.10 = (bf16[2,288,1152]{2,1,0:T(8,128)(2,1)}, bf16[2,288,1152]{2,1,0:T(8,128)(2,1)}, u32[]{:S(2)}, u32[]{:S(2)}) collective-permute-start(bf16[2,288,1152]{2,1,0:T(8,128)(2,1)} %two.1.refs_4_), channel_id=1, source_target_pairs={{0,16},{16,0},{1,17},{17,1},{2,18},{18,2},{3,19},{19,3},{4,20},{20... | collective-permute-start | bytes 3981320 | tf_op jit(solution)/shard_map/ppermute | solution.py:988
  82.3 42.3 %collective-permute-start.9 = (bf16[2,288,1152]{2,1,0:T(8,128)(2,1)}, bf16[2,288,1152]{2,1,0:T(8,128)(2,1)}, u32[]{:S(2)}, u32[]{:S(2)}) collective-permute-start(bf16[2,288,1152]{2,1,0:T(8,128)(2,1)} %two.1.refs_4_), channel_id=1, source_target_pairs={{0,8},{8,0},{1,9},{9,1},{2,10},{10,2},{3,11},{11,3},{4,12},{12,4},... | collective-permute-start | bytes 3981320 | tf_op jit(solution)/shard_map/ppermute | solution.py:988
  84.2 43.3 %copy-start.4 = (bf16[2,256,1152]{2,1,0:T(8,128)(2,1)}, bf16[2,256,1152]{2,1,0:T(8,128)(2,1)S(1)}, u32[]{:S(2)}) copy-start(bf16[2,256,1152]{2,1,0:T(8,128)(2,1)S(1)} %multiply_convert_fusion) | copy-start | bytes 3538948
  84.2 5.7 %collective-permute-start.5 = (bf16[512,1152]{1,0:T(8,128)(2,1)S(1)}, bf16[512,1152]{1,0:T(8,128)(2,1)S(1)}, u32[]{:S(2)}, u32[]{:S(2)}) collective-permute-start(bf16[512,1152]{1,0:T(8,128)(2,1)S(1)} %bitcast.29), channel_id=1, source_target_pairs={{0,4},{4,0},{1,5},{5,1},{2,6},{6,2},{3,7},{7,3},{8,12},{12,8},{9,1... | collective-permute-start | bytes 3538952 | tf_op jit(solution)/shard_map/ppermute | solution.py:988
  93.4 34.6 %collective-permute-start.6 = (bf16[2,64,1152]{2,1,0:T(8,128)(2,1)}, bf16[2,64,1152]{2,1,0:T(8,128)(2,1)S(1)}, u32[]{:S(2)}, u32[]{:S(2)}) collective-permute-start(bf16[2,64,1152]{2,1,0:T(8,128)(2,1)} %get-tuple-element.123.refs_2_), channel_id=1, source_target_pairs={{0,1},{1,2},{2,3},{3,0},{4,5},{5,6},{6,7},{7,4},{8,9},{9,10},{10,1... | collective-permute-start | bytes 884744 | tf_op jit(solution)/shard_map/ppermute | solution.py:984
  96.2 47.0 %collective-permute-start.7 = (bf16[2,64,1152]{2,1,0:T(8,128)(2,1)}, bf16[2,64,1152]{2,1,0:T(8,128)(2,1)S(1)}, u32[]{:S(2)}, u32[]{:S(2)}) collective-permute-start(bf16[2,64,1152]{2,1,0:T(8,128)(2,1)} %get-tuple-element.124), channel_id=1, source_target_pairs={{0,2},{1,3},{2,0},{3,1},{4,6},{5,7},{6,4},{7,5},{8,10},{9,11},{10,... | collective-permute-start | bytes 884744 | tf_op jit(solution)/shard_map/ppermute | solution.py:984
  99.9 43.2 %collective-permute-start.8 = (bf16[2,64,1152]{2,1,0:T(8,128)(2,1)}, bf16[2,64,1152]{2,1,0:T(8,128)(2,1)S(1)}, u32[]{:S(2)}, u32[]{:S(2)}) collective-permute-start(bf16[2,64,1152]{2,1,0:T(8,128)(2,1)} %get-tuple-element.125), channel_id=1, source_target_pairs={{0,3},{1,0},{2,1},{3,2},{4,7},{5,4},{6,5},{7,6},{8,11},{9,8},{10,9... | collective-permute-start | bytes 884744 | tf_op jit(solution)/shard_map/ppermute | solution.py:984
  121.1 31.0 %collective-permute-start.12 = (bf16[288,1152]{1,0:T(8,128)(2,1)}, bf16[288,1152]{1,0:T(8,128)(2,1)S(1)}, u32[]{:S(2)}, u32[]{:S(2)}) collective-permute-start(bf16[288,1152]{1,0:T(8,128)(2,1)} %get-tuple-element.128), channel_id=1, source_target_pairs={{0,3},{1,0},{2,1},{3,2},{4,7},{5,4},{6,5},{7,6},{8,11},{9,8},{10,9... | collective-permute-start | bytes 1990664 | tf_op jit(solution)/shard_map/ppermute | solution.py:984
  127.4 24.7 %collective-permute-start.13 = (bf16[2,144,1152]{2,1,0:T(8,128)(2,1)}, bf16[2,144,1152]{2,1,0:T(8,128)(2,1)S(1)}, u32[]{:S(2)}, u32[]{:S(2)}) collective-permute-start(bf16[2,144,1152]{2,1,0:T(8,128)(2,1)} %get-tuple-element.126.refs_9_), channel_id=1, source_target_pairs={{0,16},{16,0},{1,17},{17,1},{2,18},{18,2},{3,19},{19,3},{4,20},{20... | collective-permute-start | bytes 1990664 | tf_op jit(solution)/shard_map/ppermute | solution.py:988
  128.0 15.2 %copy-start.37 = (bf16[2,64,1152]{2,1,0:T(8,128)(2,1)}, bf16[2,64,1152]{2,1,0:T(8,128)(2,1)S(1)}, u32[]{:S(2)}) copy-start(bf16[2,64,1152]{2,1,0:T(8,128)(2,1)S(1)} %collective-permute-done.6.refs_2_.refs_12_) | copy-start | bytes 884740
  128.0 24.2 %collective-permute-start.14 = (bf16[2,144,1152]{2,1,0:T(8,128)(2,1)}, bf16[2,144,1152]{2,1,0:T(8,128)(2,1)S(1)}, u32[]{:S(2)}, u32[]{:S(2)}) collective-permute-start(bf16[2,144,1152]{2,1,0:T(8,128)(2,1)} %get-tuple-element.130), channel_id=1, source_target_pairs={{0,8},{8,0},{1,9},{9,1},{2,10},{10,2},{3,11},{11,3},{4,12},{12,4},... | collective-permute-start | bytes 1990664 | tf_op jit(solution)/shard_map/ppermute | solution.py:988
  152.0 6.9 %collective-permute-start.11 = (bf16[512,1152]{1,0:T(8,128)(2,1)}, bf16[512,1152]{1,0:T(8,128)(2,1)S(1)}, u32[]{:S(2)}, u32[]{:S(2)}) collective-permute-start(bf16[512,1152]{1,0:T(8,128)(2,1)} %bitcast.36), channel_id=1, source_target_pairs={{0,4},{4,0},{1,5},{5,1},{2,6},{6,2},{3,7},{7,3},{8,12},{12,8},{9,1... | collective-permute-start | bytes 3538952 | tf_op jit(solution)/shard_map/ppermute | solution.py:988
  155.5 38.6 %collective-permute-start.15 = (bf16[288,1152]{1,0:T(8,128)(2,1)}, bf16[288,1152]{1,0:T(8,128)(2,1)S(1)}, u32[]{:S(2)}, u32[]{:S(2)}) collective-permute-start(bf16[288,1152]{1,0:T(8,128)(2,1)} %release.4.refs_4_), channel_id=1, source_target_pairs={{0,8},{8,0},{1,9},{9,1},{2,10},{10,2},{3,11},{11,3},{4,12},{12,4},... | collective-permute-start | bytes 1990664 | tf_op jit(solution)/shard_map/ppermute | solution.py:988
  156.0 38.1 %collective-permute-start.16 = (bf16[288,1152]{1,0:T(8,128)(2,1)}, bf16[288,1152]{1,0:T(8,128)(2,1)}, u32[]{:S(2)}, u32[]{:S(2)}) collective-permute-start(bf16[288,1152]{1,0:T(8,128)(2,1)} %release.4.refs_4_), channel_id=1, source_target_pairs={{0,16},{16,0},{1,17},{17,1},{2,18},{18,2},{3,19},{19,3},{4,20},{20... | collective-permute-start | bytes 1990664 | tf_op jit(solution)/shard_map/ppermute | solution.py:988
  157.1 37.0 %collective-permute-start.17 = (bf16[288,1152]{1,0:T(8,128)(2,1)}, bf16[288,1152]{1,0:T(8,128)(2,1)}, u32[]{:S(2)}, u32[]{:S(2)}) collective-permute-start(bf16[288,1152]{1,0:T(8,128)(2,1)} %release.4.refs_4_), channel_id=1, source_target_pairs={{0,24},{8,16},{16,8},{24,0},{1,25},{9,17},{17,9},{25,1},{2,26},{10... | collective-permute-start | bytes 1990664 | tf_op jit(solution)/shard_map/ppermute | solution.py:992
  192.4 38.7 %collective-permute-start.20 = (bf16[2,2,144,1152]{3,2,1,0:T(8,128)(2,1)}, bf16[2,2,144,1152]{3,2,1,0:T(8,128)(2,1)S(1)}, u32[]{:S(2)}, u32[]{:S(2)}) collective-permute-start(bf16[2,2,144,1152]{3,2,1,0:T(8,128)(2,1)} %get-tuple-element.145), channel_id=1, source_target_pairs={{0,16},{16,0},{1,17},{17,1},{2,18},{18,2},{3,19},{19,3},{4,20},{20... | collective-permute-start | bytes 3981320 | tf_op jit(solution)/shard_map/ppermute | solution.py:988
  192.5 38.7 %collective-permute-start.21 = (bf16[2,2,144,1152]{3,2,1,0:T(8,128)(2,1)}, bf16[2,2,144,1152]{3,2,1,0:T(8,128)(2,1)}, u32[]{:S(2)}, u32[]{:S(2)}) collective-permute-start(bf16[2,2,144,1152]{3,2,1,0:T(8,128)(2,1)} %get-tuple-element.147), channel_id=1, source_target_pairs={{0,8},{8,0},{1,9},{9,1},{2,10},{10,2},{3,11},{11,3},{4,12},{12,4},... | collective-permute-start | bytes 3981320 | tf_op jit(solution)/shard_map/ppermute | solution.py:988
  230.6 8.3 %collective-permute-start.18 = (f32[512,1152]{1,0:T(8,128)}, f32[512,1152]{1,0:T(8,128)S(1)}, u32[]{:S(2)}, u32[]{:S(2)}) collective-permute-start(f32[512,1152]{1,0:T(8,128)} %get-tuple-element.140), channel_id=1, source_target_pairs={{0,4},{4,0},{1,5},{5,1},{2,6},{6,2},{3,7},{7,3},{8,12},{12,8},{9,1... | collective-permute-start | bytes 7077896 | tf_op jit(solution)/shard_map/ppermute | solution.py:988
  230.6 8.2 %collective-permute-start.19 = (f32[512,1152]{1,0:T(8,128)}, f32[512,1152]{1,0:T(8,128)}, u32[]{:S(2)}, u32[]{:S(2)}) collective-permute-start(f32[512,1152]{1,0:T(8,128)} %get-tuple-element.142), channel_id=1, source_target_pairs={{0,4},{4,0},{1,5},{5,1},{2,6},{6,2},{3,7},{7,3},{8,12},{12,8},{9,1... | collective-permute-start | bytes 7077896 | tf_op jit(solution)/shard_map/ppermute | solution.py:988
  236.5 25.4 %collective-permute-start.25 = (bf16[2,144,1152]{2,1,0:T(8,128)(2,1)}, bf16[2,144,1152]{2,1,0:T(8,128)(2,1)S(1)}, u32[]{:S(2)}, u32[]{:S(2)}) collective-permute-start(bf16[2,144,1152]{2,1,0:T(8,128)(2,1)} %get-tuple-element.155), channel_id=1, source_target_pairs={{0,8},{8,0},{1,9},{9,1},{2,10},{10,2},{3,11},{11,3},{4,12},{12,4},... | collective-permute-start | bytes 1990664 | tf_op jit(solution)/shard_map/ppermute | solution.py:988
  236.9 27.7 %collective-permute-start.26 = (bf16[2,144,1152]{2,1,0:T(8,128)(2,1)}, bf16[2,144,1152]{2,1,0:T(8,128)(2,1)S(1)}, u32[]{:S(2)}, u32[]{:S(2)}) collective-permute-start(bf16[2,144,1152]{2,1,0:T(8,128)(2,1)} %get-tuple-element.157), channel_id=1, source_target_pairs={{0,16},{16,0},{1,17},{17,1},{2,18},{18,2},{3,19},{19,3},{4,20},{20... | collective-permute-start | bytes 1990664 | tf_op jit(solution)/shard_map/ppermute | solution.py:988
  258.3 7.8 %collective-permute-start.27 = (bf16[4,144,1152]{2,1,0:T(8,128)(2,1)}, bf16[4,144,1152]{2,1,0:T(8,128)(2,1)S(1)}, u32[]{:S(2)}, u32[]{:S(2)}) collective-permute-start(bf16[4,144,1152]{2,1,0:T(8,128)(2,1)} %get-tuple-element.163), channel_id=1, source_target_pairs={{0,4},{4,0},{1,5},{5,1},{2,6},{6,2},{3,7},{7,3},{8,12},{12,8},{9,1... | collective-permute-start | bytes 3981320 | tf_op jit(solution)/shard_map/ppermute | solution.py:988
  258.4 18.1 %collective-permute-start.22 = (bf16[2,64,1152]{2,1,0:T(8,128)(2,1)}, bf16[2,64,1152]{2,1,0:T(8,128)(2,1)S(1)}, u32[]{:S(2)}, u32[]{:S(2)}) collective-permute-start(bf16[2,64,1152]{2,1,0:T(8,128)(2,1)} %get-tuple-element.151), channel_id=1, source_target_pairs={{0,3},{1,0},{2,1},{3,2},{4,7},{5,4},{6,5},{7,6},{8,11},{9,8},{10,9... | collective-permute-start | bytes 884744 | tf_op jit(solution)/shard_map/ppermute | solution.py:984
  258.5 23.7 %collective-permute-start.23 = (bf16[2,64,1152]{2,1,0:T(8,128)(2,1)}, bf16[2,64,1152]{2,1,0:T(8,128)(2,1)S(1)}, u32[]{:S(2)}, u32[]{:S(2)}) collective-permute-start(bf16[2,64,1152]{2,1,0:T(8,128)(2,1)} %get-tuple-element.152), channel_id=1, source_target_pairs={{0,2},{1,3},{2,0},{3,1},{4,6},{5,7},{6,4},{7,5},{8,10},{9,11},{10,... | collective-permute-start | bytes 884744 | tf_op jit(solution)/shard_map/ppermute | solution.py:984
  261.8 26.1 %collective-permute-start.24 = (bf16[2,64,1152]{2,1,0:T(8,128)(2,1)}, bf16[2,64,1152]{2,1,0:T(8,128)(2,1)}, u32[]{:S(2)}, u32[]{:S(2)}) collective-permute-start(bf16[2,64,1152]{2,1,0:T(8,128)(2,1)} %get-tuple-element.153), channel_id=1, source_target_pairs={{0,1},{1,2},{2,3},{3,0},{4,5},{5,6},{6,7},{7,4},{8,9},{9,10},{10,1... | collective-permute-start | bytes 884744 | tf_op jit(solution)/shard_map/ppermute | solution.py:984
  274.9 50.4 %collective-permute-start.28 = (bf16[768,1152]{1,0:T(8,128)(2,1)}, bf16[768,1152]{1,0:T(8,128)(2,1)S(1)}, u32[]{:S(2)}, u32[]{:S(2)}) collective-permute-start(bf16[768,1152]{1,0:T(8,128)(2,1)} %get-tuple-element.164.refs_4_), channel_id=1, source_target_pairs={{0,16},{16,0},{1,17},{17,1},{2,18},{18,2},{3,19},{19,3},{4,20},{20... | collective-permute-start | bytes 5308424 | tf_op jit(solution)/shard_map/ppermute | solution.py:988
  275.0 50.3 %collective-permute-start.29 = (bf16[768,1152]{1,0:T(8,128)(2,1)}, bf16[768,1152]{1,0:T(8,128)(2,1)}, u32[]{:S(2)}, u32[]{:S(2)}) collective-permute-start(bf16[768,1152]{1,0:T(8,128)(2,1)} %get-tuple-element.169), channel_id=1, source_target_pairs={{0,8},{8,0},{1,9},{9,1},{2,10},{10,2},{3,11},{11,3},{4,12},{12,4},... | collective-permute-start | bytes 5308424 | tf_op jit(solution)/shard_map/ppermute | solution.py:988
  276.5 11.4 %copy-start.40 = (bf16[2,64,1152]{2,1,0:T(8,128)(2,1)}, bf16[2,64,1152]{2,1,0:T(8,128)(2,1)S(1)}, u32[]{:S(2)}) copy-start(bf16[2,64,1152]{2,1,0:T(8,128)(2,1)S(1)} %collective-permute-done.22.refs_5_.g1) | copy-start | bytes 884740
  290.8 62.4 %collective-permute-start.33 = (bf16[288,1152]{1,0:T(8,128)(2,1)}, bf16[288,1152]{1,0:T(8,128)(2,1)S(1)}, u32[]{:S(2)}, u32[]{:S(2)}) collective-permute-start(bf16[288,1152]{1,0:T(8,128)(2,1)} %get-tuple-element.165.refs_0_), channel_id=1, source_target_pairs={{0,3},{1,0},{2,1},{3,2},{4,7},{5,4},{6,5},{7,6},{8,11},{9,8},{10,9... | collective-permute-start | bytes 1990664 | tf_op jit(solution)/shard_map/ppermute | solution.py:984
  292.1 61.2 %collective-permute-start.34 = (bf16[288,1152]{1,0:T(8,128)(2,1)}, bf16[288,1152]{1,0:T(8,128)(2,1)S(1)}, u32[]{:S(2)}, u32[]{:S(2)}) collective-permute-start(bf16[288,1152]{1,0:T(8,128)(2,1)} %get-tuple-element.179), channel_id=1, source_target_pairs={{0,2},{1,3},{2,0},{3,1},{4,6},{5,7},{6,4},{7,5},{8,10},{9,11},{10,... | collective-permute-start | bytes 1990664 | tf_op jit(solution)/shard_map/ppermute | solution.py:984
  325.3 154.8 %reduce-scatter.5.cloned.1.call-start = ((), (), s32[]{:S(2)}) async-start(), calls=%async_computation.4 | async-start | bytes 2949120 | tf_op jit(solution)/shard_map/reduce_scatter | solution.py:1258
  331.6 23.3 %collective-permute-start.31 = (bf16[384,1152]{1,0:T(8,128)(2,1)}, bf16[384,1152]{1,0:T(8,128)(2,1)}, u32[]{:S(2)}, u32[]{:S(2)}) collective-permute-start(bf16[384,1152]{1,0:T(8,128)(2,1)} %get-tuple-element.175), channel_id=1, source_target_pairs={{0,8},{8,0},{1,9},{9,1},{2,10},{10,2},{3,11},{11,3},{4,12},{12,4},... | collective-permute-start | bytes 2654216 | tf_op jit(solution)/shard_map/ppermute | solution.py:988
  332.2 22.7 %collective-permute-start.32 = (bf16[384,1152]{1,0:T(8,128)(2,1)}, bf16[384,1152]{1,0:T(8,128)(2,1)}, u32[]{:S(2)}, u32[]{:S(2)}) collective-permute-start(bf16[384,1152]{1,0:T(8,128)(2,1)} %get-tuple-element.177), channel_id=1, source_target_pairs={{0,16},{16,0},{1,17},{17,1},{2,18},{18,2},{3,19},{19,3},{4,20},{20... | collective-permute-start | bytes 2654216 | tf_op jit(solution)/shard_map/ppermute | solution.py:988
  353.2 5.3 %collective-permute-start.30 = (bf16[448,1152]{1,0:T(8,128)(2,1)}, bf16[448,1152]{1,0:T(8,128)(2,1)}, u32[]{:S(2)}, u32[]{:S(2)}) collective-permute-start(bf16[448,1152]{1,0:T(8,128)(2,1)} %get-tuple-element.174), channel_id=1, source_target_pairs={{0,4},{4,0},{1,5},{5,1},{2,6},{6,2},{3,7},{7,3},{8,12},{12,8},{9,1... | collective-permute-start | bytes 3096584 | tf_op jit(solution)/shard_map/ppermute | solution.py:988
  358.5 6.6 %copy-start.42 = (bf16[48,1152]{1,0:T(8,128)(2,1)S(1)}, bf16[48,1152]{1,0:T(8,128)(2,1)}, u32[]{:S(2)}) copy-start(bf16[48,1152]{1,0:T(8,128)(2,1)} %get-tuple-element.190) | copy-start | bytes 331780
  362.4 14.4 %collective-permute-start.35 = (bf16[224,1152]{1,0:T(8,128)(2,1)}, bf16[224,1152]{1,0:T(8,128)(2,1)S(1)}, u32[]{:S(2)}, u32[]{:S(2)}) collective-permute-start(bf16[224,1152]{1,0:T(8,128)(2,1)} %get-tuple-element.182), channel_id=1, source_target_pairs={{0,8},{8,0},{1,9},{9,1},{2,10},{10,2},{3,11},{11,3},{4,12},{12,4},... | collective-permute-start | bytes 1548296 | tf_op jit(solution)/shard_map/ppermute | solution.py:988
  362.8 49.7 %collective-permute-start.37 = (bf16[336,1152]{1,0:T(8,128)(2,1)S(1)}, bf16[336,1152]{1,0:T(8,128)(2,1)S(1)}, u32[]{:S(2)}, u32[]{:S(2)}) collective-permute-start(bf16[336,1152]{1,0:T(8,128)(2,1)S(1)} %copy-done.29), channel_id=1, source_target_pairs={{0,1},{1,2},{2,3},{3,0},{4,5},{5,6},{6,7},{7,4},{8,9},{9,10},{10,1... | collective-permute-start | bytes 2322440 | tf_op jit(solution)/shard_map/ppermute | solution.py:984
  362.9 47.8 %collective-permute-start.38 = (bf16[48,1152]{1,0:T(8,128)(2,1)S(1)}, bf16[48,1152]{1,0:T(8,128)(2,1)S(1)}, u32[]{:S(2)}, u32[]{:S(2)}) collective-permute-start(bf16[48,1152]{1,0:T(8,128)(2,1)S(1)} %copy-done.43), channel_id=1, source_target_pairs={{0,3},{1,0},{2,1},{3,2},{4,7},{5,4},{6,5},{7,6},{8,11},{9,8},{10,9... | collective-permute-start | bytes 331784 | tf_op jit(solution)/shard_map/ppermute | solution.py:984
  365.1 45.6 %collective-permute-start.39 = (bf16[48,1152]{1,0:T(8,128)(2,1)S(1)}, bf16[48,1152]{1,0:T(8,128)(2,1)S(1)}, u32[]{:S(2)}, u32[]{:S(2)}) collective-permute-start(bf16[48,1152]{1,0:T(8,128)(2,1)S(1)} %copy-done.42), channel_id=1, source_target_pairs={{0,2},{1,3},{2,0},{3,1},{4,6},{5,7},{6,4},{7,5},{8,10},{9,11},{10,... | collective-permute-start | bytes 331784 | tf_op jit(solution)/shard_map/ppermute | solution.py:984
  369.4 54.3 %collective-permute-start.43 = (f32[56,1152]{1,0:T(8,128)}, f32[56,1152]{1,0:T(8,128)}, u32[]{:S(2)}, u32[]{:S(2)}) collective-permute-start(f32[56,1152]{1,0:T(8,128)} %pile.1.refs_4_.refs_0_), channel_id=1, source_target_pairs={{0,2},{1,3},{2,0},{3,1},{4,6},{5,7},{6,4},{7,5},{8,10},{9,11},{10,... | collective-permute-start | bytes 774152 | tf_op jit(solution)/shard_map/ppermute | solution.py:984
  380.4 32.2 %collective-permute-start.36 = (bf16[112,1152]{1,0:T(8,128)(2,1)}, bf16[112,1152]{1,0:T(8,128)(2,1)S(1)}, u32[]{:S(2)}, u32[]{:S(2)}) collective-permute-start(bf16[112,1152]{1,0:T(8,128)(2,1)} %get-tuple-element.187), channel_id=1, source_target_pairs={{0,16},{16,0},{1,17},{17,1},{2,18},{18,2},{3,19},{19,3},{4,20},{20... | collective-permute-start | bytes 774152 | tf_op jit(solution)/shard_map/ppermute | solution.py:988
  416.9 56.7 %collective-permute-start.40 = (bf16[448,1152]{1,0:T(8,128)(2,1)}, bf16[448,1152]{1,0:T(8,128)(2,1)}, u32[]{:S(2)}, u32[]{:S(2)}) collective-permute-start(bf16[448,1152]{1,0:T(8,128)(2,1)} %merge.1.refs_1_.refs_2_.refs_6_), channel_id=1, source_target_pairs={{0,8},{8,0},{1,9},{9,1},{2,10},{10,2},{3,11},{11,3},{4,12},{12,4},... | collective-permute-start | bytes 3096584 | tf_op jit(solution)/shard_map/ppermute | solution.py:988
  416.9 56.7 %collective-permute-start.41 = (bf16[448,1152]{1,0:T(8,128)(2,1)}, bf16[448,1152]{1,0:T(8,128)(2,1)}, u32[]{:S(2)}, u32[]{:S(2)}) collective-permute-start(bf16[448,1152]{1,0:T(8,128)(2,1)} %merge.1.refs_1_.refs_2_.refs_6_), channel_id=1, source_target_pairs={{0,16},{16,0},{1,17},{17,1},{2,18},{18,2},{3,19},{19,3},{4,20},{20... | collective-permute-start | bytes 3096584 | tf_op jit(solution)/shard_map/ppermute | solution.py:988
  417.0 56.7 %collective-permute-start.42 = (bf16[448,1152]{1,0:T(8,128)(2,1)}, bf16[448,1152]{1,0:T(8,128)(2,1)}, u32[]{:S(2)}, u32[]{:S(2)}) collective-permute-start(bf16[448,1152]{1,0:T(8,128)(2,1)} %merge.1.refs_1_.refs_2_.refs_6_), channel_id=1, source_target_pairs={{0,24},{8,16},{16,8},{24,0},{1,25},{9,17},{17,9},{25,1},{2,26},{10... | collective-permute-start | bytes 3096584 | tf_op jit(solution)/shard_map/ppermute | solution.py:992
  423.7 21.9 %copy-start.2 = (bf16[1152,1728]{0,1:T(8,128)(2,1)S(1)}, bf16[1152,1728]{0,1:T(8,128)(2,1)}, u32[]{:S(2)}) copy-start(bf16[1152,1728]{0,1:T(8,128)(2,1)} %param.18) | copy-start | bytes 11943940
  425.7 13.2 %collective-permute-start.44 = (f32[56,1152]{1,0:T(8,128)}, f32[56,1152]{1,0:T(8,128)}, u32[]{:S(2)}, u32[]{:S(2)}) collective-permute-start(f32[56,1152]{1,0:T(8,128)} %sum.1.refs_1_), channel_id=1, source_target_pairs={{0,1},{1,2},{2,3},{3,0},{4,5},{5,6},{6,7},{7,4},{8,9},{9,10},{10,1... | collective-permute-start | bytes 774152 | tf_op jit(solution)/shard_map/ppermute | solution.py:984
  441.8 1.7 collective-permute-start.45
  445.3 26.3 %collective-permute-start.46 = (f32[2,24,1728]{2,1,0:T(8,128)}, f32[2,24,1728]{2,1,0:T(8,128)}, u32[]{:S(2)}, u32[]{:S(2)}) collective-permute-start(f32[2,24,1728]{2,1,0:T(8,128)} %pair.3.refs_0_), channel_id=1, source_target_pairs={{0,8},{8,0},{1,9},{9,1},{2,10},{10,2},{3,11},{11,3},{4,12},{12,4},... | collective-permute-start | bytes 995336 | tf_op jit(solution)/shard_map/ppermute | solution.py:988
  447.0 5.8 %collective-permute-start.47 = (f32[8,1152]{1,0:T(8,128)S(1)}, f32[8,1152]{1,0:T(8,128)S(1)}, u32[]{:S(2)}, u32[]{:S(2)}) collective-permute-start(f32[8,1152]{1,0:T(8,128)S(1)} %fusion.10), channel_id=1, source_target_pairs={{0,2},{1,3},{2,0},{3,1},{4,6},{5,7},{6,4},{7,5},{8,10},{9,11},{10,... | collective-permute-start | bytes 110600 | tf_op jit(solution)/shard_map/ppermute | solution.py:984
  452.8 6.1 %collective-permute-start.48 = (f32[8,1152]{1,0:T(8,128)S(1)}, f32[8,1152]{1,0:T(8,128)S(1)}, u32[]{:S(2)}, u32[]{:S(2)}) collective-permute-start(f32[8,1152]{1,0:T(8,128)S(1)} %add.35), channel_id=1, source_target_pairs={{0,1},{1,2},{2,3},{3,0},{4,5},{5,6},{6,7},{7,4},{8,9},{9,10},{10,1... | collective-permute-start | bytes 110600 | tf_op jit(solution)/shard_map/ppermute | solution.py:984
  478.8 7.2 %collective-permute-start.50 = (bf16[2,576,1152]{2,1,0:T(8,128)(2,1)}, bf16[2,576,1152]{2,1,0:T(8,128)(2,1)}, u32[]{:S(2)}, u32[]{:S(2)}) collective-permute-start(bf16[2,576,1152]{2,1,0:T(8,128)(2,1)} %get-tuple-element.197.refs_6_.refs_1_), channel_id=1, source_target_pairs={{0,4},{4,0},{1,5},{5,1},{2,6},{6,2},{3,7},{7,3},{8,12},{12,8},{9,1... | collective-permute-start | bytes 7962632 | tf_op jit(solution)/shard_map/ppermute | solution.py:988
  478.8 6.7 %collective-permute-start.51 = (bf16[592,1152]{1,0:T(8,128)(2,1)}, bf16[592,1152]{1,0:T(8,128)(2,1)S(1)}, u32[]{:S(2)}, u32[]{:S(2)}) collective-permute-start(bf16[592,1152]{1,0:T(8,128)(2,1)} %get-tuple-element.198.refs_3_), channel_id=1, source_target_pairs={{0,4},{4,0},{1,5},{5,1},{2,6},{6,2},{3,7},{7,3},{8,12},{12,8},{9,1... | collective-permute-start | bytes 4091912 | tf_op jit(solution)/shard_map/ppermute | solution.py:988
  480.0 17.3 %collective-permute-start.49 = (f32[4,24,1728]{2,1,0:T(8,128)S(1)}, f32[4,24,1728]{2,1,0:T(8,128)S(1)}, u32[]{:S(2)}, u32[]{:S(2)}) collective-permute-start(f32[4,24,1728]{2,1,0:T(8,128)S(1)} %copy-done.3), channel_id=1, source_target_pairs={{0,16},{16,0},{1,17},{17,1},{2,18},{18,2},{3,19},{19,3},{4,20},{20... | collective-permute-start | bytes 1990664 | tf_op jit(solution)/shard_map/ppermute | solution.py:988
  500.7 6.6 %copy-start.1 = (bf16[288,1152]{1,0:T(8,128)(2,1)S(1)}, bf16[288,1152]{1,0:T(8,128)(2,1)}, u32[]{:S(2)}) copy-start(bf16[288,1152]{1,0:T(8,128)(2,1)} %param.22) | copy-start | bytes 1990660
  (35 other events, 66.1 us)
Sparse Core Ops, SparseCore 0:
  10.7 128.8 all-gather.1
  325.4 81.1 reduce-scatter.2
  423.8 48.8 reduce-scatter.4
